TPU v7x, 32 devices: a whole 2x2x4 slice. The times are simulated.
32 devices in a mesh: dp: 8 (over z, y), mp: 4 (over x, core).
Axes of the slice: x: 2, y: 2, z: 4, core: 2. Of those that a mesh axis runs over, the one named last changes fastest.
Arguments:
- patches: bfloat16 [4, 8192, 768], P(None, ('dp', 'mp')), may hold values from -6 to 6
- heights: int32 [4, 512], P(None, ('dp', 'mp')), may hold values from 0 to 32, as said below
- widths: int32 [4, 512], P(None, ('dp', 'mp')), may hold values from 0 to 32, as said below
- labels: int32 [4, 512], P(None, 'dp'), may hold values from 0 to 999
- res_weights: int32 [4, 512], P(None, 'dp'), may hold values from 0 to 8, as said below
- w_embed: float32 [1024, 768], P(('dp', 'mp'))
- w_qkv: float32 [768, 2304], P(('dp', 'mp')), may hold values from -0.21875 to 0.21875
- w_out: float32 [768, 768], P(('dp', 'mp')), may hold values from -0.875 to 0.875
- w_up: float32 [768, 3072], P(('dp', 'mp')), may hold values from -0.21875 to 0.21875
- w_down: float32 [3072, 768], P(('dp', 'mp')), may hold values from -0.109375 to 0.109375
- vectors: float32 [6, 768], P(None, ('dp', 'mp'))
- w_cls: float32 [768, 1000], P('dp', 'mp')
- m_embed: float32 [1024, 768], P(('dp', 'mp')), may hold values from -2.3841858e-06 to 2.3841858e-06
- v_embed: float32 [1024, 768], P(('dp', 'mp')), may hold values from 1.1578191e-14 to 4.6312763e-14
- m_qkv: float32 [768, 2304], P(('dp', 'mp')), may hold values from -2.3841858e-06 to 2.3841858e-06
- v_qkv: float32 [768, 2304], P(('dp', 'mp')), may hold values from 1.1578191e-14 to 4.6312763e-14
- m_out: float32 [768, 768], P(('dp', 'mp')), may hold values from -2.3841858e-06 to 2.3841858e-06
- v_out: float32 [768, 768], P(('dp', 'mp')), may hold values from 1.1578191e-14 to 4.6312763e-14
- m_up: float32 [768, 3072], P(('dp', 'mp')), may hold values from -2.3841858e-06 to 2.3841858e-06
- v_up: float32 [768, 3072], P(('dp', 'mp')), may hold values from 1.1578191e-14 to 4.6312763e-14
- m_down: float32 [3072, 768], P(('dp', 'mp')), may hold values from -2.3841858e-06 to 2.3841858e-06
- v_down: float32 [3072, 768], P(('dp', 'mp')), may hold values from 1.1578191e-14 to 4.6312763e-14
- m_vectors: float32 [6, 768], P(None, ('dp', 'mp')), may hold values from -3.8146973e-06 to 3.8146973e-06
- v_vectors: float32 [6, 768], P(None, ('dp', 'mp')), may hold values from 2.8945477e-14 to 1.1578191e-13
- m_cls: float32 [768, 1000], P('dp', 'mp'), may hold values from -2.3841858e-06 to 2.3841858e-06
- v_cls: float32 [768, 1000], P('dp', 'mp'), may hold values from 1.1578191e-14 to 4.6312763e-14
Outputs:
- loss_terms: float32 [2], replicated
- clip_norm: float32 [], replicated
- lamb_norms: float32 [12, 2], replicated
- embed_new: float32 [1024, 768], P(('dp', 'mp'))
- embed_first: float32 [1024, 768], P(('dp', 'mp'))
- embed_second: float32 [1024, 768], P(('dp', 'mp'))
- qkv_new: float32 [768, 2304], P(('dp', 'mp'))
- qkv_first: float32 [768, 2304], P(('dp', 'mp'))
- qkv_second: float32 [768, 2304], P(('dp', 'mp'))
- out_new: float32 [768, 768], P(('dp', 'mp'))
- out_first: float32 [768, 768], P(('dp', 'mp'))
- out_second: float32 [768, 768], P(('dp', 'mp'))
- up_new: float32 [768, 3072], P(('dp', 'mp'))
- up_first: float32 [768, 3072], P(('dp', 'mp'))
- up_second: float32 [768, 3072], P(('dp', 'mp'))
- down_new: float32 [3072, 768], P(('dp', 'mp'))
- down_first: float32 [3072, 768], P(('dp', 'mp'))
- down_second: float32 [3072, 768], P(('dp', 'mp'))
- vectors_new: float32 [6, 768], P(None, ('dp', 'mp'))
- vectors_first: float32 [6, 768], P(None, ('dp', 'mp'))
- vectors_second: float32 [6, 768], P(None, ('dp', 'mp'))
- cls_new: float32 [768, 1000], P('dp', 'mp')
- cls_first: float32 [768, 1000], P('dp', 'mp')
- cls_second: float32 [768, 1000], P('dp', 'mp')
Inputs may be any that keep to these rules, and one draw needn't show every extreme that they name: In each device's slots of a micro-batch the filled slots come first and the last slot is empty; a slot is filled exactly when its height and width are 2 or more, and then height times width is at most 256; the filled slots' heights times widths add up to at most 256, and empty slots have height and width 0. `widths`: zero exactly where heights is zero. `res_weights`: zero exactly on empty slots, 1 or more on filled ones.
All inputs are finite; a program needn't handle non-finite values.
Results may differ from a plain program's by a relative error of at most 0.025.
The roundings to bfloat16 on the way count: a program that leaves them out, or rounds other values in their place, can miss the bound.
Values may be sent and summed in bfloat16 or wider, within the bound.
A program may use at most 192 MiB of HBM per device.

v0:
```python
import jax
import jax.numpy as jnp
from jax import lax
from jax.sharding import PartitionSpec as P

HEAD = 64
POS = 128
STEP = 10


epsilon = 1e-06
clip_limit = 0.01
learn_rate = 0.3
beta_first = 0.9
beta_second = 0.999
weight_decay = 0.01
adam_floor = 1e-08
highest = lax.Precision.HIGHEST
excluded = -1e30


def merged_2(part, axis, combine):
    gathered = jax.tree.map(lambda a: lax.all_gather(a, axis), part)

    def take(source):
        return jax.tree.map(lambda a: lax.dynamic_index_in_dim(a, source, 0, False), gathered)

    return lax.fori_loop(
        1, lax.axis_size(axis), lambda source, state: combine(state, take(source)), take(0)
    )


def layer_norm(values, scales):
    center = values - jnp.mean(values, axis=-1, keepdims=True)
    spread = jnp.mean(center * center, axis=-1, keepdims=True)
    return center * lax.rsqrt(spread + epsilon) * scales


def norm_back(values, scales, upstream):
    result, pullback = jax.vjp(layer_norm, values, scales)
    return pullback(upstream)


def outer_dot(left, right):
    return lax.dot_general(
        left, right, (((0,), (0,)), ((), ())), preferred_element_type=jnp.float32
    )


def inner_dot(left, right):
    return lax.dot_general(
        left, right, (((1,), (1,)), ((), ())), preferred_element_type=jnp.float32
    )


def layout(heights, widths, row_count):
    lengths = heights * widths
    image_ends = jnp.cumsum(lengths)
    starts = image_ends - lengths
    places = jnp.arange(row_count, dtype=jnp.int32)
    slot_ids = jnp.arange(heights.shape[0], dtype=jnp.int32)
    segment = jnp.sum((places[:, None] >= image_ends[None, :]).astype(jnp.int32), axis=1)
    member = segment[None, :] == slot_ids[:, None]
    member_int = member.T.astype(jnp.int32)
    within = places - jnp.sum(member_int * starts[None, :], axis=1)
    across = jnp.maximum(jnp.sum(member_int * widths[None, :], axis=1), 1)
    upright = jnp.maximum(jnp.sum(member_int * heights[None, :], axis=1), 1)
    col_pos = within % across * POS // across
    row_pos = within // across * POS // upright
    pos_table = jnp.arange(POS, dtype=jnp.int32)
    pos_rows = jnp.concatenate(
        [col_pos[:, None] == pos_table[None, :], row_pos[:, None] == pos_table[None, :]], axis=1
    )
    return (segment, member, pos_rows)


def block_scores(queries, key_rows, segment):
    scores = jnp.einsum(
        "thd,shd->hts", queries, key_rows, preferred_element_type=jnp.float32
    ) * HEAD ** (-0.5)
    same_image = segment[:, None] == segment[None, :]
    return (queries, jnp.where(same_image[None], scores, excluded))


def attend(queries, key_rows, value_rows, segment):
    block_rows = min(512, queries.shape[0])

    def one_block(block_index):
        query_block, scores = block_scores(queries, key_rows, segment)
        top_score = jnp.max(scores, axis=-1, keepdims=True)
        exp_scores = jnp.exp(scores - top_score)
        exp_total = jnp.sum(exp_scores, axis=-1, keepdims=True)
        attention = (exp_scores / exp_total).astype(jnp.bfloat16)
        result = jnp.einsum(
            "hts,shd->thd", attention, value_rows, preferred_element_type=jnp.float32
        )
        return (result.astype(jnp.bfloat16), (top_score + jnp.log(exp_total))[..., 0])

    mixed_heads, log_total = lax.map(one_block, jnp.arange(queries.shape[0] // block_rows))
    return (mixed_heads.reshape(queries.shape), log_total)


def attend_back(queries, key_rows, value_rows, segment, log_total, mixed_grad):
    block_rows = min(512, queries.shape[0])

    def one_block(running, block_index):
        key_grad, value_grad = running
        query_block, scores = block_scores(queries, key_rows, segment)
        attention = jnp.exp(scores - log_total[block_index][..., None])
        value_grad = value_grad + jnp.einsum(
            "hts,thd->shd",
            attention.astype(jnp.bfloat16),
            mixed_grad,
            preferred_element_type=jnp.float32,
        )
        prob_grad = jnp.einsum(
            "thd,shd->hts", mixed_grad, value_rows, preferred_element_type=jnp.float32
        )
        score_grad = (
            attention * (prob_grad - jnp.sum(attention * prob_grad, axis=-1, keepdims=True))
        ).astype(jnp.bfloat16)
        query_grad = jnp.einsum(
            "hts,shd->thd", score_grad, key_rows, preferred_element_type=jnp.float32
        ) * HEAD ** (-0.5)
        key_grad = key_grad + jnp.einsum(
            "hts,thd->shd", score_grad, query_block, preferred_element_type=jnp.float32
        ) * HEAD ** (-0.5)
        return ((key_grad, value_grad), query_grad)

    zero_grad = jnp.zeros(key_rows.shape, jnp.float32)
    sums, query_grad = lax.scan(
        one_block, (zero_grad, zero_grad), jnp.arange(queries.shape[0] // block_rows)
    )
    return (query_grad.reshape(queries.shape), sums[0], sums[1])


def layer_forward(weights_low, vector_low, patch_rows, heights, widths):
    embed, joined_w, out_w, up_w, down_w = weights_low
    vectors = vector_low.astype(jnp.float32)
    row_count, pixel_count = patch_rows.shape
    model_width = embed.shape[1]
    head_count = model_width // HEAD
    head_shape = (row_count, head_count, HEAD)
    segment, member, pos_rows = layout(heights, widths, row_count)
    pos_low = pos_rows.astype(jnp.bfloat16)
    embedded = jnp.dot(
        patch_rows, embed[:pixel_count], preferred_element_type=jnp.float32
    ) + jnp.dot(pos_low, embed[pixel_count:], preferred_element_type=jnp.float32)
    normed = layer_norm(embedded, vectors[0]).astype(jnp.bfloat16)
    joined = jnp.dot(normed, joined_w, preferred_element_type=jnp.float32)
    query_pre = joined[:, :model_width].reshape(head_shape)
    key_pre = joined[:, model_width : 2 * model_width].reshape(head_shape)
    queries = layer_norm(query_pre, vectors[3].reshape(head_count, HEAD)).astype(jnp.bfloat16)
    key_rows = layer_norm(key_pre, vectors[4].reshape(head_count, HEAD)).astype(jnp.bfloat16)
    value_rows = joined[:, 2 * model_width :].reshape(head_shape).astype(jnp.bfloat16)
    mixed_heads, log_total = attend(queries, key_rows, value_rows, segment)
    mixed_flat = mixed_heads.reshape(row_count, model_width)
    second = embedded + jnp.dot(mixed_flat, out_w, preferred_element_type=jnp.float32)
    hidden = layer_norm(second, vectors[1]).astype(jnp.bfloat16)
    upward = jnp.dot(hidden, up_w, preferred_element_type=jnp.float32)
    active = jax.nn.gelu(upward).astype(jnp.bfloat16)
    residual = second + jnp.dot(active, down_w, preferred_element_type=jnp.float32)
    final_heads = layer_norm(residual, vectors[2]).astype(jnp.bfloat16).reshape(head_shape)
    probe_low = vector_low[5].reshape(head_count, HEAD)
    probe_scores = jnp.einsum(
        "thd,hd->th", final_heads, probe_low, preferred_element_type=jnp.float32
    ) * HEAD ** (-0.5)
    masked = jnp.where(member[:, :, None], probe_scores[None], excluded)
    pooling = jax.nn.softmax(masked, axis=1) * member[:, :, None].astype(jnp.float32)
    pool_low = pooling.astype(jnp.bfloat16)
    pooled = jnp.einsum("ith,thd->ihd", pool_low, final_heads, preferred_element_type=jnp.float32)
    saved = (
        patch_rows,
        pos_low,
        member,
        segment,
        embedded,
        normed,
        query_pre,
        key_pre,
        queries,
        key_rows,
        value_rows,
        log_total,
        mixed_flat,
        second,
        hidden,
        upward,
        active,
        residual,
        final_heads,
        pooling,
        pool_low,
    )
    return (pooled.reshape(-1, model_width).astype(jnp.bfloat16), saved)


def layer_backward(weights_low, vector_low, saved, pooled_grad):
    (
        patch_rows,
        pos_low,
        member,
        segment,
        embedded,
        normed,
        query_pre,
        key_pre,
        queries,
        key_rows,
        value_rows,
        log_total,
        mixed_flat,
        second,
        hidden,
        upward,
        active,
        residual,
        final_heads,
        pooling,
        pool_low,
    ) = saved
    embed, joined_w, out_w, up_w, down_w = weights_low
    vectors = vector_low.astype(jnp.float32)
    row_count, head_count = (final_heads.shape[0], final_heads.shape[1])
    model_width = head_count * HEAD
    image_grad = pooled_grad.reshape(-1, head_count, HEAD)
    final_wide = final_heads.astype(jnp.float32)
    weight_grad = jnp.einsum("ihd,thd->ith", image_grad, final_wide, precision=highest) * member[
        :, :, None
    ].astype(jnp.float32)
    score_grad = pooling * (weight_grad - jnp.sum(pooling * weight_grad, axis=1, keepdims=True))
    score_grad = jnp.sum(score_grad, axis=0) * HEAD ** (-0.5)
    probe = vectors[5].reshape(head_count, HEAD)
    final_grad = (
        jnp.einsum("ith,ihd->thd", pool_low.astype(jnp.float32), image_grad, precision=highest)
        + score_grad[:, :, None] * probe[None]
    )
    probe_grad = jnp.einsum("th,thd->hd", score_grad, final_wide, precision=highest)
    residual_grad, gain_final = norm_back(
        residual, vectors[2], final_grad.reshape(row_count, model_width)
    )
    down_in = residual_grad.astype(jnp.bfloat16)
    down_grad = outer_dot(active, down_in)
    active_grad = inner_dot(down_in, down_w)
    upward_grad = jax.vjp(jax.nn.gelu, upward)[1](active_grad)[0].astype(jnp.bfloat16)
    up_grad = outer_dot(hidden, upward_grad)
    second_back, gain_second = norm_back(second, vectors[1], inner_dot(upward_grad, up_w))
    second_grad = residual_grad + second_back
    out_in = second_grad.astype(jnp.bfloat16)
    out_grad = outer_dot(mixed_flat, out_in)
    mixed_grad = inner_dot(out_in, out_w).astype(jnp.bfloat16).reshape(row_count, head_count, HEAD)
    query_grad, key_grad, value_grad = attend_back(
        queries, key_rows, value_rows, segment, log_total, mixed_grad
    )
    query_back, gain_query = norm_back(query_pre, vectors[3].reshape(head_count, HEAD), query_grad)
    key_back, gain_key = norm_back(key_pre, vectors[4].reshape(head_count, HEAD), key_grad)
    joined_grad = jnp.concatenate(
        [
            query_back.reshape(row_count, model_width),
            key_back.reshape(row_count, model_width),
            value_grad.reshape(row_count, model_width),
        ],
        axis=1,
    ).astype(jnp.bfloat16)
    joined_w_grad = outer_dot(normed, joined_grad)
    first_back, gain_first = norm_back(embedded, vectors[0], inner_dot(joined_grad, joined_w))
    embed_in = (second_grad + first_back).astype(jnp.bfloat16)
    embed_grad = jnp.concatenate(
        [outer_dot(patch_rows, embed_in), outer_dot(pos_low, embed_in)], axis=0
    )
    vector_grad = jnp.stack(
        [
            gain_first,
            gain_second,
            gain_final,
            gain_query.reshape(model_width),
            gain_key.reshape(model_width),
            probe_grad.reshape(model_width),
        ]
    )
    return (embed_grad, joined_w_grad, out_grad, up_grad, down_grad, vector_grad)


def reduce_grads(fresh):
    return (
        lax.psum_scatter(fresh[0], ("dp", "mp"), scatter_dimension=0, tiled=True),
        lax.psum_scatter(fresh[1], ("dp", "mp"), scatter_dimension=0, tiled=True),
        lax.psum_scatter(fresh[2], ("dp", "mp"), scatter_dimension=0, tiled=True),
        lax.psum_scatter(fresh[3], ("dp", "mp"), scatter_dimension=0, tiled=True),
        lax.psum_scatter(fresh[4], ("dp", "mp"), scatter_dimension=0, tiled=True),
        lax.psum_scatter(fresh[5], ("dp", "mp"), scatter_dimension=1, tiled=True),
    )


def combine_stats(earlier, later_one):
    top_score = jnp.maximum(earlier[0], later_one[0])
    exp_total = earlier[1] * jnp.exp(earlier[0] - top_score) + later_one[1] * jnp.exp(
        later_one[0] - top_score
    )
    return (top_score, exp_total, earlier[2] + later_one[2])


def lamb_update(weight, gradient, moment_one, moment_two, factor):
    gradient = gradient * factor
    moment_one = beta_first * moment_one + (1.0 - beta_first) * gradient
    moment_two = beta_second * moment_two + (1.0 - beta_second) * gradient * gradient
    update = (
        moment_one
        / (1.0 - beta_first**STEP)
        / (jnp.sqrt(moment_two / (1.0 - beta_second**STEP)) + adam_floor)
        + weight_decay * weight
    )
    return (moment_one, moment_two, update)


def body(
    patches,
    heights,
    widths,
    labels,
    res_weights,
    w_embed,
    w_qkv,
    w_out,
    w_up,
    w_down,
    vectors,
    w_cls,
    m_embed,
    v_embed,
    m_qkv,
    v_qkv,
    m_out,
    v_out,
    m_up,
    v_up,
    m_down,
    v_down,
    m_vectors,
    v_vectors,
    m_cls,
    v_cls,
):
    gathered = (
        lax.all_gather(w_embed.astype(jnp.bfloat16), ("dp", "mp"), axis=0, tiled=True),
        lax.all_gather(w_qkv.astype(jnp.bfloat16), ("dp", "mp"), axis=0, tiled=True),
        lax.all_gather(w_out.astype(jnp.bfloat16), ("dp", "mp"), axis=0, tiled=True),
        lax.all_gather(w_up.astype(jnp.bfloat16), ("dp", "mp"), axis=0, tiled=True),
        lax.all_gather(w_down.astype(jnp.bfloat16), ("dp", "mp"), axis=0, tiled=True),
        lax.all_gather(vectors.astype(jnp.bfloat16), ("dp", "mp"), axis=1, tiled=True),
    )
    weights_low = gathered[:5]
    vector_low = gathered[5]
    class_low = lax.all_gather(w_cls.astype(jnp.bfloat16), "dp", axis=0, tiled=True)
    member_index = lax.axis_index("mp")
    slot_count = heights.shape[1]
    own_start = member_index * slot_count
    own_weights = lax.dynamic_slice_in_dim(res_weights, own_start, slot_count, 1).astype(
        jnp.float32
    )
    weight_sum = lax.psum(jnp.sum(own_weights), ("dp", "mp"))
    class_count = class_low.shape[1]
    class_ids = member_index * class_count + jnp.arange(class_count, dtype=jnp.int32)
    loss_local = jnp.zeros((), jnp.float32)
    class_grad = jnp.zeros(class_low.shape, jnp.float32)
    summed = None
    for micro_index in range(patches.shape[0]):
        pooled, saved = layer_forward(
            weights_low, vector_low, patches[micro_index], heights[micro_index], widths[micro_index]
        )
        group_rows = lax.all_gather(pooled, "mp", axis=0, tiled=True)
        logits = jnp.dot(group_rows, class_low, preferred_element_type=jnp.float32)
        label_hit = labels[micro_index][:, None] == class_ids[None, :]
        top_score = jnp.max(logits, axis=1)
        exp_total = jnp.sum(jnp.exp(logits - top_score[:, None]), axis=1)
        picked = jnp.sum(jnp.where(label_hit, logits, 0.0), axis=1)
        merged = merged_2((top_score, exp_total, picked), "mp", combine_stats)
        log_total = merged[0] + jnp.log(merged[1])
        group_weights = res_weights[micro_index].astype(jnp.float32)
        weighted = group_weights * (log_total - merged[2])
        loss_local = loss_local + jnp.sum(
            lax.dynamic_slice_in_dim(weighted, own_start, slot_count, 0)
        )
        logit_grad = (
            (jnp.exp(logits - log_total[:, None]) - label_hit.astype(jnp.float32))
            * (group_weights / weight_sum)[:, None]
        ).astype(jnp.bfloat16)
        class_grad = class_grad + outer_dot(group_rows, logit_grad)
        pooled_grad = lax.psum_scatter(
            inner_dot(logit_grad, class_low), "mp", scatter_dimension=0, tiled=True
        )
        fresh = layer_backward(weights_low, vector_low, saved, pooled_grad)
        summed = fresh if summed is None else jax.tree.map(jnp.add, summed, fresh)
    summed = reduce_grads(summed)
    class_shard = lax.psum_scatter(class_grad, "dp", scatter_dimension=0, tiled=True)
    params = (w_embed, w_qkv, w_out, w_up, w_down, vectors, w_cls)
    moments = (
        (m_embed, v_embed),
        (m_qkv, v_qkv),
        (m_out, v_out),
        (m_up, v_up),
        (m_down, v_down),
        (m_vectors, v_vectors),
        (m_cls, v_cls),
    )
    gradients = (summed[0], summed[1], summed[2], summed[3], summed[4], summed[5], class_shard)
    matrix_order = (0, 1, 2, 3, 4, 6)
    grad_squares = jnp.concatenate(
        [
            jnp.stack(
                [jnp.sum(gradients[position] * gradients[position]) for position in matrix_order]
            ),
            jnp.sum(gradients[5] * gradients[5], axis=1),
        ]
    )
    square_sums, loss_total = lax.psum((grad_squares, loss_local), ("dp", "mp"))
    clip_norm = jnp.sqrt(jnp.sum(square_sums))
    factor = jnp.minimum(1.0, clip_limit / clip_norm)
    updated = [
        lamb_update(
            params[position],
            gradients[position],
            moments[position][0],
            moments[position][1],
            factor,
        )
        for position in range(7)
    ]
    matrix_parts = jnp.stack(
        [
            jnp.stack(
                [
                    jnp.sum(params[position] * params[position]),
                    jnp.sum(updated[position][2] * updated[position][2]),
                ]
            )
            for position in matrix_order
        ]
    )
    vector_parts = jnp.stack(
        [jnp.sum(params[5] * params[5], axis=1), jnp.sum(updated[5][2] * updated[5][2], axis=1)],
        axis=1,
    )
    norms = jnp.sqrt(lax.psum(jnp.concatenate([matrix_parts, vector_parts], axis=0), ("dp", "mp")))
    ratios = norms[:, 0] / norms[:, 1]
    outputs = [jnp.stack([loss_total, weight_sum]), clip_norm, norms]
    for position in range(7):
        if position == 5:
            ratio = ratios[6:][:, None]
        else:
            ratio = ratios[matrix_order.index(position)]
        moment_one, moment_two, update = updated[position]
        outputs += [params[position] - learn_rate * ratio * update, moment_one, moment_two]
    return tuple(outputs)


def solution(mesh):
    placed = (
        P(None, ("dp", "mp"), None),
        P(None, ("dp", "mp")),
        P(None, ("dp", "mp")),
        P(None, "dp"),
        P(None, "dp"),
        P(("dp", "mp"), None),
        P(("dp", "mp"), None),
        P(("dp", "mp"), None),
        P(("dp", "mp"), None),
        P(("dp", "mp"), None),
        P(None, ("dp", "mp")),
        P("dp", "mp"),
        P(("dp", "mp"), None),
        P(("dp", "mp"), None),
        P(("dp", "mp"), None),
        P(("dp", "mp"), None),
        P(("dp", "mp"), None),
        P(("dp", "mp"), None),
        P(("dp", "mp"), None),
        P(("dp", "mp"), None),
        P(("dp", "mp"), None),
        P(("dp", "mp"), None),
        P(None, ("dp", "mp")),
        P(None, ("dp", "mp")),
        P("dp", "mp"),
        P("dp", "mp"),
    )
    return jax.shard_map(
        body,
        mesh=mesh,
        in_specs=placed,
        out_specs=(
            P(),
            P(),
            P(),
            P(("dp", "mp"), None),
            P(("dp", "mp"), None),
            P(("dp", "mp"), None),
            P(("dp", "mp"), None),
            P(("dp", "mp"), None),
            P(("dp", "mp"), None),
            P(("dp", "mp"), None),
            P(("dp", "mp"), None),
            P(("dp", "mp"), None),
            P(("dp", "mp"), None),
            P(("dp", "mp"), None),
            P(("dp", "mp"), None),
            P(("dp", "mp"), None),
            P(("dp", "mp"), None),
            P(("dp", "mp"), None),
            P(None, ("dp", "mp")),
            P(None, ("dp", "mp")),
            P(None, ("dp", "mp")),
            P("dp", "mp"),
            P("dp", "mp"),
            P("dp", "mp"),
        ),
        check_vma=False,
    )
```

profile of v0, /device:TPU:0, one launch (start us, length us, event | category | flops | bytes accessed | tf_op | source)
XLA Modules:
  0.0 1467.9 jit_solution(6655106984188032592)
XLA Ops:
  25.4 42.4 %psum.29 = f32[]{:T(128)} all-reduce(f32[]{:T(128)} %convert_reduce_fusion.4), channel_id=1, replica_groups=mesh['dp'=8,'mp'=4] {'dp','mp'}, use_global_device_ids=true, to_apply=%region_102.103 | all-reduce | flops 1 | bytes 8 | tf_op jit(solution)/shard_map/psum | solution.py:361
  73.8 40.8 %all-gather.12 = bf16[32,24,6]{1,2,0:T(8,128)(2,1)S(1)} all-gather(bf16[1,24,6]{1,2,0:T(8,128)(2,1)S(1)} %convert_bitcast_fusion), channel_id=1, replica_groups=mesh['dp'=8,'mp'=4] {'dp','mp'}, dimensions={0}, use_global_device_ids=true | all-gather | bytes 9504 | tf_op jit(solution)/shard_map/all_gather | solution.py:350
  118.1 33.8 %all_gather.112 = bf16[768,250]{1,0:T(8,128)(2,1)} all-gather(bf16[96,250]{1,0:T(8,128)(2,1)S(1)} %convert_element_type.463), channel_id=1, replica_groups=mesh['dp'=8,'mp'=4] {'dp'}, dimensions={0}, use_global_device_ids=true | all-gather | bytes 432000 | tf_op jit(solution)/shard_map/all_gather | solution.py:354
  164.5 3.2 fusion.382
  193.7 2.3 copy.279
  231.0 2.5 fusion.419
  249.5 6.1 all-gather.25.cloned.1.call-done
  255.6 5.7 fusion.381
  261.3 60.1 %all-gather.27.cloned.1.call-done = bf16[3072,768]{1,0:T(8,128)(2,1)} async-done(((bf16[96,768]{1,0:T(8,128)(2,1)}), bf16[3072,768]{1,0:T(8,128)(2,1)}) %all-gather.27.cloned.1.call-update) | async-done | bytes 4718608 | tf_op jit(solution)/shard_map/all_gather | solution.py:349
  321.4 6.0 fusion.433
  353.4 6.7 all_gather.126
  370.9 5.5 all_gather.119
  376.5 2.4 fusion.441
  391.1 5.5 all_gather.133
  409.6 5.5 all_gather.111
  441.9 11.8 all-reduce.14
  484.3 4.0 while.50
  488.3 4.0 while.49
  492.3 3.9 while.48
  500.7 3.9 while.51
  514.2 2.6 convolution_add_fusion.2
  526.4 15.9 %reduce-scatter.12.cloned.1.call-done = f32[16,768]{1,0:T(8,128)} async-done(((f32[64,768]{1,0:T(8,128)}), f32[16,768]{1,0:T(8,128)}) %reduce-scatter.12.cloned.1.call-update) | async-done | bytes 49168 | tf_op jit(solution)/shard_map/reduce_scatter | solution.py:389
  547.7 17.3 %reduce-scatter.18.cloned.1.call-done = f32[16,768]{1,0:T(8,128)} async-done(((f32[64,768]{1,0:T(8,128)}), f32[16,768]{1,0:T(8,128)}) %reduce-scatter.18.cloned.1.call-update) | async-done | bytes 49168 | tf_op jit(solution)/shard_map/reduce_scatter | solution.py:389
  570.5 17.3 %reduce-scatter.16.cloned.1.call-done = f32[16,768]{1,0:T(8,128)} async-done(((f32[64,768]{1,0:T(8,128)}), f32[16,768]{1,0:T(8,128)}) %reduce-scatter.16.cloned.1.call-update) | async-done | bytes 49168 | tf_op jit(solution)/shard_map/reduce_scatter | solution.py:389
  593.3 2.5 fusion.91
  595.8 2.3 copy.299
  598.2 2.5 fusion.90
  600.7 2.3 copy.306
  605.4 2.5 fusion.93
  610.2 2.4 fusion.92
  612.6 2.3 copy.292
  615.0 4.6 multiply_reduce_fusion.10
  620.8 6.6 fusion.63
  629.9 4.3 fusion.56
  636.7 3.9 fusion.42
  643.1 4.1 fusion.49
  647.4 3.6 multiply_reduce_fusion.11
  651.0 2.5 fusion.405
  657.0 3.4 fusion.101
  668.9 3.4 fusion.98
  682.9 3.0 multiply_reduce_fusion.1
  689.9 2.7 fusion.107
  718.1 2.7 multiply_reduce_fusion.6
  737.4 2.6 fusion.161
  742.9 5.4 add_add_fusion.2
  749.5 4.3 fusion.347
  753.8 6.0 fusion.343
  759.9 5.9 fusion.345
  765.7 13.5 add_add_fusion
  780.4 3.0 fusion.386
  783.4 5.2 fusion.380
  788.6 5.2 fusion.383
  793.9 12.5 add_add_fusion.1
  814.1 39.7 %all-reduce.12 = f32[6,768]{1,0:T(8,128)S(1)} all-reduce(f32[6,768]{1,0:T(8,128)S(1)} %add_add_fusion.28), channel_id=24, replica_groups=mesh['dp'=8,'mp'=4] {'dp','mp'}, use_global_device_ids=true, to_apply=%region_191.192.clone | all-reduce | flops 4608 | bytes 36864
  857.1 76.3 %reduce-scatter.20.cloned.1.call-done = f32[32,768]{1,0:T(8,128)} async-done(((f32[1024,768]{1,0:T(8,128)}), f32[32,768]{1,0:T(8,128)}) %reduce-scatter.20.cloned.1.call-update) | async-done | bytes 98320 | tf_op jit(solution)/shard_map/reduce_scatter | solution.py:286
  934.9 122.3 %reduce-scatter.22.cloned.1.call-done = f32[24,2304]{1,0:T(8,128)} async-done(((f32[768,2304]{1,0:T(8,128)}), f32[24,2304]{1,0:T(8,128)}) %reduce-scatter.22.cloned.1.call-update) | async-done | bytes 221200 | tf_op jit(solution)/shard_map/reduce_scatter | solution.py:287
  1058.8 139.9 %reduce-scatter.28.cloned.1.call-done = f32[96,768]{1,0:T(8,128)} async-done(((f32[3072,768]{1,0:T(8,128)}), f32[96,768]{1,0:T(8,128)}) %reduce-scatter.28.cloned.1.call-update) | async-done | bytes 294928 | tf_op jit(solution)/shard_map/reduce_scatter | solution.py:290
  1200.4 138.7 %reduce-scatter.26.cloned.1.call-done = f32[24,3072]{1,0:T(8,128)} async-done(((f32[768,3072]{1,0:T(8,128)}), f32[24,3072]{1,0:T(8,128)}) %reduce-scatter.26.cloned.1.call-update) | async-done | bytes 294928 | tf_op jit(solution)/shard_map/reduce_scatter | solution.py:289
  1340.8 4.0 concatenate.58
  1345.4 40.0 %psum.30 = f32[12]{0:T(128)S(1)} all-reduce(f32[12]{0:T(128)S(1)} %concatenate.58), channel_id=1, replica_groups=mesh['dp'=8,'mp'=4] {'dp','mp'}, use_global_device_ids=true, to_apply=%region_193.194 | all-reduce | flops 12 | bytes 96 | tf_op jit(solution)/shard_map/psum | solution.py:416
  1390.5 2.7 maximum_bitcast_fusion
  1396.9 2.7 maximum_bitcast_fusion.4
  1404.0 2.7 maximum_bitcast_fusion.2
  1407.2 40.1 %all-reduce.13 = (f32[1]{0:T(128)}, f32[12,2]{0,1:T(2,128)S(1)}) all-reduce(f32[1]{0:T(128)} %bitcast.80, f32[12,2]{0,1:T(2,128)S(1)} %concatenate.59), channel_id=1, replica_groups=mesh['dp'=8,'mp'=4] {'dp','mp'}, use_global_device_ids=true, to_apply=%region_100.101 | all-reduce | flops 25 | bytes 200 | tf_op jit(solution)/shard_map/psum | solution.py:416
  (1414 shorter events, 411.2 us)
Async XLA Ops:
  7.2 144.7 %copy-start.439 = (u32[32]{0:T(128)S(1)}, u32[32]{0:T(128)}, u32[]{:S(2)}) copy-start(u32[32]{0:T(128)} %constant.623) | copy-start | bytes 388
  7.2 146.0 %copy-start.135 = (bf16[4,256,768]{2,1,0:T(8,128)(2,1)S(1)}, bf16[4,256,768]{2,1,0:T(8,128)(2,1)}, u32[]{:S(2)}) copy-start(bf16[4,256,768]{2,1,0:T(8,128)(2,1)} %param.34) | copy-start | bytes 4718596
  7.2 146.0 %all-gather.19.cloned.1.call-start = ((), (), s32[]{:S(2)}) async-start(), calls=%async_computation.10 | async-start | bytes 1622016 | tf_op jit(solution)/shard_map/all_gather | solution.py:345
  8.9 155.5 %all-gather.21.cloned.1.call-start = ((), (), s32[]{:S(2)}) async-start(), calls=%async_computation.11 | async-start | bytes 3649536 | tf_op jit(solution)/shard_map/all_gather | solution.py:346
  10.6 211.4 %all-gather.23.cloned.1.call-start = ((), (), s32[]{:S(2)}) async-start(), calls=%async_computation.12 | async-start | bytes 1216512 | tf_op jit(solution)/shard_map/all_gather | solution.py:347
  12.2 243.4 %all-gather.25.cloned.1.call-start = ((), (), s32[]{:S(2)}) async-start(), calls=%async_computation.13 | async-start | bytes 4866048 | tf_op jit(solution)/shard_map/all_gather | solution.py:348
  13.9 307.5 %all-gather.27.cloned.1.call-start = ((), (), s32[]{:S(2)}) async-start(), calls=%async_computation.14 | async-start | bytes 4866048 | tf_op jit(solution)/shard_map/all_gather | solution.py:349
  15.6 505.4 %reduce-scatter.14.cloned.1.call-start = ((), (), s32[]{:S(2)}) async-start(), calls=%async_computation.16 | async-start | bytes 245760 | tf_op jit(solution)/shard_map/reduce_scatter | solution.py:389
  71.0 91.3 %copy-start.243 = (pred[256,128]{1,0:T(32,128)(4,1)}, pred[256,128]{1,0:T(32,128)(4,1)S(1)}, u32[]{:S(2)}) copy-start(pred[256,128]{1,0:T(32,128)(4,1)S(1)} %iota_compare_fusion.7) | copy-start | bytes 98308
  71.5 85.2 %copy-start.245 = (pred[256,128]{1,0:T(32,128)(4,1)}, pred[256,128]{1,0:T(32,128)(4,1)S(1)}, u32[]{:S(2)}) copy-start(pred[256,128]{1,0:T(32,128)(4,1)S(1)} %iota_compare_fusion.5) | copy-start | bytes 98308
  71.9 87.8 %copy-start.247 = (pred[256,128]{1,0:T(32,128)(4,1)}, pred[256,128]{1,0:T(32,128)(4,1)S(1)}, u32[]{:S(2)}) copy-start(pred[256,128]{1,0:T(32,128)(4,1)S(1)} %iota_compare_fusion.1) | copy-start | bytes 98308
  72.4 84.8 %copy-start.255 = (pred[256,128]{1,0:T(32,128)(4,1)}, pred[256,128]{1,0:T(32,128)(4,1)S(1)}, u32[]{:S(2)}) copy-start(pred[256,128]{1,0:T(32,128)(4,1)S(1)} %iota_compare_fusion.3) | copy-start | bytes 98308
  72.5 89.8 %copy-start.251 = (pred[256,128]{1,0:T(32,128)(4,1)}, pred[256,128]{1,0:T(32,128)(4,1)S(1)}, u32[]{:S(2)}) copy-start(pred[256,128]{1,0:T(32,128)(4,1)S(1)} %iota_compare_fusion.6) | copy-start | bytes 98308
  72.6 84.1 %copy-start.253 = (pred[256,128]{1,0:T(32,128)(4,1)}, pred[256,128]{1,0:T(32,128)(4,1)S(1)}, u32[]{:S(2)}) copy-start(pred[256,128]{1,0:T(32,128)(4,1)S(1)} %iota_compare_fusion.4) | copy-start | bytes 98308
  72.8 87.0 %copy-start.249 = (pred[256,128]{1,0:T(32,128)(4,1)}, pred[256,128]{1,0:T(32,128)(4,1)S(1)}, u32[]{:S(2)}) copy-start(pred[256,128]{1,0:T(32,128)(4,1)S(1)} %iota_compare_fusion) | copy-start | bytes 98308
  72.9 84.4 %copy-start.257 = (pred[256,128]{1,0:T(32,128)(4,1)}, pred[256,128]{1,0:T(32,128)(4,1)S(1)}, u32[]{:S(2)}) copy-start(pred[256,128]{1,0:T(32,128)(4,1)S(1)} %iota_compare_fusion.2) | copy-start | bytes 98308
  116.1 92.2 %copy-start.170 = (f32[768]{0:T(1024)}, f32[768]{0:T(1024)S(1)}, u32[]{:S(2)}) copy-start(f32[768]{0:T(1024)S(1)} %get-tuple-element.1017) | copy-start | bytes 9220
  116.8 36.4 %copy-start.185 = (f32[12,64]{1,0:T(8,128)}, f32[12,64]{1,0:T(8,128)S(1)}, u32[]{:S(2)}) copy-start(f32[12,64]{1,0:T(8,128)S(1)} %mul.2455) | copy-start | bytes 9220
  224.3 112.1 %copy-start.300 = (f32[256]{0:T(256)}, f32[256]{0:T(256)S(1)}, u32[]{:S(2)}) copy-start(f32[256]{0:T(256)S(1)} %broadcast_multiply_fusion.21) | copy-start | bytes 3076
  240.9 86.7 %copy-start.349 = (f32[256]{0:T(256)}, f32[256]{0:T(256)S(1)}, u32[]{:S(2)}) copy-start(f32[256]{0:T(256)S(1)} %broadcast_multiply_fusion.15) | copy-start | bytes 3076
  246.9 89.5 %copy-start.333 = (f32[256]{0:T(256)}, f32[256]{0:T(256)S(1)}, u32[]{:S(2)}) copy-start(f32[256]{0:T(256)S(1)} %fusion.299) | copy-start | bytes 3076
  246.9 85.5 %copy-start.339 = (f32[256]{0:T(256)}, f32[256]{0:T(256)S(1)}, u32[]{:S(2)}) copy-start(f32[256]{0:T(256)S(1)} %fusion.302) | copy-start | bytes 3076
  247.0 80.7 %copy-start.381 = (f32[256]{0:T(256)}, f32[256]{0:T(256)S(1)}, u32[]{:S(2)}) copy-start(f32[256]{0:T(256)S(1)} %fusion.305) | copy-start | bytes 3076
  342.5 33.9 %copy-start.33 = (bf16[768,250]{1,0:T(8,128)(2,1)S(1)}, bf16[768,250]{1,0:T(8,128)(2,1)}, u32[]{:S(2)}) copy-start(bf16[768,250]{1,0:T(8,128)(2,1)} %all_gather.112) | copy-start | bytes 1152004
  500.6 41.6 %reduce-scatter.12.cloned.1.call-start = ((), (), s32[]{:S(2)}) async-start(), calls=%async_computation.15 | async-start | bytes 245760 | tf_op jit(solution)/shard_map/reduce_scatter | solution.py:389
  506.4 58.6 %reduce-scatter.18.cloned.1.call-start = ((), (), s32[]{:S(2)}) async-start(), calls=%async_computation.18 | async-start | bytes 245760 | tf_op jit(solution)/shard_map/reduce_scatter | solution.py:389
  512.4 75.5 %reduce-scatter.16.cloned.1.call-start = ((), (), s32[]{:S(2)}) async-start(), calls=%async_computation.17 | async-start | bytes 245760 | tf_op jit(solution)/shard_map/reduce_scatter | solution.py:389
  516.8 337.1 %reduce-scatter.30.cloned.1.call-start = ((), (), s32[]{:S(2)}) async-start(), calls=%async_computation.24 | async-start | bytes 884736 | tf_op jit(solution)/shard_map/reduce_scatter | solution.py:395
  520.7 334.8 %reduce-scatter.24.cloned.1.call-start = ((), (), s32[]{:S(2)}) async-start(), calls=%async_computation.21 | async-start | bytes 2433024 | tf_op jit(solution)/shard_map/reduce_scatter | solution.py:288
  523.7 65.7 %copy-start.111 = (bf16[256,768]{0,1:T(8,128)(2,1)S(1)}, bf16[256,768]{0,1:T(8,128)(2,1)}, u32[]{:S(2)}) copy-start(bf16[256,768]{0,1:T(8,128)(2,1)} %copy.274) | copy-start | bytes 1179652
  620.6 32.9 %copy-start.87 = (f32[256,768]{1,0:T(8,128)}, f32[256,768]{1,0:T(8,128)S(1)}, u32[]{:S(2)}) copy-start(f32[256,768]{1,0:T(8,128)S(1)} %get-tuple-element.1147) | copy-start | bytes 2359300
  620.6 32.9 %copy-start.384 = (f32[256]{0:T(256)}, f32[256]{0:T(256)S(1)}, u32[]{:S(2)}) copy-start(f32[256]{0:T(256)S(1)} %negate_multiply_fusion.16) | copy-start | bytes 3076
  620.7 65.3 %copy-start.386 = (f32[256]{0:T(256)}, f32[256]{0:T(256)S(1)}, u32[]{:S(2)}) copy-start(f32[256]{0:T(256)S(1)} %negate_multiply_fusion.10) | copy-start | bytes 3076
  692.7 25.0 %copy-start.130 = (bf16[12,64,256]{2,1,0:T(8,128)(2,1)}, bf16[12,64,256]{2,1,0:T(8,128)(2,1)S(1)}, u32[]{:S(2)}) copy-start(bf16[12,64,256]{2,1,0:T(8,128)(2,1)S(1)} %fusion.107) | copy-start | bytes 1179652
  728.4 205.0 %reduce-scatter.20.cloned.1.call-start = ((), (), s32[]{:S(2)}) async-start(), calls=%async_computation.19 | async-start | bytes 3244032 | tf_op jit(solution)/shard_map/reduce_scatter | solution.py:286
  737.4 319.8 %reduce-scatter.22.cloned.1.call-start = ((), (), s32[]{:S(2)}) async-start(), calls=%async_computation.20 | async-start | bytes 7299072 | tf_op jit(solution)/shard_map/reduce_scatter | solution.py:287
  748.4 450.3 %reduce-scatter.28.cloned.1.call-start = ((), (), s32[]{:S(2)}) async-start(), calls=%async_computation.23 | async-start | bytes 9732096 | tf_op jit(solution)/shard_map/reduce_scatter | solution.py:290
  779.3 559.8 %reduce-scatter.26.cloned.1.call-start = ((), (), s32[]{:S(2)}) async-start(), calls=%async_computation.22 | async-start | bytes 9732096 | tf_op jit(solution)/shard_map/reduce_scatter | solution.py:289
  806.7 580.0 %copy-start.182 = (f32[32,768]{1,0:T(8,128)S(1)}, f32[32,768]{1,0:T(8,128)}, u32[]{:S(2)}) copy-start(f32[32,768]{1,0:T(8,128)} %param.39) | copy-start | bytes 294916
  806.7 580.0 %copy-start.291 = (f32[32,768]{1,0:T(8,128)S(1)}, f32[32,768]{1,0:T(8,128)}, u32[]{:S(2)}) copy-start(f32[32,768]{1,0:T(8,128)} %param.46) | copy-start | bytes 294916
  806.7 580.0 %copy-start.292 = (f32[32,768]{1,0:T(8,128)S(1)}, f32[32,768]{1,0:T(8,128)}, u32[]{:S(2)}) copy-start(f32[32,768]{1,0:T(8,128)} %param.47) | copy-start | bytes 294916
  806.7 581.7 %copy-start.128 = (f32[24,2304]{1,0:T(8,128)S(1)}, f32[24,2304]{1,0:T(8,128)}, u32[]{:S(2)}) copy-start(f32[24,2304]{1,0:T(8,128)} %param.40) | copy-start | bytes 663556
  806.7 586.6 %copy-start.181 = (f32[96,250]{1,0:T(8,128)S(1)}, f32[96,250]{1,0:T(8,128)}, u32[]{:S(2)}) copy-start(f32[96,250]{1,0:T(8,128)} %param.45) | copy-start | bytes 288004
  806.8 588.2 %copy-start.126 = (f32[96,768]{1,0:T(8,128)S(1)}, f32[96,768]{1,0:T(8,128)}, u32[]{:S(2)}) copy-start(f32[96,768]{1,0:T(8,128)} %param.43) | copy-start | bytes 884740
  806.8 588.2 %copy-start.259 = (f32[96,768]{1,0:T(8,128)S(1)}, f32[96,768]{1,0:T(8,128)}, u32[]{:S(2)}) copy-start(f32[96,768]{1,0:T(8,128)} %param.54) | copy-start | bytes 884740
  812.5 587.3 %copy-start.217 = (f32[24,768]{1,0:T(8,128)S(1)}, f32[24,768]{1,0:T(8,128)}, u32[]{:S(2)}) copy-start(f32[24,768]{1,0:T(8,128)} %param.41) | copy-start | bytes 221188
  813.8 588.3 %copy-start.127 = (f32[24,3072]{1,0:T(8,128)S(1)}, f32[24,3072]{1,0:T(8,128)}, u32[]{:S(2)}) copy-start(f32[24,3072]{1,0:T(8,128)} %param.42) | copy-start | bytes 884740
  855.5 544.3 %copy-start.260 = (f32[24,768]{1,0:T(8,128)S(1)}, f32[24,768]{1,0:T(8,128)}, u32[]{:S(2)}) copy-start(f32[24,768]{1,0:T(8,128)} %reduce-scatter.24.cloned.1.call-done) | copy-start | bytes 221188
  1198.7 196.3 %copy-start.172 = (f32[96,768]{1,0:T(8,128)S(1)}, f32[96,768]{1,0:T(8,128)}, u32[]{:S(2)}) copy-start(f32[96,768]{1,0:T(8,128)} %reduce-scatter.28.cloned.1.call-done) | copy-start | bytes 884740
  1339.1 63.0 %copy-start.173 = (f32[24,3072]{1,0:T(8,128)S(1)}, f32[24,3072]{1,0:T(8,128)}, u32[]{:S(2)}) copy-start(f32[24,3072]{1,0:T(8,128)} %reduce-scatter.26.cloned.1.call-done) | copy-start | bytes 884740
  1386.8 20.0 %copy-start.299 = (f32[6,24]{1,0:T(8,128)S(1)}, f32[6,24]{1,0:T(8,128)}, u32[]{:S(2)}) copy-start(f32[6,24]{1,0:T(8,128)} %param.44) | copy-start | bytes 1732
  1386.8 20.0 %copy-start.432 = (f32[6,24]{1,0:T(8,128)S(1)}, f32[6,24]{1,0:T(8,128)}, u32[]{:S(2)}) copy-start(f32[6,24]{1,0:T(8,128)} %param.56) | copy-start | bytes 1732
  1388.4 68.2 %copy-start.237 = (f32[32,768]{1,0:T(8,128)}, f32[32,768]{1,0:T(8,128)S(1)}, u32[]{:S(2)}) copy-start(f32[32,768]{1,0:T(8,128)S(1)} %get-tuple-element.1134) | copy-start | bytes 294916
  1388.4 68.2 %copy-start.238 = (f32[32,768]{1,0:T(8,128)}, f32[32,768]{1,0:T(8,128)S(1)}, u32[]{:S(2)}) copy-start(f32[32,768]{1,0:T(8,128)S(1)} %get-tuple-element.1135) | copy-start | bytes 294916
  1390.5 67.7 %copy-start.183 = (f32[24,2304]{1,0:T(8,128)}, f32[24,2304]{1,0:T(8,128)S(1)}, u32[]{:S(2)}) copy-start(f32[24,2304]{1,0:T(8,128)S(1)} %get-tuple-element.1132) | copy-start | bytes 663556
  1390.5 67.7 %copy-start.184 = (f32[24,2304]{1,0:T(8,128)}, f32[24,2304]{1,0:T(8,128)S(1)}, u32[]{:S(2)}) copy-start(f32[24,2304]{1,0:T(8,128)S(1)} %get-tuple-element.1133) | copy-start | bytes 663556
  1395.0 64.0 %copy-start.239 = (f32[96,250]{1,0:T(8,128)}, f32[96,250]{1,0:T(8,128)S(1)}, u32[]{:S(2)}) copy-start(f32[96,250]{1,0:T(8,128)S(1)} %get-tuple-element.1124) | copy-start | bytes 288004
  1395.0 64.0 %copy-start.240 = (f32[96,250]{1,0:T(8,128)}, f32[96,250]{1,0:T(8,128)S(1)}, u32[]{:S(2)}) copy-start(f32[96,250]{1,0:T(8,128)S(1)} %get-tuple-element.1125) | copy-start | bytes 288004
  1396.9 63.0 %copy-start.174 = (f32[96,768]{1,0:T(8,128)}, f32[96,768]{1,0:T(8,128)S(1)}, u32[]{:S(2)}) copy-start(f32[96,768]{1,0:T(8,128)S(1)} %get-tuple-element.1126) | copy-start | bytes 884740
  1396.9 63.0 %copy-start.175 = (f32[96,768]{1,0:T(8,128)}, f32[96,768]{1,0:T(8,128)S(1)}, u32[]{:S(2)}) copy-start(f32[96,768]{1,0:T(8,128)S(1)} %get-tuple-element.1127) | copy-start | bytes 884740
  1404.0 56.0 %copy-start.176 = (f32[24,3072]{1,0:T(8,128)}, f32[24,3072]{1,0:T(8,128)S(1)}, u32[]{:S(2)}) copy-start(f32[24,3072]{1,0:T(8,128)S(1)} %get-tuple-element.1128) | copy-start | bytes 884740
  1404.0 56.0 %copy-start.177 = (f32[24,3072]{1,0:T(8,128)}, f32[24,3072]{1,0:T(8,128)S(1)}, u32[]{:S(2)}) copy-start(f32[24,3072]{1,0:T(8,128)S(1)} %get-tuple-element.1129) | copy-start | bytes 884740
  1407.0 52.9 %copy-start.367 = (f32[6,24]{1,0:T(8,128)}, f32[6,24]{1,0:T(8,128)S(1)}, u32[]{:S(2)}) copy-start(f32[6,24]{1,0:T(8,128)S(1)} %get-tuple-element.1122) | copy-start | bytes 1732
  1407.0 52.9 %copy-start.368 = (f32[6,24]{1,0:T(8,128)}, f32[6,24]{1,0:T(8,128)S(1)}, u32[]{:S(2)}) copy-start(f32[6,24]{1,0:T(8,128)S(1)} %get-tuple-element.1123) | copy-start | bytes 1732
  (397 other events, 1514.2 us)
Sparse Core Ops, SparseCore 0:
  11.5 57.7 all-gather.18
  72.7 59.5 all-gather.20
  135.8 53.8 all-gather.22
  193.0 62.5 all-gather.24
  258.9 62.4 all-gather.26
  500.7 18.6 reduce-scatter.13
  522.5 19.7 reduce-scatter.11
  545.3 19.7 reduce-scatter.17
  568.1 19.7 reduce-scatter.15
  591.0 62.4 reduce-scatter.29
  728.5 99.0 reduce-scatter.23
  832.9 100.4 reduce-scatter.19
  939.1 118.0 reduce-scatter.21
  1063.9 134.6 reduce-scatter.27
  1204.4 134.5 reduce-scatter.25
where the time goes:
time: 1480 us; the launch traced here: 1470 us
  waiting for transfers between devices  594 us (40%)
  blocking collectives  272 us (18%)
  matrix products  243 us (16%)
  local copies, waits for them, and re-layouts  165 us (11%)
  other arithmetic  163 us (11%)
  between operations  29.2 us (2%)
    reduce_scatter x1, waiting for transfers between devices, reduce_grads(): lax.psum_scatter(fresh[4], ('dp', 'mp'), scatter_dimension=0, tiled=True)  140 us
    reduce_scatter x1, waiting for transfers between devices, reduce_grads(): lax.psum_scatter(fresh[3], ('dp', 'mp'), scatter_dimension=0, tiled=True)  139 us
    reduce_scatter x1, waiting for transfers between devices, reduce_grads(): lax.psum_scatter(fresh[1], ('dp', 'mp'), scatter_dimension=0, tiled=True)  122 us
    dot_general x28, matrix products, outer_dot(): lax.dot_general(left, right, (((0,), (0,)), ((), ())), preferred_element_...  82.5 us
    psum x2, blocking collectives, body(): square_sums, loss_total = lax.psum((grad_squares, loss_local), ('dp', 'mp'))  80.1 us
    reduce_scatter x1, waiting for transfers between devices, reduce_grads(): lax.psum_scatter(fresh[0], ('dp', 'mp'), scatter_dimension=0, tiled=True)  76.3 us
    unnamed x918, local copies, waits for them, and re-layouts  62.1 us
    all_gather x1, waiting for transfers between devices, body(): lax.all_gather(w_down.astype(jnp.bfloat16), ('dp', 'mp'), axis=0, tiled=T...  60.1 us
  transfers between devices with their start and end apart: 15, of which 9 were waited for; matrix products, arithmetic and copies ran while one was open for 24% of the time, Pallas kernels for 0%

commit v1 on v0

--- a/solution.py
+++ b/solution.py
@@ -1,6 +1,10 @@
+import functools
+
 import jax
 import jax.numpy as jnp
 from jax import lax
+from jax.experimental import pallas as pl
+from jax.experimental.pallas import tpu as pltpu
 from jax.sharding import PartitionSpec as P
 
 HEAD = 64
@@ -83,55 +87,37 @@
 
 
 def attend(queries, key_rows, value_rows, segment):
-    block_rows = min(512, queries.shape[0])
-
-    def one_block(block_index):
-        query_block, scores = block_scores(queries, key_rows, segment)
-        top_score = jnp.max(scores, axis=-1, keepdims=True)
-        exp_scores = jnp.exp(scores - top_score)
-        exp_total = jnp.sum(exp_scores, axis=-1, keepdims=True)
-        attention = (exp_scores / exp_total).astype(jnp.bfloat16)
-        result = jnp.einsum(
-            "hts,shd->thd", attention, value_rows, preferred_element_type=jnp.float32
-        )
-        return (result.astype(jnp.bfloat16), (top_score + jnp.log(exp_total))[..., 0])
-
-    mixed_heads, log_total = lax.map(one_block, jnp.arange(queries.shape[0] // block_rows))
-    return (mixed_heads.reshape(queries.shape), log_total)
+    query_block, scores = block_scores(queries, key_rows, segment)
+    top_score = jnp.max(scores, axis=-1, keepdims=True)
+    exp_scores = jnp.exp(scores - top_score)
+    exp_total = jnp.sum(exp_scores, axis=-1, keepdims=True)
+    attention = (exp_scores / exp_total).astype(jnp.bfloat16)
+    result = jnp.einsum("hts,shd->thd", attention, value_rows, preferred_element_type=jnp.float32)
+    return (result.astype(jnp.bfloat16), (top_score + jnp.log(exp_total))[..., 0])
 
 
 def attend_back(queries, key_rows, value_rows, segment, log_total, mixed_grad):
-    block_rows = min(512, queries.shape[0])
-
-    def one_block(running, block_index):
-        key_grad, value_grad = running
-        query_block, scores = block_scores(queries, key_rows, segment)
-        attention = jnp.exp(scores - log_total[block_index][..., None])
-        value_grad = value_grad + jnp.einsum(
-            "hts,thd->shd",
-            attention.astype(jnp.bfloat16),
-            mixed_grad,
-            preferred_element_type=jnp.float32,
-        )
-        prob_grad = jnp.einsum(
-            "thd,shd->hts", mixed_grad, value_rows, preferred_element_type=jnp.float32
-        )
-        score_grad = (
-            attention * (prob_grad - jnp.sum(attention * prob_grad, axis=-1, keepdims=True))
-        ).astype(jnp.bfloat16)
-        query_grad = jnp.einsum(
-            "hts,shd->thd", score_grad, key_rows, preferred_element_type=jnp.float32
-        ) * HEAD ** (-0.5)
-        key_grad = key_grad + jnp.einsum(
-            "hts,thd->shd", score_grad, query_block, preferred_element_type=jnp.float32
-        ) * HEAD ** (-0.5)
-        return ((key_grad, value_grad), query_grad)
-
-    zero_grad = jnp.zeros(key_rows.shape, jnp.float32)
-    sums, query_grad = lax.scan(
-        one_block, (zero_grad, zero_grad), jnp.arange(queries.shape[0] // block_rows)
-    )
-    return (query_grad.reshape(queries.shape), sums[0], sums[1])
+    query_block, scores = block_scores(queries, key_rows, segment)
+    attention = jnp.exp(scores - log_total[..., None])
+    value_grad = jnp.einsum(
+        "hts,thd->shd",
+        attention.astype(jnp.bfloat16),
+        mixed_grad,
+        preferred_element_type=jnp.float32,
+    )
+    prob_grad = jnp.einsum(
+        "thd,shd->hts", mixed_grad, value_rows, preferred_element_type=jnp.float32
+    )
+    score_grad = (
+        attention * (prob_grad - jnp.sum(attention * prob_grad, axis=-1, keepdims=True))
+    ).astype(jnp.bfloat16)
+    query_grad = jnp.einsum(
+        "hts,shd->thd", score_grad, key_rows, preferred_element_type=jnp.float32
+    ) * HEAD ** (-0.5)
+    key_grad = jnp.einsum(
+        "hts,thd->shd", score_grad, query_block, preferred_element_type=jnp.float32
+    ) * HEAD ** (-0.5)
+    return (query_grad, key_grad, value_grad)
 
 
 def layer_forward(weights_low, vector_low, patch_rows, heights, widths):
@@ -240,14 +226,11 @@
         residual, vectors[2], final_grad.reshape(row_count, model_width)
     )
     down_in = residual_grad.astype(jnp.bfloat16)
-    down_grad = outer_dot(active, down_in)
     active_grad = inner_dot(down_in, down_w)
     upward_grad = jax.vjp(jax.nn.gelu, upward)[1](active_grad)[0].astype(jnp.bfloat16)
-    up_grad = outer_dot(hidden, upward_grad)
     second_back, gain_second = norm_back(second, vectors[1], inner_dot(upward_grad, up_w))
     second_grad = residual_grad + second_back
     out_in = second_grad.astype(jnp.bfloat16)
-    out_grad = outer_dot(mixed_flat, out_in)
     mixed_grad = inner_dot(out_in, out_w).astype(jnp.bfloat16).reshape(row_count, head_count, HEAD)
     query_grad, key_grad, value_grad = attend_back(
         queries, key_rows, value_rows, segment, log_total, mixed_grad
@@ -262,12 +245,9 @@
         ],
         axis=1,
     ).astype(jnp.bfloat16)
-    joined_w_grad = outer_dot(normed, joined_grad)
     first_back, gain_first = norm_back(embedded, vectors[0], inner_dot(joined_grad, joined_w))
     embed_in = (second_grad + first_back).astype(jnp.bfloat16)
-    embed_grad = jnp.concatenate(
-        [outer_dot(patch_rows, embed_in), outer_dot(pos_low, embed_in)], axis=0
-    )
+    inputs = jnp.concatenate([patch_rows, pos_low], axis=1)
     vector_grad = jnp.stack(
         [
             gain_first,
@@ -278,7 +258,14 @@
             probe_grad.reshape(model_width),
         ]
     )
-    return (embed_grad, joined_w_grad, out_grad, up_grad, down_grad, vector_grad)
+    pairs = (
+        (inputs, embed_in),
+        (normed, joined_grad),
+        (mixed_flat, out_in),
+        (hidden, upward_grad),
+        (active, down_in),
+    )
+    return (pairs, vector_grad)
 
 
 def reduce_grads(fresh):
@@ -389,7 +376,8 @@
         pooled_grad = lax.psum_scatter(
             inner_dot(logit_grad, class_low), "mp", scatter_dimension=0, tiled=True
         )
-        fresh = layer_backward(weights_low, vector_low, saved, pooled_grad)
+        pairs, vector_grad = layer_backward(weights_low, vector_low, saved, pooled_grad)
+        fresh = tuple(outer_dot(left, right) for left, right in pairs) + (vector_grad,)
         summed = fresh if summed is None else jax.tree.map(jnp.add, summed, fresh)
     summed = reduce_grads(summed)
     class_shard = lax.psum_scatter(class_grad, "dp", scatter_dimension=0, tiled=True)
@@ -454,6 +442,592 @@
     return tuple(outputs)
 
 
+MESH_ID = pl.DeviceIdType.MESH
+CORES = 2
+ALL = slice(None)
+LOW = jnp.bfloat16
+FULL = jnp.float32
+
+
+class Place:
+    def __init__(self, dims):
+        self.sizes = dict(dims, c=CORES)
+        dp, mp = lax.axis_index("dp"), lax.axis_index("mp")
+        wide = self.sizes["y"]
+        self.at = {"z": dp // wide, "y": dp % wide, "x": mp // CORES, "c": mp % CORES}
+
+    def peer(self, axis, step):
+        at = dict(self.at)
+        at[axis] = self.source(axis, -step)
+        return (at["z"] * self.sizes["y"] + at["y"], at["x"] * CORES + at["c"])
+
+    def source(self, axis, step):
+        size = self.sizes[axis]
+        return (self.at[axis] + (size - step) % size) % size
+
+    def steps(self, axis):
+        return range(1, self.sizes[axis])
+
+    def greet(self):
+        barrier = pltpu.get_barrier_semaphore()
+        count = 0
+        for axis in "cxyz":
+            for step in self.steps(axis):
+                pl.semaphore_signal(
+                    barrier, inc=1, device_id=self.peer(axis, step), device_id_type=MESH_ID
+                )
+                count += 1
+        pl.semaphore_wait(barrier, count)
+
+
+class Courier:
+    def __init__(self, place, send, recv):
+        self.place, self.send, self.recv, self.sent = place, send, recv, []
+
+    def start(self, axis, step, source, target):
+        slot = len(self.sent)
+        copy = pltpu.make_async_remote_copy(
+            src_ref=source,
+            dst_ref=target,
+            send_sem=self.send.at[slot],
+            recv_sem=self.recv.at[slot],
+            device_id=self.place.peer(axis, step),
+            device_id_type=MESH_ID,
+        )
+        copy.start()
+        self.sent.append(copy)
+        return copy
+
+    def finish(self):
+        for copy in self.sent:
+            copy.wait_send()
+
+
+class Spread:
+    def __init__(self, courier, view, order):
+        self.courier, self.place, self.view, self.order = courier, courier.place, view, order
+        self.relayed = []
+
+    def part(self, stage, **fixed):
+        where = {axis: self.place.at[axis] for axis in "xyz"}
+        for axis in ("z" + self.order)[:stage]:
+            where[axis] = ALL
+        where.update(fixed)
+        return self.view(**where)
+
+    def send(self, axis, stage):
+        part = self.part(stage)
+        return [self.courier.start(axis, step, part, part) for step in self.place.steps(axis)]
+
+    def relay(self, part):
+        self.relayed.append(self.courier.start("c", 1, part, part))
+
+    def begin(self):
+        self.coming = self.send("z", 0)
+
+    def middle(self, stage):
+        for copy in self.coming:
+            copy.wait_recv()
+        if stage == 1:
+            self.relay(self.part(1))
+        else:
+            axis = self.order[stage - 2]
+            for step in self.place.steps(axis):
+                self.relay(self.part(stage - 1, **{axis: self.place.source(axis, step)}))
+        self.coming = self.send(self.order[stage - 1], stage) if stage < 3 else []
+
+    def done(self):
+        for copy in self.relayed:
+            copy.wait_recv()
+
+
+class Fold:
+    def __init__(self, courier, view, order, stage_refs, axes):
+        self.courier, self.place, self.view, self.order = courier, courier.place, view, order
+        self.held, self.first, self.second, self.third = stage_refs
+        self.axes = axes
+
+    def key(self, **fixed):
+        return tuple(fixed.get(axis, ALL) for axis in self.axes)
+
+    def begin(self):
+        place = self.place
+        self.coming = [self.courier.start("c", 1, self.view(1 - place.at["c"]), self.held)]
+
+    def landed(self):
+        for copy in self.coming:
+            copy.wait_recv()
+
+    def send(self, axis, target, **fixed):
+        place = self.place
+        self.coming = [
+            self.courier.start(
+                axis,
+                step,
+                self.held.at[self.key(**{axis: place.source(axis, -step)}, **fixed)],
+                target.at[step - 1],
+            )
+            for step in place.steps(axis)
+        ]
+
+    def between_cores(self):
+        self.landed()
+        mine = self.view(self.place.at["c"])
+        held = self.held
+        count = held.shape[0]
+
+        def one(lead, carry):
+            held[lead] = (mine[lead].astype(FULL) + held[lead].astype(FULL)).astype(LOW)
+            return carry
+
+        lax.fori_loop(0, count, one, 0)
+        self.send(self.order[0], self.first)
+
+    def along_first(self):
+        self.landed()
+        axis = self.order[0]
+        here = self.held.at[self.key(**{axis: self.place.at[axis]})]
+        came = self.first
+
+        def one(lead, carry):
+            total = here[lead].astype(FULL)
+            for step in range(came.shape[0]):
+                total = total + came[step, lead].astype(FULL)
+            here[lead] = total.astype(LOW)
+            return carry
+
+        lax.fori_loop(0, here.shape[0], one, 0)
+        self.send(self.order[1], self.second, **{axis: self.place.at[axis]})
+
+    def along_second(self):
+        self.landed()
+        place = self.place
+        here = self.held.at[self.key(x=place.at["x"], y=place.at["y"])]
+        came = self.second
+
+        def one(lead, carry):
+            total = here[lead].astype(FULL)
+            for step in range(came.shape[0]):
+                total = total + came[step, lead].astype(FULL)
+            here[lead] = total.astype(LOW)
+            return carry
+
+        lax.fori_loop(0, here.shape[0], one, 0)
+        self.send("z", self.third, x=place.at["x"], y=place.at["y"])
+
+    def along_z(self):
+        self.landed()
+        place = self.place
+        total = self.held[self.key(x=place.at["x"], y=place.at["y"], z=place.at["z"])].astype(FULL)
+        for step in range(self.third.shape[0]):
+            total = total + self.third[step].astype(FULL)
+        return total
+
+
+class Total:
+    def __init__(self, courier, slots):
+        self.courier, self.place, self.slots = courier, courier.place, slots
+        self.axes = list("cxyz")
+
+    def begin(self, block):
+        self.send("c", block)
+
+    def send(self, axis, block):
+        place, slots = self.place, self.slots["cxyz".index(axis)]
+        mine = slots.at[place.at[axis]]
+        mine[...] = block
+        self.coming = [self.courier.start(axis, step, mine, mine) for step in place.steps(axis)]
+
+    def sum(self, axis):
+        for copy in self.coming:
+            copy.wait_recv()
+        slots = self.slots["cxyz".index(axis)]
+        total = slots[0]
+        for index in range(1, slots.shape[0]):
+            total = total + slots[index]
+        return total
+
+    def advance(self, axis):
+        following = "cxyz".index(axis) + 1
+        total = self.sum(axis)
+        if following < 4:
+            self.send("cxyz"[following], total)
+        return total
+
+    def through(self, block):
+        self.begin(block)
+        for axis in "cxyz":
+            total = self.advance(axis)
+        return total
+
+
+def total_slots(dims, shape):
+    sizes = dict(dims, c=CORES)
+    return [pltpu.VMEM((sizes[axis],) + shape, FULL) for axis in "cxyz"]
+
+
+def cut(rows, width, parts):
+    if rows % (16 * parts) == 0:
+        size = rows // parts
+        return [((part * size, size), (0, width)) for part in range(parts)]
+    units = width // 128
+    marks = [units * part // parts * 128 for part in range(parts + 1)]
+    return [((0, rows), (low, high - low)) for low, high in zip(marks, marks[1:]) if high > low]
+
+
+def pieces_of(blocks, class_block):
+    found = []
+    turn = 0
+    for index, (rows, width) in enumerate(blocks + [class_block]):
+        parts = max(2, min(4, rows * width * 2 // 32768 // 2 * 2))
+        for row_range, column_range in cut(rows, width, parts):
+            found.append((index, row_range, column_range, ("xy", "yx")[turn % 2]))
+            turn += 1
+    return found
+
+
+def block_ref(ref, class_ref, place, piece, core):
+    index, rows, columns, _ = piece
+
+    def of_matrix(z, y, x):
+        half = ref.shape[-1] // CORES
+        across = pl.ds(pl.multiple_of(core * half + columns[0], 128), columns[1])
+        return ref.at[z, y, x, pl.ds(rows[0], rows[1]), across]
+
+    def of_classes(z, y, x):
+        return class_ref.at[x, core, z, y, pl.ds(rows[0], rows[1])]
+
+    return of_matrix if ref is not None else of_classes
+
+
+def gather_kernel(dims, pieces, *refs):
+    shards, (vectors, weights, w_cls), refs = refs[:5], refs[5:8], refs[8:]
+    full, (g_cls, g_vec), refs = refs[:5], refs[5:7], refs[7:]
+    pairs, (send, recv) = refs[:5], refs[5:]
+    place = Place(dims)
+    place.greet()
+    courier = Courier(place, send, recv)
+    z, y, x, core = (place.at[axis] for axis in "zyxc")
+    arriving = []
+    for shard, pair in zip(shards, pairs):
+        rows, half = shard.shape[0], shard.shape[1] // CORES
+        at = pl.ds(pl.multiple_of(core * rows, 8), rows)
+        other = pl.ds(pl.multiple_of((1 - core) * half, 128), half)
+        arriving.append(courier.start("c", 1, shard.at[:, other], pair.at[at]))
+        pair[at] = shard[:, pl.ds(pl.multiple_of(core * half, 128), half)]
+    small = jnp.zeros((8, 128), FULL)
+    g_vec[z, y, x, core] = small
+    count = vectors.shape[1]
+    g_vec[z, y, x, core, pl.ds(0, 6), pl.ds(0, count)] = vectors[...].astype(LOW).astype(FULL)
+    width = weights.shape[1]
+    slots = width // (dims["x"] * CORES)
+    own = (x * CORES + core) * slots
+    lanes = lax.broadcasted_iota(jnp.int32, weights.shape, 1)
+    inside = (lanes >= own) & (lanes < own + slots)
+    counted = jnp.sum(jnp.where(inside, weights[...], 0).astype(FULL), axis=0, keepdims=True)
+    g_vec[z, y, x, core, pl.ds(6, 1), pl.ds(0, width)] = counted
+    block = g_cls.at[x, core, z, y]
+    block[...] = jnp.zeros(block.shape, LOW)
+    block[:, pl.ds(0, w_cls.shape[1])] = w_cls[...].astype(LOW)
+    spreads = [Spread(courier, lambda z, y, x: g_vec.at[z, y, x, core], "xy")]
+    first_of = {}
+    for piece in pieces:
+        index = piece[0]
+        if index < 5:
+            first_of.setdefault(index, len(spreads))
+        view = block_ref(full[index] if index < 5 else None, g_cls, place, piece, core)
+        spreads.append(Spread(courier, view, piece[3]))
+    ready = {position: index for index, position in first_of.items()}
+
+    def begin(position):
+        if position in ready:
+            index = ready[position]
+            arriving[index].wait_recv()
+            half = pairs[index].shape[1]
+            across = pl.ds(pl.multiple_of(core * half, 128), half)
+            full[index][z, y, x, :, across] = pairs[index][...].astype(LOW)
+        spreads[position].begin()
+
+    count = len(spreads)
+    steps = ((-2, begin), (0, lambda i: spreads[i].middle(1)), (2, lambda i: spreads[i].middle(2)))
+    steps += ((4, lambda i: spreads[i].middle(3)), (6, lambda i: spreads[i].done()))
+    for turn in range(-2, count + 6):
+        for lag, action in steps:
+            if 0 <= turn - lag < count:
+                action(turn - lag)
+    courier.finish()
+
+
+def copies_per_piece(dims):
+    X, Y, Z = (dims[axis] for axis in "xyz")
+    return (Z - 1) + 2 * (X - 1) + 2 * (Y - 1) + 1
+
+
+def gather_weights(dims, mats, vectors, weights, w_cls):
+    X, Y, Z = (dims[axis] for axis in "xyz")
+    blocks = [(CORES * w.shape[0], w.shape[1] // CORES) for w in mats]
+    padded = -(-w_cls.shape[1] // 128) * 128
+    pieces = pieces_of(blocks, (w_cls.shape[0], padded))
+    outs = [jax.ShapeDtypeStruct((Z, Y, X, CORES * w.shape[0], w.shape[1]), LOW) for w in mats]
+    outs.append(jax.ShapeDtypeStruct((X, CORES, Z, Y, w_cls.shape[0], padded), LOW))
+    outs.append(jax.ShapeDtypeStruct((Z, Y, X, CORES, 8, 128), FULL))
+    count = 5 + (1 + len(pieces)) * copies_per_piece(dims)
+    scratch = [pltpu.VMEM(block, FULL) for block in blocks]
+    scratch += [pltpu.SemaphoreType.DMA((count,)), pltpu.SemaphoreType.DMA((count,))]
+    whole = pl.BlockSpec(memory_space=pltpu.VMEM)
+    return pl.pallas_call(
+        functools.partial(gather_kernel, dims, pieces),
+        out_shape=outs,
+        in_specs=[whole] * 8,
+        out_specs=[whole] * 7,
+        scratch_shapes=scratch,
+        compiler_params=pltpu.CompilerParams(
+            collective_id=0, has_side_effects=True, vmem_limit_bytes=60 << 20
+        ),
+    )(*mats, vectors, weights, w_cls)
+
+
+def squares(values):
+    rows, width = values.shape
+    total = jnp.zeros((1, 128), FULL)
+    whole = width // 128 * 128
+    for low in range(0, whole, 128):
+        part = values[:, low : low + 128]
+        total = total + jnp.sum(part * part, axis=0, keepdims=True)
+    if whole < width:
+        part = values[:, whole:]
+        rest = jnp.sum(part * part, axis=0, keepdims=True)
+        total = total + jnp.concatenate([rest, jnp.zeros((1, 128 - rest.shape[1]), FULL)], axis=1)
+    return total
+
+
+def wide_rows(values):
+    squared = values * values
+    return jnp.concatenate([squared, jnp.zeros((squared.shape[0], 128 - squared.shape[1]), FULL)], axis=1)
+
+
+def moments_step(gradient, moment_one, moment_two):
+    first = beta_first * moment_one + (1.0 - beta_first) * gradient
+    second = beta_second * moment_two + (1.0 - beta_second) * gradient * gradient
+    return first, second
+
+
+def update_of(first, second, weight):
+    return (
+        first
+        / (1.0 - beta_first**STEP)
+        / (jnp.sqrt(second / (1.0 - beta_second**STEP)) + adam_floor)
+        + weight_decay * weight
+    )
+
+
+def step_kernel(dims, pieces, *refs):
+    grads, (g_cls, g_vec), refs = refs[:5], refs[5:7], refs[7:]
+    params, moments, refs = refs[:7], refs[7:21], refs[21:]
+    (loss_out, clip_out, norm_out), outs, refs = refs[:3], refs[3:24], refs[24:]
+    shards, wholes, refs = refs[:7], refs[7:12], refs[12:]
+    updates, refs = refs[:7], refs[7:]
+    slots_vec, slots_one, slots_two, refs = refs[:4], refs[4:8], refs[8:12], refs[12:]
+    (send, recv), stage_refs = refs[:2], refs[2:]
+    place = Place(dims)
+    place.greet()
+    courier = Courier(place, send, recv)
+    z, y, x, core = (place.at[axis] for axis in "zyxc")
+    folds = []
+    for position, piece in enumerate(pieces):
+        index = piece[0]
+        ref = grads[index] if index < 5 else None
+
+        def view(core, piece=piece, ref=ref):
+            return block_ref(ref, g_cls, place, piece, core)(ALL, ALL, ALL)
+
+        axes = "zyx" if index < 5 else "xzy"
+        folds.append(Fold(courier, view, piece[3], stage_refs[4 * position : 4 * position + 4], axes))
+    left = {index: sum(piece[0] == index for piece in pieces) for index in range(6)}
+    closing = {}
+
+    def finish(position):
+        index, rows, columns, _ = pieces[position]
+        total = folds[position].along_z()
+        if index == 5:
+            own = shards[6]
+            own[pl.ds(rows[0], rows[1])] = total[:, : own.shape[1]]
+            return
+        whole, own = wholes[index], shards[index]
+        whole[pl.ds(rows[0], rows[1]), pl.ds(columns[0], columns[1])] = total
+        left[index] -= 1
+        if left[index] == 0:
+            count, half = own.shape[0], own.shape[1] // CORES
+            across = pl.ds(pl.multiple_of(core * half, 128), half)
+            other = whole.at[pl.ds(pl.multiple_of((1 - core) * count, 8), count)]
+            closing[index] = courier.start("c", 1, other, own.at[:, across])
+            own[:, across] = whole[pl.ds(pl.multiple_of(core * count, 8), count)]
+
+    vec_total = Total(courier, slots_vec)
+    vec_total.begin(g_vec[...])
+    count = len(folds)
+    steps = ((-3, lambda i: folds[i].begin()), (0, lambda i: folds[i].between_cores()))
+    steps += ((2, lambda i: folds[i].along_first()), (4, lambda i: folds[i].along_second()), (6, finish))
+    for turn in range(-3, count + 6):
+        for lag, action in steps:
+            if 0 <= turn - lag < count:
+                action(turn - lag)
+    for axis in "cxyz":
+        vec_sum = vec_total.advance(axis)
+    for index in range(5):
+        closing[index].wait_recv()
+    vec_count = params[5].shape[1]
+    own = ((z * dims["y"] + y) * dims["x"] + x) * CORES + core
+    at_row = lax.broadcasted_iota(jnp.int32, (vec_sum.shape[1], 128), 0)
+    at_lane = lax.broadcasted_iota(jnp.int32, (vec_sum.shape[1], 128), 1)
+    chosen = ((at_row == own * vec_count + at_lane) & (at_lane < vec_count)).astype(FULL)
+    picked = jnp.dot(vec_sum, chosen, precision=highest, preferred_element_type=FULL)
+    shards[5][...] = picked[:6, :vec_count]
+    mats = (0, 1, 2, 3, 4, 6)
+    blank = jnp.zeros((6, 128), FULL)
+    parts = [squares(shards[i][...]) for i in mats] + [squares(params[i][...]) for i in mats]
+    block = jnp.concatenate(parts + [wide_rows(params[5][...]), blank], axis=0)
+    block = Total(courier, slots_one).through(block)
+    sums = jnp.sum(block, axis=1, keepdims=True)
+    vec_squares = jnp.sum(vec_sum * vec_sum, axis=1, keepdims=True)
+    loss_out[...] = vec_sum[6:7, :2]
+    clip_norm = jnp.sqrt(
+        jnp.sum(sums[:6], axis=0, keepdims=True) + jnp.sum(vec_squares[:6], axis=0, keepdims=True)
+    )
+    clip_out[...] = clip_norm
+    factor = jnp.minimum(1.0, clip_limit / clip_norm)
+    for index in range(7):
+        weight = params[index][...]
+        first, second = moments_step(
+            shards[index][...] * factor, moments[2 * index][...], moments[2 * index + 1][...]
+        )
+        outs[3 * index + 1][...] = first
+        outs[3 * index + 2][...] = second
+        updates[index][...] = update_of(first, second, weight)
+    parts = [squares(updates[i][...]) for i in mats]
+    block = jnp.concatenate(parts + [wide_rows(updates[5][...]), jnp.zeros((4, 128), FULL)], axis=0)
+    block = Total(courier, slots_two).through(block)
+    grown = jnp.sqrt(jnp.sum(block, axis=1, keepdims=True))
+    weight_norms = jnp.sqrt(sums[6:18])
+    norm_out[:, 0:1] = weight_norms
+    norm_out[:, 1:2] = grown[:12]
+    ratios = weight_norms / grown[:12]
+    for row, index in enumerate(mats):
+        ratio = learn_rate * ratios[row : row + 1]
+        outs[3 * index][...] = params[index][...] - ratio * updates[index][...]
+    outs[15][...] = params[5][...] - learn_rate * ratios[6:12] * updates[5][...]
+    courier.finish()
+
+
+def take_step(dims, grads, g_cls, g_vec, params, moments):
+    X, Y, Z = (dims[axis] for axis in "xyz")
+    mats = params[:5]
+    blocks = [(CORES * w.shape[0], w.shape[1] // CORES) for w in mats]
+    class_block = g_cls.shape[-2:]
+    pieces = pieces_of(blocks, class_block)
+    pieces = [piece for index in (5, 4, 3, 2, 1, 0) for piece in pieces if piece[0] == index]
+    outs = [jax.ShapeDtypeStruct((1, 2), FULL), jax.ShapeDtypeStruct((1, 1), FULL)]
+    outs.append(jax.ShapeDtypeStruct((12, 2), FULL))
+    for param in params:
+        outs += [jax.ShapeDtypeStruct(param.shape, FULL)] * 3
+    scratch = [pltpu.VMEM(param.shape, FULL) for param in params]
+    scratch += [pltpu.VMEM(block, FULL) for block in blocks]
+    scratch += [pltpu.VMEM(param.shape, FULL) for param in params]
+    scratch += total_slots(dims, g_vec.shape) + total_slots(dims, (24, 128)) + total_slots(dims, (16, 128))
+    count = 5 + 3 * (1 + X - 1 + Y - 1 + Z - 1) + len(pieces) * (1 + X - 1 + Y - 1 + Z - 1)
+    scratch += [pltpu.SemaphoreType.DMA((count,)), pltpu.SemaphoreType.DMA((count,))]
+    for index, rows, columns, order in pieces:
+        piece = (rows[1], columns[1])
+        axes = "zyx" if index < 5 else "xzy"
+
+        def rest(dropped):
+            return tuple(dims[axis] for axis in axes if axis not in dropped)
+
+        one, two = order
+        scratch += [
+            pltpu.VMEM(rest("") + piece, LOW),
+            pltpu.VMEM((dims[one] - 1,) + rest(one) + piece, LOW),
+            pltpu.VMEM((dims[two] - 1,) + rest("xy") + piece, LOW),
+            pltpu.VMEM((Z - 1,) + piece, LOW),
+        ]
+    whole = pl.BlockSpec(memory_space=pltpu.VMEM)
+    return pl.pallas_call(
+        functools.partial(step_kernel, dims, pieces),
+        out_shape=outs,
+        in_specs=[whole] * 28,
+        out_specs=[whole] * 24,
+        scratch_shapes=scratch,
+        compiler_params=pltpu.CompilerParams(
+            collective_id=1, has_side_effects=True, vmem_limit_bytes=60 << 20
+        ),
+    )(*grads, g_cls, g_vec, *params, *moments)
+
+def fast_body(dims, patches, heights, widths, labels, res_weights, *params_moments):
+    params, moments = params_moments[:7], params_moments[7:]
+    mats, vectors, w_cls = params[:5], params[5], params[6]
+    across, groups = dims["x"], dims["x"] * CORES
+    count = dims["z"] * dims["y"] * groups
+    *full, g_cls, g_vec = gather_weights(dims, mats, vectors, res_weights, w_cls)
+    weights_low = tuple(g.reshape(-1, g.shape[-1]) for g in full)
+    small = g_vec.reshape(count, 8, 128)
+    vec_count = vectors.shape[1]
+    vector_low = small[:, :6, :vec_count].transpose(1, 0, 2).reshape(6, -1).astype(LOW)
+    weight_sum = jnp.sum(small[:, 6])
+    classes, padded = w_cls.shape[1], g_cls.shape[-1]
+    class_low = g_cls.reshape(groups, -1, padded).transpose(1, 0, 2).reshape(-1, groups * padded)
+    slots = heights.shape[1]
+    own_start = lax.axis_index("mp") * slots
+    own_labels = lax.dynamic_slice_in_dim(labels, own_start, slots, 1).reshape(-1)
+    own_weights = lax.dynamic_slice_in_dim(res_weights, own_start, slots, 1)
+    own_weights = own_weights.astype(FULL).reshape(-1)
+    columns = jnp.arange(groups * padded, dtype=jnp.int32)
+    place_in = columns % padded
+    class_ids = jnp.where(place_in < classes, columns // padded * classes + place_in, -1)
+    pooled, saved = jax.vmap(layer_forward, in_axes=(None, None, 0, 0, 0))(
+        weights_low, vector_low, patches, heights, widths
+    )
+    pooled = pooled.reshape(-1, pooled.shape[-1])
+    logits = jnp.dot(pooled, class_low, preferred_element_type=FULL)
+    logits = jnp.where(class_ids[None] >= 0, logits, excluded)
+    hit = own_labels[:, None] == class_ids[None, :]
+    top = jnp.max(logits, axis=1)
+    log_total = top + jnp.log(jnp.sum(jnp.exp(logits - top[:, None]), axis=1))
+    losses = log_total - jnp.sum(jnp.where(hit, logits, 0.0), axis=1)
+    loss_local = jnp.sum(own_weights * losses)
+    logit_grad = (
+        (jnp.exp(logits - log_total[:, None]) - hit.astype(FULL)) * (own_weights / weight_sum)[:, None]
+    ).astype(LOW)
+    class_grad = outer_dot(pooled, logit_grad).astype(LOW)
+    class_grad = class_grad.reshape(-1, groups, padded).transpose(1, 0, 2).reshape(g_cls.shape)
+    pooled_grad = inner_dot(logit_grad, class_low).reshape(heights.shape[0], slots, -1)
+    pairs, vector_grad = jax.vmap(layer_backward, in_axes=(None, None, 0, 0))(
+        weights_low, vector_low, saved, pooled_grad
+    )
+    grads = []
+    for (left, right), like in zip(pairs, full):
+        left = left.reshape(-1, left.shape[-1])
+        right = right.reshape(-1, right.shape[-1])
+        grads.append(outer_dot(left, right).astype(LOW).reshape(like.shape))
+    vector_grad = jnp.sum(vector_grad, axis=0)
+    rest = jnp.zeros((2, vector_grad.shape[1]), FULL)
+    rest = rest.at[0, 0].set(loss_local).at[0, 1].set(weight_sum / count)
+    g_small = jnp.concatenate([vector_grad, rest], axis=0)
+    loss_terms, clip_norm, *updated = take_step(dims, grads, class_grad, g_small, params, moments)
+    return (loss_terms.reshape(2), clip_norm.reshape(()), *updated)
+
+
+def chip_dims(mesh):
+    across, along = mesh.shape["mp"] // CORES, mesh.shape["dp"]
+    return {"x": across, "y": across, "z": along // across}
+
+
+def fits(mesh, width):
+    devices = mesh.shape["dp"] * mesh.shape["mp"]
+    dims = chip_dims(mesh)
+    same = dims["x"] * dims["y"] * dims["z"] * CORES == devices
+    return same and width % (8 * devices) == 0 and width // devices * CORES % 16 == 0
+
+
 def solution(mesh):
     placed = (
         P(None, ("dp", "mp"), None),
@@ -483,8 +1057,11 @@
         P("dp", "mp"),
         P("dp", "mp"),
     )
+    run = body
+    if fits(mesh, 768):
+        run = functools.partial(fast_body, chip_dims(mesh))
     return jax.shard_map(
-        body,
+        run,
         mesh=mesh,
         in_specs=placed,
         out_specs=(

time: 1480 us -> 548 us (0.37)
  waiting for transfers between devices: 594 us -> 0 us
  blocking collectives: 272 us -> 0 us
  Pallas kernels: 0 us -> 232 us
  other arithmetic: 163 us -> 62.4 us
  matrix products: 243 us -> 149 us
  local copies, waits for them, and re-layouts: 165 us -> 89.8 us
  between operations: 29.2 us -> 5.08 us
    reduce_scatter x10 -> x0, waiting for transfers between devices: 528 us -> none  [the longest x1 140 us: reduce_grads(): lax.psum_scatter(fresh[4], ('dp', 'mp'), scatter_dimension=0, tiled=True)]
    pallas_call x0 -> x2, Pallas kernels: none -> 232 us  [the longest x1 129 us: take_step(): pl.pallas_call(functools.partial(step_kernel, dims, pieces), out_shape=ou...]
    psum x3 -> x0, blocking collectives: 122 us -> none  [the longest x2 80.1 us: body(): square_sums, loss_total = lax.psum((grad_squares, loss_local), ('dp', 'mp'))]
    all_gather x6 -> x0, blocking collectives: 97.9 us -> none  [the longest x1 40.8 us: body(): lax.all_gather(vectors.astype(jnp.bfloat16), ('dp', 'mp'), axis=1, tiled=...]
    all_gather x5 -> x0, waiting for transfers between devices: 66.2 us -> none  [the longest x1 60.1 us: body(): lax.all_gather(w_down.astype(jnp.bfloat16), ('dp', 'mp'), axis=0, tiled=T...]
    unnamed x2 -> x0, blocking collectives: 51.5 us -> none
    dot_general x28 -> x6, matrix products: 82.5 us -> 35.2 us  [outer_dot(): lax.dot_general(left, right, (((0,), (0,)), ((), ())), preferred_element_...]
    unnamed x918 -> x271, local copies, waits for them, and re-layouts: 62.1 us -> 39.2 us
  transfers between devices with their start and end apart: 15 -> 0, of which waited for: 9 -> 0; matrix products, arithmetic and copies ran while one was open for 24% -> 0% of each run, Pallas kernels for 0% -> 0%
where the time goes in v1:
time: 548 us; the launch traced here: 538 us
  Pallas kernels  232 us (42%)
  matrix products  149 us (27%)
  local copies, waits for them, and re-layouts  89.8 us (16%)
  other arithmetic  62.4 us (11%)
    pallas_call x1, Pallas kernels, take_step(): pl.pallas_call(functools.partial(step_kernel, dims, pieces), out_shape=ou...  129 us
    pallas_call x1, Pallas kernels, gather_weights(): pl.pallas_call(functools.partial(gather_kernel, dims, pieces), out_shape=...  102 us
    dot_general x5, matrix products, inner_dot(): lax.dot_general(left, right, (((1,), (1,)), ((), ())), preferred_element_...  40.4 us
    unnamed x271, local copies, waits for them, and re-layouts  39.2 us
    dot_general x6, matrix products, outer_dot(): lax.dot_general(left, right, (((0,), (0,)), ((), ())), preferred_element_...  35.2 us
    dot_general x1, matrix products, layer_forward(): jnp.dot(active, down_w, preferred_element_type=jnp.float32)  12.1 us

profile of v1, /device:TPU:0, one launch (start us, length us, event | category | flops | bytes accessed | tf_op | source)
XLA Modules:
  0.0 537.5 jit_solution(12920482073629203406)
XLA Ops:
  7.8 1.6 copy.158
  9.4 102.2 %shard_map.433 = (bf16[4,2,2,64,768]{4,3,2,1,0:T(8,128)(2,1)}, bf16[4,2,2,48,2304]{4,3,2,1,0:T(8,128)(2,1)}, bf16[4,2,2,48,768]{4,3,2,1,0:T(8,128)(2,1)}, bf16[4...) custom-call(f32[32,768]{1,0:T(8,128)} %refs_7_.3, ...), custom_call_target="tpu_custom_call" | custom-call | tf_op jit(solution)/shard_map/pallas_call | solution.py:778
  111.6 1.7 slice_reduce_fusion
  118.5 1.8 slice.101
  120.2 2.4 slice.99
  122.6 1.6 copy.173
  125.5 2.4 reshape.569
  127.9 2.8 fusion.114
  131.7 2.0 copy-done.111
  133.7 4.1 fusion.96
  139.1 3.2 fusion.105
  142.2 2.4 copy.166
  144.6 3.6 copy.164
  150.0 2.4 copy.165
  155.6 3.9 fusion.15
  159.6 4.1 fusion.9
  164.4 3.7 fusion.28
  169.4 1.5 copy.223
  170.9 1.7 fusion.109
  173.2 8.5 %fusion.97 = f32[4,256,3072]{2,1,0:T(8,128)} fusion(bf16[768,3072,1]{1,0,2:T(8,128)(2,1)S(1)} %bitcast.217, f32[4,256,768]{1,2,0:T(8,128)S(1)} %get-tuple-element.250, f32[768]{0:T(1024)S(1)} %mul.533, f32[4,256]{1,0:T(4,128)S(1)} %fusion.82, f32[4,256]{1,0:T(4,128)S(1)} %broadcast_multiply_fusion.6), kind=kOutput, calls=%fused_computation.224 | convolution fusion | flops 4834983936 | bytes 20458496 | tf_op jit(solution)/shard_map/vmap()/dot_general | solution.py:146
  181.8 12.1 %fusion.110 = (f32[4,256]{1,0:T(4,128)S(1)}, f32[4,256,768]{1,2,0:T(8,128)S(1)}) fusion(f32[4,256,768]{1,2,0:T(8,128)S(1)} %get-tuple-element.250, bf16[3072,768,1]{1,0,2:T(8,128)(2,1)S(1)} %bitcast.239, f32[4,256,3072]{2,1,0:T(8,128)} %fusion.97), kind=kOutput, calls=%fused_computation.233 | convolution fusion | flops 4861721600 | bytes 23597056 | tf_op jit(solution)/shard_map/vmap()/dot_general | solution.py:148
  198.9 3.6 fusion.40
  202.4 1.7 copy.172
  205.3 2.1 fusion.112
  212.0 3.0 fusion.115
  216.3 2.4 scatter.9
  218.7 2.3 fusion.39
  221.0 5.7 %fusion.113 = f32[4,256,12]{1,2,0:T(8,128)S(1)} fusion(f32[4,16,256,12]{2,1,3,0:T(8,128)S(1)} %fusion.39, f32[4,16,256]{2,1,0:T(8,128)} %get-tuple-element.240, f32[4,16,256,12]{2,1,3,0:T(8,128)} %get-tuple-element.254, f32[4,16,12]{1,2,0:T(8,128)} %copy-done.92), kind=kOutput, calls=%fused_computation.236 | output fusion | flops 1561599 | bytes 1690624 | tf_op jit(solution)/shard_map/vmap()/sub | solution.py:217
  230.8 1.6 convolution_convert_fusion
  233.7 2.0 bitcast_add_fusion
  237.2 2.4 fusion.104
  239.7 19.5 %fusion.8 = bf16[4,256,3072]{2,1,0:T(8,128)(2,1)} fusion(f32[4,256,3072]{2,1,0:T(8,128)} %fusion.97, bf16[3072,768,1]{1,0,2:T(8,128)(2,1)} %bitcast.236, f32[4,256,768]{1,2,0:T(8,128)} %get-tuple-element.226, f32[4,256]{1,0:T(4,128)S(1)} %negate_multiply_fusion.4), kind=kOutput, calls=%fused_computation.10 | convolution fusion | flops 4896325632 | bytes 26742784 | tf_op jit(solution)/shard_map/vmap()/dot_general | solution.py:55
  259.2 12.2 %bitcast_convert_fusion = bf16[3072,768]{1,0:T(8,128)(2,1)} fusion(f32[4,256,768]{1,2,0:T(8,128)} %get-tuple-element.226, f32[4,256]{1,0:T(4,128)S(1)} %negate_multiply_fusion.4, f32[4,256,3072]{2,1,0:T(8,128)S(1)} %bitcast.199), kind=kOutput, calls=%fused_computation.20 | convolution fusion | flops 4864081920 | bytes 20451328 | tf_op jit(solution)/shard_map/dot_general | solution.py:49
  271.3 8.3 %multiply_reduce_fusion.1 = (f32[4,768]{1,0:T(4,128)}, f32[4,256]{1,0:T(4,128)S(1)}, f32[4,256,768]{1,2,0:T(8,128)S(1)}) fusion(f32[4,256,768]{1,2,0:T(8,128)S(1)} %get-tuple-element.250, f32[4,256]{1,0:T(4,128)S(1)} %fusion.82, f32[4,256]{1,0:T(4,128)S(1)} %broadcast_multiply_fusion.6, f32[768]{0:T(1024)S(1)} %mul.533, ...), kind=kOutput, calls=%fused_computation.50 | convolution fusion | flops 4837339136 | bytes 17329152 | tf_op jit(solution)/shard_map/vmap()/dot_general | solution.py:55
  279.7 7.1 %bitcast_convert_fusion.1 = bf16[768,3072]{1,0:T(8,128)(2,1)} fusion(bf16[4,256,3072]{2,1,0:T(8,128)(2,1)S(1)} %copy-done.112, f32[4,256,768]{1,2,0:T(8,128)S(1)} %get-tuple-element.250, f32[768]{0:T(1024)S(1)} %mul.533, f32[4,256]{1,0:T(4,128)S(1)} %fusion.82, f32[4,256]{1,0:T(4,128)S(1)} %broadcast_multiply_fusion.6), kind=kOutput, calls=%fused_computation.21 | convolution fusion | flops 4837343232 | bytes 14167040 | tf_op jit(solution)/shard_map/dot_general | solution.py:49
  290.1 2.6 convolution_convert_fusion.1
  292.6 1.6 copy.188
  294.2 3.9 convolution_convert_fusion.2
  299.0 8.6 %fusion.29 = bf16[4,12,64,256]{3,2,1,0:T(8,128)(2,1)} fusion(bf16[4,256,12,64]{1,3,2,0:T(8,128)(2,1)S(1)} %bitcast.206, f32[4,12,256]{2,1,0:T(8,128)S(1)} %copy-done.49, f32[4,12,256,256]{2,3,1,0:T(8,128)} %copy-done.7, pred[4,256,256]{1,2,0:T(8,128)(4,1)S(1)} %broadcast_compare_fusion), kind=kOutput, calls=%fused_computation.79 | convolution fusion | flops 416022528 | bytes 16039936 | tf_op jit(solution)/shard_map/vmap(hts,thd->shd)/dot_general | solution.py:102
  307.6 2.7 copy.184
  310.3 9.4 %multiply_reduce_fusion = (f32[4,12,256]{2,1,0:T(8,128)S(1)}, f32[4,12,256,256]{2,3,1,0:T(8,128)}) fusion(f32[4,12,256]{2,1,0:T(8,128)S(1)} %copy-done.49, f32[4,12,256,256]{2,3,1,0:T(8,128)} %copy-done.7, pred[4,256,256]{1,2,0:T(8,128)(4,1)S(1)} %broadcast_compare_fusion, bf16[4,256,12,64]{1,3,2,0:T(8,128)(2,1)S(1)} %bitcast.207, ...), kind=kOutput, calls=%fused_computation.12 | convolution fusion | flops 418369536 | bytes 28672000 | tf_op jit(solution)/shard_map/vmap(thd,shd->hts)/dot_general | solution.py:108
  319.7 10.9 %multiply_convert_fusion = bf16[4,12,256,256]{2,3,1,0:T(8,128)(2,1)S(1)} fusion(f32[4,12,256,256]{2,3,1,0:T(8,128)} %get-tuple-element.259, f32[4,12,256]{2,1,0:T(8,128)S(1)} %get-tuple-element.258, f32[4,12,256]{2,1,0:T(8,128)S(1)} %copy-done.50, f32[4,12,256,256]{2,3,1,0:T(8,128)} %copy-done.7, pred[4,256,256]{1,2,0:T(8,128)(4,1)S(1)} %broadcast_compare_fusion), kind=kLoop, calls=%fused_computation.11 | loop fusion | flops 18874368 | bytes 31817728 | tf_op jit(solution)/shard_map/vmap()/convert_element_type | solution.py:113
  330.8 2.4 fusion.18
  333.3 3.5 fusion.19
  336.9 1.9 fusion.16
  340.4 5.3 add_convert_fusion.1
  345.7 2.6 copy.183
  348.3 3.3 fusion.17
  351.7 4.2 add_convert_fusion.2
  355.9 2.7 copy.182
  358.7 7.0 %multiply_reduce_fusion.3 = (f32[4,256]{1,0:T(4,128)S(1)}, f32[4,256,768]{1,2,0:T(8,128)S(1)}) fusion(f32[4,256,768]{1,2,0:T(8,128)S(1)} %copy-done.10, f32[768]{0:T(1024)S(1)} %copy-done.98, f32[4,256]{1,0:T(4,128)S(1)} %copy-done.84, bf16[768,2304,1]{1,0,2:T(8,128)(2,1)} %bitcast.240, bf16[4,256,768]{2,1,0:T(8,128)(2,1)} %copy.184, ...), kind=kOutput, calls=%fused_computation.53 | convolution fusion | flops 3641179136 | bytes 14560256 | tf_op jit(solution)/shard_map/vmap()/dot_general | solution.py:55
  365.8 7.0 %bitcast_convert_fusion.2 = bf16[768,2304]{1,0:T(8,128)(2,1)} fusion(bf16[4,256,768]{2,1,0:T(8,128)(2,1)S(1)} %copy-done.38, bf16[4,256,768]{2,1,0:T(8,128)(2,1)S(1)} %copy-done.39, bf16[4,256,768]{2,1,0:T(8,128)(2,1)S(1)} %copy-done.40, f32[4,256,768]{1,2,0:T(8,128)S(1)} %copy-done.10, f32[768]{0:T(1024)S(1)} %copy-done.98, f32[4,256]{1,0:T(4,128)S(1)} %copy-done.100, ...), kind=kOutput, calls=%fused_computation.22 | convolution fusion | flops 3642949632 | bytes 11414528 | tf_op jit(solution)/shard_map/dot_general | solution.py:49
  375.7 3.5 bitcast_convert_fusion.3
  379.9 129.5 %shard_map.434 = (f32[1,2]{1,0:T(1,128)}, f32[1,1]{1,0:T(1,128)}, f32[12,2]{1,0:T(8,128)}, f32[32,768]{1,0:T(8,128)}, f32[32,768]{1,0:T(8,128)}, /*index=5*/f32[...) custom-call(bf16[4,2,2,64,768]{4,3,2,1,0:T(8,128)(2,1)} %bitcast.221, ...), custom_call_target="tpu_custom_call" | custom-call | tf_op jit(solution)/shard_map/pallas_call | solution.py:954
  512.8 1.6 copy.274
  514.4 1.5 copy.275
  515.9 1.5 copy.276
  517.5 1.6 copy.277
  519.1 1.6 copy.278
  520.7 1.6 copy.279
  522.4 1.5 copy.280
  523.9 1.5 copy.281
  525.4 1.5 copy.282
  526.9 1.7 copy.283
  (349 shorter events, 60.4 us)
Async XLA Ops:
  0.7 7.1 %copy-start.34 = (bf16[4,256,768]{2,1,0:T(8,128)(2,1)S(1)}, bf16[4,256,768]{2,1,0:T(8,128)(2,1)}, u32[]{:S(2)}) copy-start(bf16[4,256,768]{2,1,0:T(8,128)(2,1)} %param.30) | copy-start | bytes 4718596
  6.4 105.2 %copy-start.43 = (pred[4,256,128]{2,1,0:T(32,128)(4,1)}, pred[4,256,128]{2,1,0:T(32,128)(4,1)S(1)}, u32[]{:S(2)}) copy-start(pred[4,256,128]{2,1,0:T(32,128)(4,1)S(1)} %get-tuple-element.267) | copy-start | bytes 393220
  111.6 11.0 %copy-start.22 = (bf16[2,2,4,2,96,256]{5,4,3,2,1,0:T(8,128)(2,1)S(1)}, bf16[2,2,4,2,96,256]{5,4,3,2,1,0:T(8,128)(2,1)}, u32[]{:S(2)}) copy-start(bf16[2,2,4,2,96,256]{5,4,3,2,1,0:T(8,128)(2,1)} %get-tuple-element.85) | copy-start | bytes 4718596
  116.3 15.4 %copy-start.97 = (f32[768]{0:T(1024)}, f32[768]{0:T(1024)S(1)}, u32[]{:S(2)}) copy-start(f32[768]{0:T(1024)S(1)} %mul.514) | copy-start | bytes 9220
  117.2 38.2 %copy-start.66 = (f32[12,64]{1,0:T(8,128)}, f32[12,64]{1,0:T(8,128)S(1)}, u32[]{:S(2)}) copy-start(f32[12,64]{1,0:T(8,128)S(1)} %mul.526) | copy-start | bytes 9220
  117.8 6.4 %copy-start.69 = (f32[12,64]{1,0:T(8,128)}, f32[12,64]{1,0:T(8,128)S(1)}, u32[]{:S(2)}) copy-start(f32[12,64]{1,0:T(8,128)S(1)} %mul.520) | copy-start | bytes 9220
  131.3 6.4 %copy-start.8 = (f32[4,256,768]{1,2,0:T(8,128)}, f32[4,256,768]{1,2,0:T(8,128)S(1)}, u32[]{:S(2)}) copy-start(f32[4,256,768]{1,2,0:T(8,128)S(1)} %get-tuple-element.246) | copy-start | bytes 9437188
  131.3 6.4 %copy-start.83 = (f32[4,256]{1,0:T(4,128)}, f32[4,256]{1,0:T(4,128)S(1)}, u32[]{:S(2)}) copy-start(f32[4,256]{1,0:T(4,128)S(1)} %broadcast_multiply_fusion.7) | copy-start | bytes 12292
  131.7 6.1 %copy-start.86 = (f32[4,256]{1,0:T(4,128)}, f32[4,256]{1,0:T(4,128)S(1)}, u32[]{:S(2)}) copy-start(f32[4,256]{1,0:T(4,128)S(1)} %multiply_reduce_fusion.10) | copy-start | bytes 12292
  133.7 4.1 copy-start.99
  144.6 4.0 copy-start.4
  148.6 6.7 %copy-start.25 = (f32[4,256,12]{1,2,0:T(8,128)}, f32[4,256,12]{1,2,0:T(8,128)S(1)}, u32[]{:S(2)}) copy-start(f32[4,256,12]{1,2,0:T(8,128)S(1)} %broadcast_multiply_fusion.1) | copy-start | bytes 147460
  149.9 5.5 %copy-start.29 = (f32[4,256,12]{1,2,0:T(8,128)}, f32[4,256,12]{1,2,0:T(8,128)S(1)}, u32[]{:S(2)}) copy-start(f32[4,256,12]{1,2,0:T(8,128)S(1)} %fusion.61) | copy-start | bytes 147460
  154.7 4.9 copy-start.23
  155.3 4.2 copy-start.56
  155.6 4.0 copy-start.31
  159.6 4.8 copy-start.7
  159.6 4.2 copy-start.51
  159.6 4.8 copy-start.20
  172.6 9.2 %slice-start.5 = ((s8[4718592]{0:T(1024)(128)(4,1)}), s8[4194304]{0:T(1024)(128)(4,1)S(1)}, s32[]{:S(2)}) async-start(s8[4718592]{0:T(1024)(128)(4,1)} %bitcast.237), calls=%async_computation.5 | async-start | bytes 8388608
  172.9 8.8 %copy-start.88 = (f32[4,256]{1,0:T(4,128)}, f32[4,256]{1,0:T(4,128)S(1)}, u32[]{:S(2)}) copy-start(f32[4,256]{1,0:T(4,128)S(1)} %multiply_reduce_fusion.7) | copy-start | bytes 12292
  173.2 8.5 %slice-start.6 = ((s8[4718592]{0:T(1024)(128)(4,1)}), s8[524288]{0:T(1024)(128)(4,1)S(1)}, s32[]{:S(2)}) async-start(s8[4718592]{0:T(1024)(128)(4,1)} %bitcast.237), calls=%async_computation.6 | async-start | bytes 1048576
  194.6 4.2 copy-start.52
  198.8 6.4 %copy-start.110 = (pred[1024]{0:T(1024)(128)(4,1)S(1)}, pred[1024]{0:T(1024)(128)(4,1)}, u32[]{:S(2)}) copy-start(pred[1024]{0:T(1024)(128)(4,1)} %broadcast_compare_fusion.1) | copy-start | bytes 3076
  198.8 9.3 %copy-start.85 = (s32[1024]{0:T(1024)S(1)}, s32[1024]{0:T(1024)}, u32[]{:S(2)}) copy-start(s32[1024]{0:T(1024)} %fusion.75) | copy-start | bytes 12292
  198.8 9.3 %copy-start.106 = (s32[64]{0:T(128)S(1)}, s32[64]{0:T(128)}, u32[]{:S(2)}) copy-start(s32[64]{0:T(128)} %eq.118) | copy-start | bytes 772
  198.9 10.1 %copy-start.105 = (s32[4,64]{1,0:T(4,128)S(1)}, s32[4,64]{1,0:T(4,128)}, u32[]{:S(2)}) copy-start(s32[4,64]{1,0:T(4,128)} %refs_6_.1) | copy-start | bytes 3076
  205.2 5.0 copy-start.47
  221.0 6.4 %copy-start.15 = (bf16[4,256,768]{1,2,0:T(8,128)(2,1)S(1)}, bf16[4,256,768]{1,2,0:T(8,128)(2,1)}, u32[]{:S(2)}) copy-start(bf16[4,256,768]{1,2,0:T(8,128)(2,1)} %copy-done.14) | copy-start | bytes 4718596
  237.2 21.9 %slice-start = ((s8[12582912]{0:T(1024)(128)(4,1)}), s8[4194304]{0:T(1024)(128)(4,1)S(1)}, s32[]{:S(2)}) async-start(s8[12582912]{0:T(1024)(128)(4,1)} %bitcast.198), calls=%async_computation | async-start | bytes 8388608
  239.7 19.5 %slice-start.1 = ((s8[12582912]{0:T(1024)(128)(4,1)}), s8[4194304]{0:T(1024)(128)(4,1)S(1)}, s32[]{:S(2)}) async-start(s8[12582912]{0:T(1024)(128)(4,1)} %bitcast.198), calls=%async_computation.1 | async-start | bytes 8388608
  239.7 19.5 %slice-start.2 = ((s8[12582912]{0:T(1024)(128)(4,1)}), s8[4194304]{0:T(1024)(128)(4,1)S(1)}, s32[]{:S(2)}) async-start(s8[12582912]{0:T(1024)(128)(4,1)} %bitcast.198), calls=%async_computation.2 | async-start | bytes 8388608
  259.2 12.2 %copy-start.112 = (bf16[4,256,3072]{2,1,0:T(8,128)(2,1)S(1)}, bf16[4,256,3072]{2,1,0:T(8,128)(2,1)}, u32[]{:S(2)}) copy-start(bf16[4,256,3072]{2,1,0:T(8,128)(2,1)} %fusion.8) | copy-start | bytes 18874372
  279.6 7.1 %copy-start.89 = (f32[4,256]{1,0:T(4,128)S(1)}, f32[4,256]{1,0:T(4,128)}, u32[]{:S(2)}) copy-start(f32[4,256]{1,0:T(4,128)} %copy-done.88) | copy-start | bytes 12292
  294.2 3.9 copy-start.41
  310.3 9.4 %copy-start.50 = (f32[4,12,256]{2,1,0:T(8,128)S(1)}, f32[4,12,256]{2,1,0:T(8,128)}, u32[]{:S(2)}) copy-start(f32[4,12,256]{2,1,0:T(8,128)} %log_add_fusion) | copy-start | bytes 147460
  319.7 11.0 %copy-start.3 = (f32[4,256,768]{1,2,0:T(8,128)S(1)}, f32[4,256,768]{1,2,0:T(8,128)}, u32[]{:S(2)}) copy-start(f32[4,256,768]{1,2,0:T(8,128)} %copy-done.2) | copy-start | bytes 9437188
  319.7 11.0 %copy-start.6 = (f32[4,256,768]{1,2,0:T(8,128)S(1)}, f32[4,256,768]{1,2,0:T(8,128)}, u32[]{:S(2)}) copy-start(f32[4,256,768]{1,2,0:T(8,128)} %copy-done.4) | copy-start | bytes 9437188
  319.7 11.0 %copy-start.24 = (f32[4,256,12]{1,2,0:T(8,128)S(1)}, f32[4,256,12]{1,2,0:T(8,128)}, u32[]{:S(2)}) copy-start(f32[4,256,12]{1,2,0:T(8,128)} %copy-done.23) | copy-start | bytes 147460
  319.7 11.0 %copy-start.26 = (f32[4,256,12]{1,2,0:T(8,128)S(1)}, f32[4,256,12]{1,2,0:T(8,128)}, u32[]{:S(2)}) copy-start(f32[4,256,12]{1,2,0:T(8,128)} %copy-done.25) | copy-start | bytes 147460
  319.7 11.0 %copy-start.32 = (f32[4,256,12]{1,2,0:T(8,128)S(1)}, f32[4,256,12]{1,2,0:T(8,128)}, u32[]{:S(2)}) copy-start(f32[4,256,12]{1,2,0:T(8,128)} %copy-done.31) | copy-start | bytes 147460
  319.7 11.0 %copy-start.68 = (f32[12,64]{1,0:T(8,128)S(1)}, f32[12,64]{1,0:T(8,128)}, u32[]{:S(2)}) copy-start(f32[12,64]{1,0:T(8,128)} %broadcast_multiply_fusion.3) | copy-start | bytes 9220
  319.7 11.0 %copy-start.71 = (f32[12,64]{1,0:T(8,128)S(1)}, f32[12,64]{1,0:T(8,128)}, u32[]{:S(2)}) copy-start(f32[12,64]{1,0:T(8,128)} %copy-done.69) | copy-start | bytes 9220
  351.7 7.0 %copy-start.84 = (f32[4,256]{1,0:T(4,128)S(1)}, f32[4,256]{1,0:T(4,128)}, u32[]{:S(2)}) copy-start(f32[4,256]{1,0:T(4,128)} %copy-done.83) | copy-start | bytes 12292
  351.7 7.0 %copy-start.98 = (f32[768]{0:T(1024)S(1)}, f32[768]{0:T(1024)}, u32[]{:S(2)}) copy-start(f32[768]{0:T(1024)} %copy-done.97) | copy-start | bytes 9220
  358.7 7.1 %copy-start.38 = (bf16[4,256,768]{2,1,0:T(8,128)(2,1)S(1)}, bf16[4,256,768]{2,1,0:T(8,128)(2,1)}, u32[]{:S(2)}) copy-start(bf16[4,256,768]{2,1,0:T(8,128)(2,1)} %copy.184) | copy-start | bytes 4718596
  358.7 7.1 %copy-start.39 = (bf16[4,256,768]{2,1,0:T(8,128)(2,1)S(1)}, bf16[4,256,768]{2,1,0:T(8,128)(2,1)}, u32[]{:S(2)}) copy-start(bf16[4,256,768]{2,1,0:T(8,128)(2,1)} %copy.183) | copy-start | bytes 4718596
  358.7 7.1 %copy-start.40 = (bf16[4,256,768]{2,1,0:T(8,128)(2,1)S(1)}, bf16[4,256,768]{2,1,0:T(8,128)(2,1)}, u32[]{:S(2)}) copy-start(bf16[4,256,768]{2,1,0:T(8,128)(2,1)} %copy.182) | copy-start | bytes 4718596
  358.7 7.1 %copy-start.100 = (f32[4,256]{1,0:T(4,128)S(1)}, f32[4,256]{1,0:T(4,128)}, u32[]{:S(2)}) copy-start(f32[4,256]{1,0:T(4,128)} %copy-done.99) | copy-start | bytes 12292
  365.8 7.0 %copy-start.87 = (f32[4,256]{1,0:T(4,128)S(1)}, f32[4,256]{1,0:T(4,128)}, u32[]{:S(2)}) copy-start(f32[4,256]{1,0:T(4,128)} %copy-done.86) | copy-start | bytes 12292
  365.8 8.4 %copy-start.36 = (bf16[4,256,768]{1,2,0:T(8,128)(2,1)S(1)}, bf16[4,256,768]{1,2,0:T(8,128)(2,1)}, u32[]{:S(2)}) copy-start(bf16[4,256,768]{1,2,0:T(8,128)(2,1)} %copy.158) | copy-start | bytes 4718596
  365.8 8.4 %copy-start.58 = (bf16[4,256,256]{1,2,0:T(8,128)(2,1)S(1)}, bf16[4,256,256]{1,2,0:T(8,128)(2,1)}, u32[]{:S(2)}) copy-start(bf16[4,256,256]{1,2,0:T(8,128)(2,1)} %copy.159) | copy-start | bytes 1572868
  509.4 19.2 %copy-start.63 = (f32[24,3072]{1,0:T(8,128)S(1)}, f32[24,3072]{1,0:T(8,128)}, u32[]{:S(2)}) copy-start(f32[24,3072]{1,0:T(8,128)} %get-tuple-element.305) | copy-start | bytes 884740
  509.4 19.9 %copy-start.62 = (f32[24,3072]{1,0:T(8,128)S(1)}, f32[24,3072]{1,0:T(8,128)}, u32[]{:S(2)}) copy-start(f32[24,3072]{1,0:T(8,128)} %get-tuple-element.306) | copy-start | bytes 884740
  509.4 20.6 %copy-start.61 = (f32[96,768]{1,0:T(8,128)S(1)}, f32[96,768]{1,0:T(8,128)}, u32[]{:S(2)}) copy-start(f32[96,768]{1,0:T(8,128)} %get-tuple-element.307) | copy-start | bytes 884740
  509.4 21.3 %copy-start.60 = (f32[96,768]{1,0:T(8,128)S(1)}, f32[96,768]{1,0:T(8,128)}, u32[]{:S(2)}) copy-start(f32[96,768]{1,0:T(8,128)} %get-tuple-element.308) | copy-start | bytes 884740
  509.5 22.0 %copy-start.59 = (f32[96,768]{1,0:T(8,128)S(1)}, f32[96,768]{1,0:T(8,128)}, u32[]{:S(2)}) copy-start(f32[96,768]{1,0:T(8,128)} %get-tuple-element.309) | copy-start | bytes 884740
  509.5 22.8 %copy-start.109 = (f32[6,24]{1,0:T(8,128)S(1)}, f32[6,24]{1,0:T(8,128)}, u32[]{:S(2)}) copy-start(f32[6,24]{1,0:T(8,128)} %get-tuple-element.310) | copy-start | bytes 1732
  509.5 23.3 %copy-start.108 = (f32[6,24]{1,0:T(8,128)S(1)}, f32[6,24]{1,0:T(8,128)}, u32[]{:S(2)}) copy-start(f32[6,24]{1,0:T(8,128)} %get-tuple-element.311) | copy-start | bytes 1732
  509.5 23.9 %copy-start.107 = (f32[6,24]{1,0:T(8,128)S(1)}, f32[6,24]{1,0:T(8,128)}, u32[]{:S(2)}) copy-start(f32[6,24]{1,0:T(8,128)} %get-tuple-element.312) | copy-start | bytes 1732
  509.5 24.5 %copy-start.74 = (f32[96,250]{1,0:T(8,128)S(1)}, f32[96,250]{1,0:T(8,128)}, u32[]{:S(2)}) copy-start(f32[96,250]{1,0:T(8,128)} %get-tuple-element.313) | copy-start | bytes 288004
  509.5 25.1 %copy-start.73 = (f32[96,250]{1,0:T(8,128)S(1)}, f32[96,250]{1,0:T(8,128)}, u32[]{:S(2)}) copy-start(f32[96,250]{1,0:T(8,128)} %get-tuple-element.314) | copy-start | bytes 288004
  512.8 22.5 %copy-start.72 = (f32[96,250]{1,0:T(8,128)S(1)}, f32[96,250]{1,0:T(8,128)}, u32[]{:S(2)}) copy-start(f32[96,250]{1,0:T(8,128)} %get-tuple-element.315) | copy-start | bytes 288004
  512.8 23.1 %copy-start.1 = (s32[4,64]{1,0:T(4,128)S(1)}, s32[4,64]{1,0:T(4,128)}, u32[]{:S(2)}) copy-start(s32[4,64]{1,0:T(4,128)} %param.33) | copy-start | bytes 3076
  (56 other events, 136.6 us)

commit v2 on v0

--- a/solution.py
+++ b/solution.py
@@ -1,6 +1,12 @@
+import functools
+import itertools
+import types
+
 import jax
 import jax.numpy as jnp
 from jax import lax
+from jax.experimental import pallas as pl
+from jax.experimental.pallas import tpu as pltpu
 from jax.sharding import PartitionSpec as P
 
 HEAD = 64
@@ -454,6 +460,1124 @@
     return tuple(outputs)
 
 
+MESH_ID = pl.DeviceIdType.MESH
+CORES = 2
+ALL = slice(None)
+LOW = jnp.bfloat16
+FULL = jnp.float32
+NN = (((1,), (0,)), ((), ()))
+NT = (((1,), (1,)), ((), ()))
+TN = (((0,), (0,)), ((), ()))
+COLUMNS = 768
+
+
+class Place:
+    def __init__(self, dims):
+        self.sizes = dict(dims, c=CORES)
+        dp, mp = lax.axis_index("dp"), lax.axis_index("mp")
+        wide = self.sizes["y"]
+        self.at = {"z": dp // wide, "y": dp % wide, "x": mp // CORES, "c": mp % CORES}
+
+    def source(self, axis, step):
+        size = self.sizes[axis]
+        return (self.at[axis] + (size - step) % size) % size
+
+    def peer(self, axis, step):
+        at = dict(self.at)
+        at[axis] = self.source(axis, -step)
+        return (at["z"] * self.sizes["y"] + at["y"], at["x"] * CORES + at["c"])
+
+    def steps(self, axis):
+        return range(1, self.sizes[axis])
+
+    def tell(self, semaphore):
+        count = 0
+        for axis in "cxyz":
+            for step in self.steps(axis):
+                pl.semaphore_signal(
+                    semaphore, inc=1, device_id=self.peer(axis, step), device_id_type=MESH_ID
+                )
+                count += 1
+        return count
+
+
+class Courier:
+    def __init__(self, place, send, recv):
+        self.place, self.send, self.recv, self.open, self.count = place, send, recv, [], 0
+
+    def start(self, axis, step, source, target):
+        slot = self.count
+        self.count += 1
+        copy = pltpu.make_async_remote_copy(
+            src_ref=source,
+            dst_ref=target,
+            send_sem=self.send.at[slot],
+            recv_sem=self.recv.at[slot],
+            device_id=self.place.peer(axis, step),
+            device_id_type=MESH_ID,
+        )
+        copy.start()
+        self.open.append(copy)
+        return copy
+
+    def sent(self, copies):
+        for copy in copies:
+            copy.wait_send()
+            self.open = [other for other in self.open if other is not copy]
+
+    def finish(self):
+        self.sent(list(self.open))
+
+
+class Spread:
+    def __init__(self, courier, view, order):
+        self.courier, self.place, self.view, self.order = courier, courier.place, view, order
+        self.relayed = []
+
+    def part(self, stage, **fixed):
+        where = {axis: self.place.at[axis] for axis in "xyz"}
+        for axis in ("z" + self.order)[:stage]:
+            where[axis] = ALL
+        where.update(fixed)
+        return self.view(**where)
+
+    def send(self, axis, stage):
+        part = self.part(stage)
+        return [self.courier.start(axis, step, part, part) for step in self.place.steps(axis)]
+
+    def relay(self, part):
+        self.relayed.append(self.courier.start("c", 1, part, part))
+
+    def begin(self):
+        self.coming = self.send("z", 0)
+
+    def middle(self, stage):
+        for copy in self.coming:
+            copy.wait_recv()
+        if stage == 1:
+            self.relay(self.part(1))
+        else:
+            axis = self.order[stage - 2]
+            for step in self.place.steps(axis):
+                self.relay(self.part(stage - 1, **{axis: self.place.source(axis, step)}))
+        self.coming = self.send(self.order[stage - 1], stage) if stage < 3 else []
+
+    def done(self):
+        for copy in self.relayed:
+            copy.wait_recv()
+
+
+class Pool:
+    def __init__(self, ref, axes, rows, held, rest, width):
+        self.ref, self.axes, self.rows, self.marks, self.width = ref, axes, rows, (held, rest), width
+
+    def at(self, half, **where):
+        key = tuple(where.get(axis, ALL) for axis in self.axes)
+        return self.ref.at[key + (pl.ds(*self.rows), pl.ds(self.marks[half], self.width))]
+
+
+class Fold:
+    def __init__(self, courier, view, order, pool, finish):
+        self.courier, self.place, self.view, self.order = courier, courier.place, view, order
+        self.pool, self.finish, self.copies, self.stage = pool, finish, [], 0
+
+    def start(self, axis, step, source, target):
+        copy = self.courier.start(axis, step, source, target)
+        self.copies.append(copy)
+        self.coming.append(copy)
+
+    def landing(self, stage, step):
+        first, second = self.order
+        sizes = self.place.sizes
+        if stage == 1:
+            return self.pool.at(1, **{first: step - 1})
+        if stage == 2:
+            return self.pool.at(1, **{first: sizes[first] - 1, second: step - 1})
+        return self.pool.at(1, **{first: sizes[first] - 1, second: sizes[second] - 1, "z": step - 1})
+
+    def send(self, stage):
+        axis = (self.order + "z")[stage - 1]
+        fixed = {a: self.place.at[a] for a in self.order[: stage - 1]}
+        self.coming = []
+        for step in self.place.steps(axis):
+            source = self.pool.at(0, **{axis: self.place.source(axis, -step)}, **fixed)
+            self.start(axis, step, source, self.landing(stage, step))
+
+    def begin(self):
+        self.coming = []
+        self.start("c", 1, self.view(1 - self.place.at["c"]), self.pool.at(0))
+
+    def advance(self):
+        for copy in self.coming:
+            copy.wait_recv()
+        stage, place = self.stage, self.place
+        self.stage += 1
+        if stage == 3:
+            here = self.pool.at(0, **place_of(place, "xyz"))
+            total = here[...].astype(FULL)
+            for step in place.steps("z"):
+                total = total + self.landing(3, step)[...].astype(FULL)
+            self.finish(total)
+            return True
+        here = self.pool.at(0, **place_of(place, self.order[:stage]))
+        if stage == 0:
+            came = [self.view(place.at["c"])]
+        else:
+            came = [self.landing(stage, step) for step in place.steps(self.order[stage - 1])]
+
+        def one(lead, carry):
+            total = here[lead].astype(FULL)
+            for part in came:
+                total = total + part[lead].astype(FULL)
+            here[lead] = total.astype(LOW)
+            return carry
+
+        lax.fori_loop(0, here.shape[0], one, 0)
+        self.send(stage + 1)
+        return False
+
+
+def place_of(place, axes):
+    return {axis: place.at[axis] for axis in axes}
+
+
+class Total:
+    def __init__(self, courier, slots):
+        self.courier, self.place, self.slots = courier, courier.place, dict(zip("cxyz", slots))
+
+    def send(self, axis, block):
+        mine = self.slots[axis].at[self.place.at[axis]]
+        mine[...] = block
+        self.coming = [
+            self.courier.start(axis, step, mine, mine) for step in self.place.steps(axis)
+        ]
+
+    def receive(self, axis):
+        for copy in self.coming:
+            copy.wait_recv()
+        slots = self.slots[axis]
+        total = slots[0]
+        for index in range(1, slots.shape[0]):
+            total = total + slots[index]
+        return total
+
+    def through(self, block):
+        for axis in "cxyz":
+            self.send(axis, block)
+            block = self.receive(axis)
+        return block
+
+
+def total_slots(dims, shape):
+    sizes = dict(dims, c=CORES)
+    return [pltpu.VMEM((sizes[axis],) + shape, FULL) for axis in "cxyz"]
+
+
+def cut(rows, width, parts):
+    if rows % (16 * parts) == 0:
+        size = rows // parts
+        return [((part * size, size), (0, width)) for part in range(parts)]
+    units = width // 128
+    marks = [units * part // parts * 128 for part in range(parts + 1)]
+    return [((0, rows), (low, high - low)) for low, high in zip(marks, marks[1:]) if high > low]
+
+
+def pieces_of(blocks):
+    found = []
+    for index, (rows, width) in enumerate(blocks):
+        parts = max(2, min(4, rows * width // 16384 // 2 * 2))
+        for row_range, column_range in cut(rows, width, parts):
+            found.append((index, row_range, column_range, ("xy", "yx")[len(found) % 2]))
+    return found
+
+
+def dot(left, right, form=NN):
+    return lax.dot_general(left, right, form, preferred_element_type=FULL)
+
+
+def halves(values):
+    high = values.astype(LOW)
+    return high, (values - high.astype(FULL)).astype(LOW)
+
+
+def fine_dot(left, values, form):
+    high, rest = halves(values)
+    return dot(left, high, form) + dot(left, rest, form)
+
+
+def iota(shape, axis):
+    return lax.broadcasted_iota(jnp.int32, shape, axis).astype(FULL)
+
+
+def normal(values, axis):
+    center = values - jnp.mean(values, axis=axis, keepdims=True)
+    scale = lax.rsqrt(jnp.mean(center * center, axis=axis, keepdims=True) + epsilon)
+    return center * scale, scale
+
+
+def normal_back(upstream, shape, scale, axis):
+    mean = jnp.mean(upstream, axis=axis, keepdims=True)
+    along = jnp.mean(upstream * shape, axis=axis, keepdims=True)
+    return scale * (upstream - mean - shape * along)
+
+
+def column_sum(values):
+    return jnp.sum(values, axis=0, keepdims=True)
+
+
+def row_sum(values):
+    return jnp.sum(values, axis=1, keepdims=True)
+
+
+def curve(values):
+    return jnp.tanh(0.7978845608 * (values + 0.044715 * values * values * values))
+
+
+def squares(values):
+    total = jnp.zeros((1, 128), FULL)
+    for low in range(0, values.shape[1], 128):
+        part = values[:, low : low + 128]
+        part = column_sum(part * part)
+        if part.shape[1] < 128:
+            part = jnp.concatenate([part, jnp.zeros((1, 128 - part.shape[1]), FULL)], axis=1)
+        total = total + part
+    return total
+
+
+def wide_rows(values):
+    squared = values * values
+    rest = jnp.zeros((squared.shape[0], 128 - squared.shape[1]), FULL)
+    return jnp.concatenate([squared, rest], axis=1)
+
+
+def moments_step(gradient, moment_one, moment_two):
+    first = beta_first * moment_one + (1.0 - beta_first) * gradient
+    second = beta_second * moment_two + (1.0 - beta_second) * gradient * gradient
+    return first, second
+
+
+def update_of(first, second, weight):
+    return (
+        first
+        / (1.0 - beta_first**STEP)
+        / (jnp.sqrt(second / (1.0 - beta_second**STEP)) + adam_floor)
+        + weight_decay * weight
+    )
+
+
+def loop(count, body):
+    def one(index, carry):
+        body(index)
+        return carry
+
+    lax.fori_loop(0, count, one, 0)
+
+
+def tile(index, size):
+    return pl.ds(pl.multiple_of(index * size, size), size)
+
+
+class Layer:
+    def __init__(self, r, place, dims):
+        self.r, self.place = r, place
+        self.rows, self.width = r.patches.shape
+        self.packs, self.slots = r.heights.shape
+        self.tokens = self.rows // self.packs
+        self.head_count = self.width // HEAD
+        self.hidden_units = r.g_up.shape[-1]
+        self.groups = dims["x"] * CORES
+        self.member_index = place.at["x"] * CORES + place.at["c"]
+        self.w_embed = r.g_embed.reshape(-1, self.width)
+        self.w_qkv = r.g_qkv.reshape(self.width, 3 * self.width)
+        self.w_out = r.g_out.reshape(self.width, self.width)
+        self.w_up = r.g_up.reshape(self.width, self.hidden_units)
+        self.w_down = r.g_down.reshape(self.hidden_units, self.width)
+        self.upward = r.upward.reshape(self.rows, self.hidden_units)
+        self.active = r.active.reshape(self.rows, self.hidden_units)
+
+    def span(self, pack):
+        return pl.ds(pack * self.tokens, self.tokens)
+
+    def gain(self, row):
+        return self.r.vec[row : row + 1]
+
+    def class_block(self, group):
+        block = self.r.g_cls.at[group // CORES, group % CORES]
+        return block.reshape(self.width, block.shape[-1])
+
+    def head_marks(self):
+        return (
+            jnp.floor((iota((16, self.width), 1) + 0.5) / HEAD) == iota((16, self.width), 0)
+        ).astype(FULL)
+
+    def place_rows(self, pack):
+        r, tokens, slots = self.r, self.tokens, self.slots
+        high = r.heights[pack : pack + 1].astype(FULL)
+        wide = r.widths[pack : pack + 1].astype(FULL)
+        lengths = high * wide
+        square = (slots, slots)
+        below, beside = iota(square, 0), iota(square, 1)
+        ends_column = row_sum(jnp.where(beside <= below, lengths, 0.0))
+        length_column = row_sum(jnp.where(beside == below, lengths, 0.0))
+        ends = column_sum(jnp.where(below <= beside, length_column, 0.0))
+        spots = iota((tokens, slots), 0)
+        segment = row_sum((spots >= ends).astype(FULL))
+        member = (iota((tokens, slots), 1) == segment).astype(FULL)
+        within = spots[:, :1] - row_sum(member * (ends - lengths))
+        across = jnp.maximum(row_sum(member * wide), 1.0)
+        upright = jnp.maximum(row_sum(member * high), 1.0)
+        line = jnp.floor((within + 0.5) / across)
+        column = within - line * across
+        table = iota((tokens, POS), 1)
+        span = self.span(pack)
+        r.pos[span, :POS] = (jnp.floor((column * POS + 0.5) / across) == table).astype(LOW)
+        r.pos[span, POS:] = (jnp.floor((line * POS + 0.5) / upright) == table).astype(LOW)
+        r.cols[span, 0:1] = segment
+        r.segment[pack : pack + 1] = column_sum((iota((slots, tokens), 1) >= ends_column).astype(FULL))
+
+    def read_vectors(self):
+        r = self.r
+        blocks = r.g_vec[...].reshape(-1, 8, 128)
+        count = blocks.shape[0]
+        share = self.width // count
+        wide = iota((128, self.width), 1)
+        owner = jnp.floor((wide[:1] + 0.5) / share)
+        spread = (wide - owner * share == iota((128, self.width), 0)).astype(LOW)
+        everywhere = dot(blocks.reshape(count * 8, 128).astype(LOW), spread).reshape(count, 8, self.width)
+        mine = lax.broadcasted_iota(jnp.int32, (count, 1, self.width), 0).astype(FULL) == owner[None]
+        r.vec[...] = jnp.sum(jnp.where(mine, everywhere, 0.0), axis=0)
+        r.gains[...] = r.vec[...].T
+        total = jnp.sum(blocks, axis=0)[6:7]
+        r.weight_sum[...] = jnp.broadcast_to(row_sum(total), (1, 128))
+        r.vgrad[...] = jnp.zeros(r.vgrad.shape, FULL)
+        r.gacc[...] = jnp.zeros(r.gacc.shape, FULL)
+
+    def embed(self, pack):
+        r, span = self.r, self.span(pack)
+        embedded = dot(r.patches[span], self.w_embed[: self.width])
+        embedded = embedded + dot(r.pos[span], self.w_embed[self.width :])
+        shape, scale = normal(embedded, -1)
+        r.stream[span] = embedded
+        r.shape_first[span] = shape.astype(LOW)
+        r.cols[span, 1:2] = scale
+        r.normed[span] = (shape * self.gain(0)).astype(LOW)
+
+    def project(self, pack):
+        r, span, width = self.r, self.span(pack), self.width
+        for part in range(3):
+            joined = dot(r.normed[span], self.w_qkv[:, part * width : (part + 1) * width])
+            if part == 2:
+                r.joined[2 * width :, span] = joined.T.astype(LOW)
+                continue
+            r.turned[...] = joined.T
+
+            def one_head(head, part=part):
+                own = tile(head, HEAD)
+                at = pl.ds(pl.multiple_of(part * width + head * HEAD, HEAD), HEAD)
+                shape, scale = normal(r.turned[own], 0)
+                r.shape_heads[at, span] = shape.astype(LOW)
+                r.scale_heads[pl.ds(part * self.head_count + head, 1), span] = scale
+                r.joined[at, span] = (shape * r.gains[own, 3 + part : 4 + part]).astype(LOW)
+
+            loop(self.head_count, one_head)
+
+    def mask(self, pack):
+        r = self.r
+        same = r.cols[self.span(pack), 0:1] == r.segment[pack : pack + 1]
+        r.mask[...] = jnp.where(same, 0.0, excluded)
+
+    def head_parts(self, head, span):
+        starts = (part * self.width + head * HEAD for part in range(3))
+        return [pl.ds(pl.multiple_of(start, HEAD), HEAD) for start in starts]
+
+    def attend(self, pack):
+        r, span = self.r, self.span(pack)
+        self.mask(pack)
+
+        def one_head(head):
+            query, key, value = (r.joined[at, span] for at in self.head_parts(head, span))
+            scores = dot(key, query, TN) * HEAD ** (-0.5) + r.mask[...]
+            top = jnp.max(scores, axis=0, keepdims=True)
+            grown = jnp.exp(scores - top)
+            total = column_sum(grown)
+            r.log_total[pl.ds(head, 1), span] = top + jnp.log(total)
+            attention = (grown * (1.0 / total)).astype(LOW)
+            r.mixed[tile(head, HEAD), span] = dot(value, attention).astype(LOW)
+
+        loop(self.head_count, one_head)
+
+    def join(self, pack):
+        r, span = self.r, self.span(pack)
+        second = r.stream[span] + dot(r.mixed[:, span], self.w_out[...], TN)
+        shape, scale = normal(second, -1)
+        r.stream[span] = second
+        r.shape_second[span] = shape.astype(LOW)
+        r.cols[span, 2:3] = scale
+        r.hidden[span] = (shape * self.gain(1)).astype(LOW)
+
+    def widen(self, index):
+        at = tile(index, 256)
+        upward = dot(self.r.hidden[...], self.w_up[:, at])
+        self.upward[:, at] = upward.astype(LOW)
+        self.active[:, at] = (upward * (0.5 * (1.0 + curve(upward)))).astype(LOW)
+
+    def narrow(self, index):
+        at = tile(index, 256)
+        self.r.stream[:, at] += dot(self.active[...], self.w_down[:, at])
+
+    def own_slots(self, ref, pack):
+        wide = ref.shape[1]
+        row = jnp.broadcast_to(ref[pack : pack + 1].astype(FULL), (self.slots, wide))
+        own = self.member_index * self.slots
+        lanes = lax.broadcasted_iota(jnp.int32, row.shape, 1)
+        places = lax.broadcasted_iota(jnp.int32, row.shape, 0)
+        return row_sum(jnp.where(lanes == own + places, row, 0.0))
+
+    def image_spread(self, values, segment, reduce, start):
+        out = jnp.full(values.shape, start, FULL)
+        for slot in range(self.slots):
+            inside = segment == float(slot)
+            one = reduce(jnp.where(inside, values, start if reduce is jnp.max else 0.0), axis=1, keepdims=True)
+            out = jnp.where(inside, one, out)
+        return out
+
+    def classify(self, pack):
+        r, span, slots, width = self.r, self.span(pack), self.slots, self.width
+        strip = 128
+        strips = self.tokens // strip
+
+        def strip_rows(index):
+            return pl.ds(pl.multiple_of(pack * self.tokens + index * strip, strip), strip)
+
+        def finish_norm(index):
+            shape, _ = normal(r.stream[strip_rows(index)], -1)
+            r.low[strip_rows(index)] = (shape * self.gain(2)).astype(LOW)
+
+        loop(strips, finish_norm)
+        final = r.low[span]
+        marks = self.head_marks()
+        marks_low = marks.astype(LOW)
+        probe = self.gain(5)
+        segment = r.segment[pack : pack + 1]
+        scores = dot((marks * probe).astype(LOW), final, NT) * HEAD ** (-0.5)
+        top = self.image_spread(scores, segment, jnp.max, excluded)
+        grown = jnp.where(segment < float(slots), jnp.exp(scores - top), 0.0)
+        pooling = grown / jnp.maximum(self.image_spread(grown, segment, jnp.sum, 1.0), 1e-30)
+        member = (segment == iota((slots, self.tokens), 0)).astype(FULL)
+        pool_wide = pooling.astype(LOW).astype(FULL)
+        r.pool_heads[...] = pool_wide
+        stacked = [member * pool_wide[head : head + 1] for head in range(self.head_count)]
+        stacked = dot(jnp.concatenate(stacked, axis=0).astype(LOW), final)
+        pooled = jnp.zeros((slots, width), FULL)
+        for head in range(self.head_count):
+            pooled = pooled + stacked[head * slots : (head + 1) * slots] * marks[head : head + 1]
+        pooled = pooled.astype(LOW)
+        image_span = pl.ds(pack * slots, slots)
+        r.pooled[image_span] = pooled
+        padded, classes = r.g_cls.shape[-1], r.w_cls.shape[1]
+        logits = [dot(pooled, self.class_block(group)[...]) for group in range(self.groups)]
+        logits = jnp.concatenate(logits, axis=1)
+        lanes = iota(logits.shape, 1)
+        block = jnp.floor((lanes + 0.5) / padded)
+        within = lanes - block * padded
+        logits = jnp.where(within < classes, logits, excluded)
+        hit = block * classes + within == self.own_slots(r.labels, pack)
+        hit = (hit & (within < classes)).astype(FULL)
+        weights = self.own_slots(r.weights, pack)
+        top = jnp.max(logits, axis=1, keepdims=True)
+        log_total = top + jnp.log(row_sum(jnp.exp(logits - top)))
+        losses = weights * (log_total - row_sum(hit * logits))
+        first = (iota((1, width), 1) == 0.0).astype(FULL)
+        r.vgrad[6:7] += first * column_sum(losses)
+        share = weights / r.weight_sum[:, :1]
+        logit_grad = ((jnp.exp(logits - log_total) - hit) * share).astype(LOW)
+        r.logit_grad[image_span] = logit_grad
+        pooled_grad = jnp.zeros((slots, width), FULL)
+        for group in range(self.groups):
+            part = logit_grad[:, group * padded : (group + 1) * padded]
+            pooled_grad = pooled_grad + dot(part, self.class_block(group)[...], NT)
+        r.image_high[...], r.image_rest[...] = halves(pooled_grad)
+
+        def image_rows(index):
+            owner = r.cols[strip_rows(index), 0:1]
+            member_rows = (iota((strip, slots), 1) == owner).astype(LOW)
+            return dot(member_rows, r.image_high[...]) + dot(member_rows, r.image_rest[...])
+
+        def weigh(index):
+            product = image_rows(index) * r.low[strip_rows(index)].astype(FULL)
+            r.score_heads[:, tile(index, strip)] = fine_dot(marks_low, product, NT)
+
+        loop(strips, weigh)
+        weight_grad = r.score_heads[...]
+        mean = self.image_spread(pooling * weight_grad, segment, jnp.sum, 0.0)
+        r.score_heads[...] = pooling * (weight_grad - mean) * HEAD ** (-0.5)
+
+        def strip_back(index):
+            rows, lanes = strip_rows(index), tile(index, strip)
+            high, rest = halves(r.score_heads[:, lanes])
+            score_rows = dot(high, marks_low, TN) + dot(rest, marks_low, TN)
+            pool_rows = dot(r.pool_heads[:, lanes].astype(LOW), marks_low, TN)
+            r.vgrad[5:6] += column_sum(score_rows * r.low[rows].astype(FULL))
+            final_grad = pool_rows * image_rows(index) + score_rows * probe
+            shape, scale = normal(r.stream[rows], -1)
+            r.vgrad[2:3] += column_sum(final_grad * shape)
+            residual_grad = normal_back(final_grad * self.gain(2), shape, scale, -1)
+            r.stream[rows] = residual_grad
+            r.low[rows] = residual_grad.astype(LOW)
+
+        loop(strips, strip_back)
+
+    def class_back(self):
+        r = self.r
+        padded = r.g_cls.shape[-1]
+        for group in range(self.groups):
+            part = r.logit_grad[:, group * padded : (group + 1) * padded]
+            self.class_block(group)[...] = dot(r.pooled[...], part, TN).astype(LOW)
+
+    def active_back(self, index):
+        at = tile(index, 256)
+        upstream = dot(self.r.low[...], self.w_down[at], NT)
+        upward = self.upward[:, at].astype(FULL)
+        bend = curve(upward)
+        squared = upward * upward
+        slope = 0.5 * (1.0 + bend) + (0.5 * 0.7978845608) * upward * (1.0 - bend * bend) * (
+            1.0 + (3 * 0.044715) * squared
+        )
+        self.upward[:, at] = (upstream * slope).astype(LOW)
+
+    def down_weight(self, index):
+        at = tile(index, 256)
+        self.w_down[at] = dot(self.active[:, at], self.r.low[...], TN).astype(LOW)
+
+    def second_back(self, pack):
+        r, span = self.r, self.span(pack)
+        upstream = dot(self.upward[span], self.w_up[...], NT)
+        shape = r.shape_second[span].astype(FULL)
+        r.vgrad[1:2] += column_sum(upstream * shape)
+        back = normal_back(upstream * self.gain(1), shape, r.cols[span, 2:3], -1)
+        total = r.stream[span] + back
+        r.stream[span] = total
+        r.low[span] = total.astype(LOW)
+
+    def up_weight(self, index, part):
+        rows, columns = tile(index, 256), pl.ds(part * COLUMNS, COLUMNS)
+        self.w_up[rows, columns] = dot(self.r.hidden[:, rows], self.upward[:, columns], TN).astype(LOW)
+
+    def mixed_back(self, pack):
+        r, span = self.r, self.span(pack)
+        r.hidden[span] = dot(r.low[span], self.w_out[...], NT).astype(LOW)
+
+    def out_weight(self, index):
+        at = tile(index, 256)
+        self.w_out[at] = dot(self.r.mixed[at], self.r.low[...]).astype(LOW)
+
+    def attend_back(self, pack):
+        r, span = self.r, self.span(pack)
+        self.mask(pack)
+        r.mixed[:, span] = r.hidden[span].T
+        count = self.head_count
+
+        def head_back(grad, part, head, at):
+            own = tile(head, HEAD)
+            shape = r.shape_heads[at, span].astype(FULL)
+            scale = r.scale_heads[pl.ds(part * count + head, 1), span]
+            term = grad * shape
+            for low in range(0, self.tokens, 128):
+                r.gacc[at] += term[:, low : low + 128]
+            back = normal_back(grad * r.gains[own, 3 + part : 4 + part], shape, scale, 0)
+            r.joined[at, span] = back.astype(LOW)
+
+        def one_head(head):
+            parts = self.head_parts(head, span)
+            query, key, value = (r.joined[at, span] for at in parts)
+            mixed_grad = r.mixed[tile(head, HEAD), span]
+            scores = dot(key, query, TN) * HEAD ** (-0.5) + r.mask[...]
+            attention = jnp.exp(scores - r.log_total[pl.ds(head, 1), span])
+            prob_grad = dot(value, mixed_grad, TN)
+            mean = column_sum(attention * prob_grad)
+            score_grad = (attention * (prob_grad - mean)).astype(LOW)
+            r.joined[parts[2], span] = dot(mixed_grad, attention.astype(LOW), NT).astype(LOW)
+            head_back(dot(key, score_grad) * HEAD ** (-0.5), 0, head, parts[0])
+            head_back(dot(query, score_grad, NT) * HEAD ** (-0.5), 1, head, parts[1])
+
+        loop(count, one_head)
+
+    def first_back(self, pack):
+        r, span = self.r, self.span(pack)
+        upstream = dot(r.joined[:, span].T, self.w_qkv[...], NT)
+        shape = r.shape_first[span].astype(FULL)
+        r.vgrad[0:1] += column_sum(upstream * shape)
+        back = normal_back(upstream * self.gain(0), shape, r.cols[span, 1:2], -1)
+        r.low[span] = (r.stream[span] + back).astype(LOW)
+
+    def qkv_weight(self, index):
+        rows = tile(index, 256)
+        turned = self.r.normed[:, rows].T
+        for part in range(3):
+            columns = pl.ds(part * COLUMNS, COLUMNS)
+            self.w_qkv[rows, columns] = dot(turned, self.r.joined[columns], NT).astype(LOW)
+
+    def embed_weight(self):
+        r, width = self.r, self.width
+
+        def one(index):
+            at = tile(index, 256)
+            self.w_embed[at] = dot(r.patches[:, at], r.low[...], TN).astype(LOW)
+
+        loop(width // 256, one)
+        self.w_embed[width:] = dot(r.pos[...], r.low[...], TN).astype(LOW)
+
+    def head_gains(self):
+        r, width = self.r, self.width
+        for part in range(2):
+            r.vgrad[3 + part : 4 + part] = column_sum(r.gacc[part * width : (part + 1) * width].T)
+
+
+def kernel(dims, names, pieces, class_pieces, *refs):
+    r = types.SimpleNamespace(**dict(zip(names, refs)))
+    place = Place(dims)
+    barrier = pltpu.get_barrier_semaphore()
+    pl.semaphore_wait(barrier, place.tell(barrier))
+    courier = Courier(place, r.send, r.recv)
+    layer = Layer(r, place, dims)
+    z, y, x, core = (place.at[axis] for axis in "zyxc")
+    shards = [r.w_embed, r.w_qkv, r.w_out, r.w_up, r.w_down]
+    full = [r.g_embed, r.g_qkv, r.g_out, r.g_up, r.g_down]
+    pairs = [r.p_embed, r.p_qkv, r.p_out, r.p_up, r.p_down]
+    owned = [r.o_embed, r.o_qkv, r.o_out, r.o_up, r.o_down]
+    order = (0, 1, 2, 3, 4)
+
+    arriving = []
+    for shard, pair in zip(shards, pairs):
+        rows, half = shard.shape[0], shard.shape[1] // CORES
+        at = pl.ds(pl.multiple_of(core * rows, 8), rows)
+        other = pl.ds(pl.multiple_of((1 - core) * half, 128), half)
+        arriving.append(courier.start("c", 1, shard.at[:, other], pair.at[at]))
+        pair[at] = shard[:, pl.ds(pl.multiple_of(core * half, 128), half)]
+    r.g_vec[z, y, x, core] = jnp.zeros((8, 128), FULL)
+    count = r.vectors.shape[1]
+    r.g_vec[z, y, x, core, pl.ds(0, 6), pl.ds(0, count)] = r.vectors[...].astype(LOW).astype(FULL)
+    wide = r.weights.shape[1]
+    own = layer.member_index * layer.slots
+    lanes = lax.broadcasted_iota(jnp.int32, r.weights.shape, 1)
+    inside = (lanes >= own) & (lanes < own + layer.slots)
+    counted = column_sum(jnp.where(inside, r.weights[...], 0).astype(FULL))
+    r.g_vec[z, y, x, core, pl.ds(6, 1), pl.ds(0, wide)] = counted
+    block = r.g_cls.at[x, core, z, y]
+    block[...] = jnp.zeros(block.shape, LOW)
+    block[:, pl.ds(0, r.w_cls.shape[1])] = r.w_cls[...].astype(LOW)
+
+    def matrix_view(piece, core):
+        index, rows, columns, _ = piece
+        half = full[index].shape[-1] // CORES
+        across = pl.ds(pl.multiple_of(core * half + columns[0], 128), columns[1])
+        return lambda z, y, x: full[index].at[z, y, x, pl.ds(*rows), across]
+
+    def class_view(piece, core):
+        return lambda z, y, x: r.g_cls.at[x, core, z, y, pl.ds(*piece[1])]
+
+    spreads = [Spread(courier, lambda z, y, x: r.g_vec.at[z, y, x, core], "xy")]
+    ready, last = {}, {}
+    for piece in pieces:
+        ready.setdefault(len(spreads), piece[0]) if piece[0] not in ready.values() else None
+        last[piece[0]] = len(spreads)
+        spreads.append(Spread(courier, matrix_view(piece, core), piece[3]))
+    for piece in class_pieces:
+        last[5] = len(spreads)
+        spreads.append(Spread(courier, class_view(piece, core), piece[3]))
+
+    def begin(position):
+        if position in ready:
+            index = ready[position]
+            arriving[index].wait_recv()
+            half = pairs[index].shape[1]
+            across = pl.ds(pl.multiple_of(core * half, 128), half)
+            full[index][z, y, x, :, across] = pairs[index][...].astype(LOW)
+        spreads[position].begin()
+
+    lag = (-2, 0, 2, 4, 6)
+    actions = (
+        begin,
+        lambda i: spreads[i].middle(1),
+        lambda i: spreads[i].middle(2),
+        lambda i: spreads[i].middle(3),
+        lambda i: spreads[i].done(),
+    )
+    turns = iter(range(lag[0], len(spreads) + lag[-1]))
+    gathered = [0]
+
+    def turn(times=1):
+        for now in itertools.islice(turns, times):
+            for late, action in zip(lag, actions):
+                if 0 <= now - late < len(spreads):
+                    action(now - late)
+            gathered[0] = now - lag[-1] + 1
+
+    def until(index):
+        while gathered[0] <= last[index]:
+            turn()
+
+    turn(3)
+    for pack in range(layer.packs):
+        layer.place_rows(pack)
+        turn()
+    until(0)
+    layer.read_vectors()
+    for pack in range(layer.packs):
+        layer.embed(pack)
+        turn()
+    until(1)
+    for pack in range(layer.packs):
+        layer.project(pack)
+        layer.attend(pack)
+        turn()
+    until(2)
+    for pack in range(layer.packs):
+        layer.join(pack)
+    turn()
+    until(3)
+    tiles = layer.hidden_units // 256
+    loop(tiles, layer.widen)
+    turn()
+    until(4)
+    loop(layer.width // 256, layer.narrow)
+    until(5)
+
+    for pack in range(layer.packs):
+        layer.classify(pack)
+    courier.finish()
+    layer.class_back()
+    left = {index: sum(piece[0] == index for piece in pieces) for index in order}
+    closing = {}
+
+    def keep(piece):
+        index, rows, columns, _ = piece
+
+        def finish(total):
+            pairs[index][pl.ds(*rows), pl.ds(*columns)] = total
+            left[index] -= 1
+            if left[index]:
+                return
+            count, half = owned[index].shape[0], owned[index].shape[1] // CORES
+            across = pl.ds(pl.multiple_of(core * half, 128), half)
+            other = pairs[index].at[pl.ds(pl.multiple_of((1 - core) * count, 8), count)]
+            closing[index] = courier.start("c", 1, other, owned[index].at[:, across])
+            owned[index][:, across] = pairs[index][pl.ds(pl.multiple_of(core * count, 8), count)]
+
+        return finish
+
+    def keep_class(piece):
+        def finish(total):
+            r.o_cls[pl.ds(*piece[1])] = total[:, : r.o_cls.shape[1]]
+
+        return finish
+
+    under_way = []
+
+    def send_class():
+        padded = r.g_cls.shape[-1]
+        for piece in class_pieces:
+            pool = Pool(r.pool_cls, "xzy", piece[1], 0, padded, padded)
+
+            def view(core, piece=piece):
+                return class_view(piece, core)(ALL, ALL, ALL)
+
+            fold = Fold(courier, view, piece[3], pool, keep_class(piece))
+            fold.begin()
+            under_way.append(fold)
+
+    def send_matrix(index, pool_ref, at):
+        mine = [piece for piece in pieces if piece[0] == index]
+        stack = pool_ref.shape[-2] // mine[0][1][1]
+        spots, total = [], 0
+        for position, (_, rows, columns, _) in enumerate(mine):
+            if position % stack == 0:
+                total += columns[1]
+            spots.append(((position % stack * rows[1], rows[1]), at + total - columns[1]))
+        folds = []
+        for piece, (rows, column) in zip(mine, spots):
+            width = piece[2][1]
+            pool = Pool(pool_ref, "zyx", rows, column, column + total, width)
+
+            def view(core, piece=piece):
+                return matrix_view(piece, core)(ALL, ALL, ALL)
+
+            fold = Fold(courier, view, piece[3], pool, keep(piece))
+            fold.begin()
+            folds.append(fold)
+        under_way.extend(folds)
+        return folds
+
+    def pump(times=1, abreast=4):
+        for _ in range(times):
+            for fold in list(under_way[:abreast]):
+                if fold.advance():
+                    under_way.remove(fold)
+
+    def drain(folds):
+        while any(fold in under_way for fold in folds):
+            pump()
+
+    def free(which):
+        pl.semaphore_wait(r.free.at[which], place.tell(r.free.at[which]))
+
+    send_class()
+    loop(tiles // 2, layer.active_back)
+    pump()
+    loop(tiles // 2, lambda index: layer.active_back(index + tiles // 2))
+    pump()
+    loop(tiles, layer.down_weight)
+    free(0)
+    down_folds = send_matrix(4, r.active, 0)
+    pump()
+    for pack in range(layer.packs):
+        layer.second_back(pack)
+        pump()
+    for part in range(layer.hidden_units // COLUMNS):
+        loop(layer.width // 256, lambda index: layer.up_weight(index, part))
+        pump()
+    free(1)
+    send_matrix(3, r.upward, 0)
+    for pack in range(layer.packs):
+        layer.mixed_back(pack)
+    pump()
+    loop(layer.width // 256, layer.out_weight)
+    send_matrix(2, r.pool_out, 0)
+    for pack in range(layer.packs):
+        layer.attend_back(pack)
+        pump()
+    for pack in range(layer.packs):
+        layer.first_back(pack)
+        pump()
+    loop(layer.width // 256, layer.qkv_weight)
+    drain(down_folds)
+    courier.sent([copy for fold in down_folds for copy in fold.copies])
+    free(2)
+    half = full[1].shape[-1] // CORES
+    send_matrix(1, r.active, 0)
+    layer.embed_weight()
+    send_matrix(0, r.active, 2 * half)
+    layer.head_gains()
+    lanes = iota((1, layer.width), 1)
+    devices = dims["x"] * dims["y"] * dims["z"] * CORES
+    r.vgrad[6:7] += jnp.where(lanes == 1.0, r.weight_sum[:, :1] / devices, 0.0)
+
+    strips = []
+    at = 0
+    for index in order:
+        rows, wide = shards[index].shape
+        for low in range(0, wide, COLUMNS):
+            strips.append((index, pl.ds(low, COLUMNS), rows, at))
+            at += rows
+    total_rows = at
+    moments = [
+        (r.m_embed, r.v_embed), (r.m_qkv, r.v_qkv), (r.m_out, r.v_out), (r.m_up, r.v_up),
+        (r.m_down, r.v_down), (r.m_vectors, r.v_vectors), (r.m_cls, r.v_cls),
+    ]
+    outs = [
+        (r.embed_new, r.embed_first, r.embed_second), (r.qkv_new, r.qkv_first, r.qkv_second),
+        (r.out_new, r.out_first, r.out_second), (r.up_new, r.up_first, r.up_second),
+        (r.down_new, r.down_first, r.down_second),
+        (r.vectors_new, r.vectors_first, r.vectors_second), (r.cls_new, r.cls_first, r.cls_second),
+    ]
+    loads = []
+    for position, (index, columns, rows, at) in enumerate(strips):
+        for which in range(2):
+            loads.append(
+                pltpu.make_async_copy(
+                    moments[index][which].at[:, columns],
+                    r.stream.at[pl.ds(at + which * total_rows, rows)],
+                    r.local.at[len(loads)],
+                )
+            )
+            loads[-1].start()
+    vec_total = Total(courier, (r.vec_c, r.vec_x, r.vec_y, r.vec_z))
+    vec_total.send("c", r.vgrad[...])
+    for before, after in zip("cxyz", "xyz "):
+        pump()
+        vec_sum = vec_total.receive(before)
+        if after != " ":
+            vec_total.send(after, vec_sum)
+    while under_way:
+        pump()
+    for index in order:
+        closing[index].wait_recv()
+    for load in loads:
+        load.wait()
+
+    vec_count = r.vectors.shape[1]
+    device = ((z * dims["y"] + y) * dims["x"] + x) * CORES + core
+    at_row = lax.broadcasted_iota(jnp.int32, (layer.width, 128), 0)
+    at_lane = lax.broadcasted_iota(jnp.int32, (layer.width, 128), 1)
+    chosen = ((at_row == device * vec_count + at_lane) & (at_lane < vec_count)).astype(FULL)
+    picked = jnp.dot(vec_sum, chosen, precision=highest, preferred_element_type=FULL)
+    vec_grad = picked[:6, :vec_count]
+    mats = list(zip(owned + [r.o_cls], shards + [r.w_cls]))
+    parts = [squares(grad[...]) for grad, _ in mats] + [squares(weight[...]) for _, weight in mats]
+    block = jnp.concatenate(parts + [wide_rows(r.vectors[...]), jnp.zeros((6, 128), FULL)], axis=0)
+    block = Total(courier, (r.one_c, r.one_x, r.one_y, r.one_z)).through(block)
+    sums = row_sum(block)
+    vec_squares = row_sum(vec_sum * vec_sum)
+    r.loss[...] = vec_sum[6:7, :2]
+    clip_norm = jnp.sqrt(column_sum(sums[:6]) + column_sum(vec_squares[:6]))
+    r.clip[...] = clip_norm
+    factor = jnp.minimum(1.0, clip_limit / clip_norm)
+    partial = {index: jnp.zeros((1, 128), FULL) for index in order}
+    stores = []
+
+    def store(source, target):
+        copy = pltpu.make_async_copy(source, target, r.local.at[len(loads) + len(stores)])
+        copy.start()
+        stores.append(copy)
+
+    for index, columns, rows, at in strips:
+        spot = [pl.ds(at + which * total_rows, rows) for which in range(2)]
+        first, second = moments_step(
+            owned[index][:, columns] * factor, r.stream[spot[0]], r.stream[spot[1]]
+        )
+        update = update_of(first, second, shards[index][:, columns])
+        owned[index][:, columns] = update
+        partial[index] = partial[index] + squares(update)
+        for which, value in enumerate((first, second)):
+            r.stream[spot[which]] = value
+            store(r.stream.at[spot[which]], outs[index][1 + which].at[:, columns])
+    first, second = moments_step(r.o_cls[...] * factor, r.m_cls[...], r.v_cls[...])
+    r.cls_first[...], r.cls_second[...] = first, second
+    class_update = update_of(first, second, r.w_cls[...])
+    r.o_cls[...] = class_update
+    first, second = moments_step(vec_grad * factor, r.m_vectors[...], r.v_vectors[...])
+    r.vectors_first[...], r.vectors_second[...] = first, second
+    vec_update = update_of(first, second, r.vectors[...])
+    parts = [partial[index] for index in order] + [squares(class_update), wide_rows(vec_update)]
+    block = jnp.concatenate(parts + [jnp.zeros((4, 128), FULL)], axis=0)
+    block = Total(courier, (r.two_c, r.two_x, r.two_y, r.two_z)).through(block)
+    grown = jnp.sqrt(row_sum(block))[:12]
+    weight_norms = jnp.sqrt(sums[6:18])
+    r.norms[:, 0:1] = weight_norms
+    r.norms[:, 1:2] = grown
+    ratios = learn_rate * (weight_norms / grown)
+    for index, columns, rows, at in strips:
+        update = owned[index][:, columns]
+        owned[index][:, columns] = shards[index][:, columns] - ratios[index : index + 1] * update
+        store(owned[index].at[:, columns], outs[index][0].at[:, columns])
+    r.cls_new[...] = r.w_cls[...] - ratios[5:6] * r.o_cls[...]
+    r.vectors_new[...] = r.vectors[...] - ratios[6:12] * vec_update
+    for copy in stores:
+        copy.wait()
+    courier.finish()
+
+
+WEIGHTS = ("embed", "qkv", "out", "up", "down", "vectors", "cls")
+
+
+def kernel_body(
+    dims, patches, heights, widths, labels, res_weights, *params_moments
+):
+    X, Y, Z = (dims[axis] for axis in "xyz")
+    params, moments = params_moments[:7], params_moments[7:]
+    mats, w_cls = params[:5], params[6]
+    blocks = [(CORES * w.shape[0], w.shape[1] // CORES) for w in mats]
+    pieces = pieces_of(blocks)
+    padded = -(-w_cls.shape[1] // 128) * 128
+    class_rows = w_cls.shape[0]
+    class_pieces = [
+        (5, rows, columns, ("xy", "yx")[turn])
+        for turn, (rows, columns) in enumerate(cut(class_rows, padded, 2))
+    ]
+    packs, tokens, width = patches.shape
+    rows = packs * tokens
+    chips = X * Y * Z
+    hidden_units = mats[3].shape[1]
+    heads = width // HEAD
+    images = packs * heights.shape[1]
+    vmem = pl.BlockSpec(memory_space=pltpu.VMEM)
+    anywhere = pl.BlockSpec(memory_space=pl.ANY)
+    inputs = {"patches": patches.reshape(rows, width), "heights": heights, "widths": widths}
+    inputs.update(labels=labels, weights=res_weights)
+    specs = [vmem] * 5
+    for name, param in zip(WEIGHTS, params):
+        inputs["vectors" if name == "vectors" else "w_" + name] = param
+        specs.append(vmem)
+    for position, name in enumerate(WEIGHTS):
+        inputs["m_" + name], inputs["v_" + name] = moments[2 * position : 2 * position + 2]
+        specs += [anywhere if position < 5 else vmem] * 2
+    outs = {"loss": (1, 2), "clip": (1, 1), "norms": (12, 2)}
+    out_specs = [vmem] * 3
+    for position, (name, param) in enumerate(zip(WEIGHTS, params)):
+        for kind in ("_new", "_first", "_second"):
+            outs[name + kind] = param.shape
+            out_specs.append(anywhere if position < 5 else vmem)
+    scratch = {}
+    for name, param, block in zip(WEIGHTS, mats, blocks):
+        scratch["g_" + name] = pltpu.VMEM((Z, Y, X, block[0], param.shape[1]), LOW)
+        scratch["p_" + name] = pltpu.VMEM(block, FULL)
+        scratch["o_" + name] = pltpu.VMEM(param.shape, FULL)
+    scratch["o_cls"] = pltpu.VMEM(w_cls.shape, FULL)
+    scratch["g_cls"] = pltpu.VMEM((X, CORES, Z, Y, class_rows, padded), LOW)
+    scratch["g_vec"] = pltpu.VMEM((Z, Y, X, CORES, 8, 128), FULL)
+    scratch["pool_cls"] = pltpu.VMEM((X, Z, Y, class_rows, 2 * padded), LOW)
+    scratch["pool_out"] = pltpu.VMEM((Z, Y, X) + (blocks[2][0], 2 * blocks[2][1]), LOW)
+    low_rows = ("normed", "hidden", "shape_first", "shape_second", "low")
+    scratch.update({name: pltpu.VMEM((rows, width), LOW) for name in low_rows})
+    scratch["pos"] = pltpu.VMEM((rows, 2 * POS), LOW)
+    scratch["cols"] = pltpu.VMEM((rows, 128), FULL)
+    scratch["segment"] = pltpu.VMEM((packs, tokens), FULL)
+    scratch["stream"] = pltpu.VMEM((rows, width), FULL)
+    scratch["turned"] = pltpu.VMEM((width, tokens), FULL)
+    scratch["joined"] = pltpu.VMEM((3 * width, rows), LOW)
+    scratch["shape_heads"] = pltpu.VMEM((2 * width, rows), LOW)
+    scratch["scale_heads"] = pltpu.VMEM((2 * heads, rows), FULL)
+    scratch["log_total"] = pltpu.VMEM((heads, rows), FULL)
+    scratch["mixed"] = pltpu.VMEM((width, rows), LOW)
+    scratch["mask"] = pltpu.VMEM((tokens, tokens), FULL)
+    wide = (Z, Y, X, rows // chips, hidden_units)
+    scratch["upward"], scratch["active"] = pltpu.VMEM(wide, LOW), pltpu.VMEM(wide, LOW)
+    scratch["vec"], scratch["vgrad"] = pltpu.VMEM((8, width), FULL), pltpu.VMEM((8, width), FULL)
+    scratch["gains"] = pltpu.VMEM((width, 8), FULL)
+    scratch["gacc"] = pltpu.VMEM((2 * width, 128), FULL)
+    scratch["weight_sum"] = pltpu.VMEM((1, 128), FULL)
+    scratch["pooled"] = pltpu.VMEM((images, width), LOW)
+    for name in ("pool_heads", "score_heads"):
+        scratch[name] = pltpu.VMEM((16, tokens), FULL)
+    for name in ("image_high", "image_rest"):
+        scratch[name] = pltpu.VMEM((heights.shape[1], width), LOW)
+    scratch["logit_grad"] = pltpu.VMEM((images, X * CORES * padded), LOW)
+    for name, shape in (("vec_", (8, width)), ("one_", (24, 128)), ("two_", (16, 128))):
+        for axis, slots in zip("cxyz", total_slots(dims, shape)):
+            scratch[name + axis] = slots
+    peers = (X - 1) + (Y - 1) + (Z - 1) + 1
+    count = (len(pieces) + len(class_pieces)) * (2 * peers + X - 1 + Y - 1)
+    count += 10 + 3 * peers + 2 * peers
+    scratch["send"] = pltpu.SemaphoreType.DMA((count,))
+    scratch["recv"] = pltpu.SemaphoreType.DMA((count,))
+    scratch["local"] = pltpu.SemaphoreType.DMA((5 * sum(w.shape[1] // COLUMNS for w in mats),))
+    scratch["free"] = pltpu.SemaphoreType.REGULAR((3,))
+    names = list(inputs) + list(outs) + list(scratch)
+    loss_terms, clip_norm, *updated = pl.pallas_call(
+        functools.partial(kernel, dims, names, pieces, class_pieces),
+        out_shape=[jax.ShapeDtypeStruct(shape, FULL) for shape in outs.values()],
+        in_specs=specs,
+        out_specs=out_specs,
+        scratch_shapes=list(scratch.values()),
+        compiler_params=pltpu.CompilerParams(
+            collective_id=0, has_side_effects=True, vmem_limit_bytes=(64 << 20) - 4096
+        ),
+    )(*inputs.values())
+    return (loss_terms.reshape(2), clip_norm.reshape(()), *updated)
+
+
+def chip_dims(mesh):
+    across, along = mesh.shape["mp"] // CORES, mesh.shape["dp"]
+    return {"x": across, "y": across, "z": along // across}
+
+
+def fits(mesh, width):
+    devices = mesh.shape["dp"] * mesh.shape["mp"]
+    dims = chip_dims(mesh)
+    same = dims["x"] * dims["y"] * dims["z"] * CORES == devices
+    return same and width % (8 * devices) == 0 and width // devices * CORES % 16 == 0
+
+
 def solution(mesh):
     placed = (
         P(None, ("dp", "mp"), None),
@@ -483,8 +1607,11 @@
         P("dp", "mp"),
         P("dp", "mp"),
     )
+    run = body
+    if fits(mesh, 768):
+        run = functools.partial(kernel_body, chip_dims(mesh))
     return jax.shard_map(
-        body,
+        run,
         mesh=mesh,
         in_specs=placed,
         out_specs=(

time: 1480 us -> 373 us (0.25)
  waiting for transfers between devices: 594 us -> 0 us
  Pallas kernels: 0 us -> 344 us
  blocking collectives: 272 us -> 0 us
  matrix products: 243 us -> 0 us
  other arithmetic: 163 us -> 0 us
  local copies, waits for them, and re-layouts: 165 us -> 21.1 us
  between operations: 29.2 us -> 3.04 us
    reduce_scatter x10 -> x0, waiting for transfers between devices: 528 us -> none  [the longest x1 140 us: reduce_grads(): lax.psum_scatter(fresh[4], ('dp', 'mp'), scatter_dimension=0, tiled=True)]
    pallas_call x0 -> x1, Pallas kernels: none -> 344 us  [kernel_body(): pl.pallas_call(functools.partial(kernel, dims, names, pieces, class_piece...]
    dot_general x120 -> x0, matrix products: 243 us -> none  [the longest x28 82.5 us: outer_dot(): lax.dot_general(left, right, (((0,), (0,)), ((), ())), preferred_element_...]
    psum x3 -> x0, blocking collectives: 122 us -> none  [the longest x2 80.1 us: body(): square_sums, loss_total = lax.psum((grad_squares, loss_local), ('dp', 'mp'))]
    all_gather x6 -> x0, blocking collectives: 97.9 us -> none  [the longest x1 40.8 us: body(): lax.all_gather(vectors.astype(jnp.bfloat16), ('dp', 'mp'), axis=1, tiled=...]
    all_gather x5 -> x0, waiting for transfers between devices: 66.2 us -> none  [the longest x1 60.1 us: body(): lax.all_gather(w_down.astype(jnp.bfloat16), ('dp', 'mp'), axis=0, tiled=T...]
    reduce_sum x67 -> x0, other arithmetic: 64 us -> none  [the longest x11 12.8 us: layer_norm(): center = values - jnp.mean(values, axis=-1, keepdims=True)]
    unnamed x2 -> x0, blocking collectives: 51.5 us -> none
  transfers between devices with their start and end apart: 15 -> 0, of which waited for: 9 -> 0; matrix products, arithmetic and copies ran while one was open for 24% -> 0% of each run, Pallas kernels for 0% -> 0%
where the time goes in v2:
time: 373 us; the launch traced here: 368 us
  Pallas kernels  344 us (92%)
  local copies, waits for them, and re-layouts  21.1 us (6%)
    pallas_call x1, Pallas kernels, kernel_body(): pl.pallas_call(functools.partial(kernel, dims, names, pieces, class_piece...  344 us
    unnamed x55, local copies, waits for them, and re-layouts  21.1 us

profile of v2, /device:TPU:0, one launch (start us, length us, event | category | flops | bytes accessed | tf_op | source)
XLA Modules:
  0.0 368.2 jit_solution(1966174738674620200)
XLA Ops:
  0.7 344.1 %shard_map.433 = (f32[1,2]{1,0:T(1,128)}, f32[1,1]{1,0:T(1,128)}, f32[12,2]{1,0:T(8,128)}, f32[32,768]{1,0:T(8,128)}, f32[32,768]{1,0:T(8,128)}, /*index=5*/f32[...) custom-call(bf16[1024,768]{1,0:T(8,128)(2,1)} %bitcast.3, ...), custom_call_target="tpu_custom_call" | custom-call | tf_op jit(solution)/shard_map/pallas_call | solution.py:1556
  344.7 0.0 copy-start.6
  344.7 0.0 copy-start.12
  344.8 0.0 copy-start.11
  344.8 0.0 copy-start.10
  344.8 0.0 copy-start.5
  344.8 0.0 copy-start.4
  344.8 1.4 copy.50
  346.2 1.1 copy.74
  348.0 1.5 copy.76
  349.6 1.5 copy.77
  351.1 0.0 copy-start.3
  351.1 1.6 copy.78
  352.7 1.6 copy.79
  354.3 0.0 copy-start.2
  354.3 1.7 copy.80
  356.0 0.0 copy-done.6
  356.0 0.0 copy-start.1
  356.0 0.7 copy.81
  356.7 0.0 copy-done.12
  356.7 0.6 copy.82
  357.3 0.0 copy-done.11
  357.3 0.6 copy.83
  358.0 0.0 copy-done.10
  358.0 0.0 copy-start
  358.0 0.6 copy.84
  358.6 0.0 copy-done.5
  358.6 0.7 copy.85
  359.3 0.0 copy-done.4
  359.3 0.0 copy-start.15
  359.3 0.0 copy-start.14
  359.3 0.0 copy-start.13
  359.3 0.0 copy-start.9
  359.3 0.0 copy-start.8
  359.4 0.0 copy-start.7
  359.4 0.7 copy.86
  360.1 0.0 copy-done.3
  360.1 0.7 copy.87
  360.8 0.0 copy-done.2
  360.8 0.7 copy.88
  361.5 0.0 copy-done.1
  361.5 0.7 copy.89
  362.2 0.0 copy-done
  362.2 0.7 copy.90
  362.9 0.0 copy-done.15
  362.9 0.6 copy.91
  363.5 0.0 copy-done.14
  363.5 0.6 copy.92
  364.1 0.0 copy-done.13
  364.1 0.6 copy.93
  364.7 0.0 copy-done.9
  364.7 0.6 copy.94
  365.4 0.0 copy-done.8
  365.4 0.6 copy.95
  366.0 0.0 copy-done.7
  366.0 0.6 copy.96
Async XLA Ops:
  344.7 11.3 %copy-start.6 = (f32[24,2304]{1,0:T(8,128)S(1)}, f32[24,2304]{1,0:T(8,128)}, u32[]{:S(2)}) copy-start(f32[24,2304]{1,0:T(8,128)} %get-tuple-element.128) | copy-start | bytes 663556
  344.7 12.0 %copy-start.12 = (f32[24,768]{1,0:T(8,128)S(1)}, f32[24,768]{1,0:T(8,128)}, u32[]{:S(2)}) copy-start(f32[24,768]{1,0:T(8,128)} %get-tuple-element.129) | copy-start | bytes 221188
  344.8 12.6 %copy-start.11 = (f32[24,768]{1,0:T(8,128)S(1)}, f32[24,768]{1,0:T(8,128)}, u32[]{:S(2)}) copy-start(f32[24,768]{1,0:T(8,128)} %get-tuple-element.130) | copy-start | bytes 221188
  344.8 13.2 %copy-start.10 = (f32[24,768]{1,0:T(8,128)S(1)}, f32[24,768]{1,0:T(8,128)}, u32[]{:S(2)}) copy-start(f32[24,768]{1,0:T(8,128)} %get-tuple-element.131) | copy-start | bytes 221188
  344.8 13.8 %copy-start.5 = (f32[24,3072]{1,0:T(8,128)S(1)}, f32[24,3072]{1,0:T(8,128)}, u32[]{:S(2)}) copy-start(f32[24,3072]{1,0:T(8,128)} %get-tuple-element.132) | copy-start | bytes 884740
  344.8 14.5 %copy-start.4 = (f32[24,3072]{1,0:T(8,128)S(1)}, f32[24,3072]{1,0:T(8,128)}, u32[]{:S(2)}) copy-start(f32[24,3072]{1,0:T(8,128)} %get-tuple-element.133) | copy-start | bytes 884740
  351.1 9.0 %copy-start.3 = (f32[24,3072]{1,0:T(8,128)S(1)}, f32[24,3072]{1,0:T(8,128)}, u32[]{:S(2)}) copy-start(f32[24,3072]{1,0:T(8,128)} %get-tuple-element.134) | copy-start | bytes 884740
  354.3 6.5 %copy-start.2 = (f32[96,768]{1,0:T(8,128)S(1)}, f32[96,768]{1,0:T(8,128)}, u32[]{:S(2)}) copy-start(f32[96,768]{1,0:T(8,128)} %get-tuple-element.135) | copy-start | bytes 884740
  356.0 5.5 %copy-start.1 = (f32[96,768]{1,0:T(8,128)S(1)}, f32[96,768]{1,0:T(8,128)}, u32[]{:S(2)}) copy-start(f32[96,768]{1,0:T(8,128)} %get-tuple-element.136) | copy-start | bytes 884740
  358.0 4.3 %copy-start = (f32[96,768]{1,0:T(8,128)S(1)}, f32[96,768]{1,0:T(8,128)}, u32[]{:S(2)}) copy-start(f32[96,768]{1,0:T(8,128)} %get-tuple-element.137) | copy-start | bytes 884740
  359.3 3.6 copy-start.15
  359.3 4.2 %copy-start.14 = (f32[6,24]{1,0:T(8,128)S(1)}, f32[6,24]{1,0:T(8,128)}, u32[]{:S(2)}) copy-start(f32[6,24]{1,0:T(8,128)} %get-tuple-element.139) | copy-start | bytes 1732
  359.3 4.8 %copy-start.13 = (f32[6,24]{1,0:T(8,128)S(1)}, f32[6,24]{1,0:T(8,128)}, u32[]{:S(2)}) copy-start(f32[6,24]{1,0:T(8,128)} %get-tuple-element.140) | copy-start | bytes 1732
  359.3 5.4 %copy-start.9 = (f32[96,250]{1,0:T(8,128)S(1)}, f32[96,250]{1,0:T(8,128)}, u32[]{:S(2)}) copy-start(f32[96,250]{1,0:T(8,128)} %get-tuple-element.141) | copy-start | bytes 288004
  359.3 6.0 %copy-start.8 = (f32[96,250]{1,0:T(8,128)S(1)}, f32[96,250]{1,0:T(8,128)}, u32[]{:S(2)}) copy-start(f32[96,250]{1,0:T(8,128)} %get-tuple-element.142) | copy-start | bytes 288004
  359.4 6.7 %copy-start.7 = (f32[96,250]{1,0:T(8,128)S(1)}, f32[96,250]{1,0:T(8,128)}, u32[]{:S(2)}) copy-start(f32[96,250]{1,0:T(8,128)} %get-tuple-element.143) | copy-start | bytes 288004

commit v3 on v2

--- a/solution.py
+++ b/solution.py
@@ -469,6 +469,18 @@
 NT = (((1,), (1,)), ((), ()))
 TN = (((0,), (0,)), ((), ()))
 COLUMNS = 768
+SCORE_SCALE = HEAD ** (-0.5) * 1.4426950408889634
+FOLD_LAG = 4
+NEWEST_FIRST = 1
+ENTER = 1
+GATHER_LAGS = (-2, 0, 2, 4, 6)
+PIECE_SIZE = 9216
+MOST_PIECES = 6
+WIDE = 3
+ACROSS = 0
+HEADS_AT_ONCE = 3
+NORMS_AT_ONCE = 6
+STRIP = 256
 
 
 class Place:
@@ -482,30 +494,33 @@
         size = self.sizes[axis]
         return (self.at[axis] + (size - step) % size) % size
 
-    def peer(self, axis, step):
-        at = dict(self.at)
-        at[axis] = self.source(axis, -step)
+    def peer(self, steps):
+        at = {axis: self.source(axis, -steps.get(axis, 0)) for axis in "zyxc"}
         return (at["z"] * self.sizes["y"] + at["y"], at["x"] * CORES + at["c"])
 
     def steps(self, axis):
         return range(1, self.sizes[axis])
 
-    def tell(self, semaphore):
-        count = 0
-        for axis in "cxyz":
-            for step in self.steps(axis):
-                pl.semaphore_signal(
-                    semaphore, inc=1, device_id=self.peer(axis, step), device_id_type=MESH_ID
-                )
-                count += 1
-        return count
+    def lines(self):
+        return [{axis: step} for axis in "cxyz" for step in self.steps(axis)]
+
+    def plane(self):
+        ranges = (range(self.sizes[axis]) for axis in "yxc")
+        return [dict(zip("yxc", steps)) for steps in itertools.product(*ranges) if any(steps)]
+
+    def tell(self, semaphore, peers):
+        for steps in peers:
+            pl.semaphore_signal(
+                semaphore, inc=1, device_id=self.peer(steps), device_id_type=MESH_ID
+            )
+        return len(peers)
 
 
 class Courier:
     def __init__(self, place, send, recv):
         self.place, self.send, self.recv, self.open, self.count = place, send, recv, [], 0
 
-    def start(self, axis, step, source, target):
+    def start(self, steps, source, target):
         slot = self.count
         self.count += 1
         copy = pltpu.make_async_remote_copy(
@@ -513,7 +528,7 @@
             dst_ref=target,
             send_sem=self.send.at[slot],
             recv_sem=self.recv.at[slot],
-            device_id=self.place.peer(axis, step),
+            device_id=self.place.peer(steps),
             device_id_type=MESH_ID,
         )
         copy.start()
@@ -536,31 +551,34 @@
 
     def part(self, stage, **fixed):
         where = {axis: self.place.at[axis] for axis in "xyz"}
-        for axis in ("z" + self.order)[:stage]:
+        for axis in self.order[:stage]:
             where[axis] = ALL
         where.update(fixed)
         return self.view(**where)
 
-    def send(self, axis, stage):
-        part = self.part(stage)
-        return [self.courier.start(axis, step, part, part) for step in self.place.steps(axis)]
+    def send(self, stage):
+        axis, part = self.order[stage], self.part(stage)
+        self.coming = [
+            self.courier.start({axis: step}, part, part) for step in self.place.steps(axis)
+        ]
 
     def relay(self, part):
-        self.relayed.append(self.courier.start("c", 1, part, part))
+        self.relayed.append(self.courier.start({"c": 1}, part, part))
 
     def begin(self):
-        self.coming = self.send("z", 0)
+        self.send(0)
 
     def middle(self, stage):
         for copy in self.coming:
             copy.wait_recv()
+        if stage < 3:
+            self.send(stage)
         if stage == 1:
             self.relay(self.part(1))
-        else:
-            axis = self.order[stage - 2]
-            for step in self.place.steps(axis):
-                self.relay(self.part(stage - 1, **{axis: self.place.source(axis, step)}))
-        self.coming = self.send(self.order[stage - 1], stage) if stage < 3 else []
+            return
+        axis = self.order[stage - 1]
+        for step in self.place.steps(axis):
+            self.relay(self.part(stage - 1, **{axis: self.place.source(axis, step)}))
 
     def done(self):
         for copy in self.relayed:
@@ -579,25 +597,21 @@
 class Fold:
     def __init__(self, courier, view, order, pool, finish):
         self.courier, self.place, self.view, self.order = courier, courier.place, view, order
-        self.pool, self.finish, self.copies, self.stage = pool, finish, [], 0
+        self.pool, self.finish, self.copies, self.stage, self.due = pool, finish, [], 0, None
 
     def start(self, axis, step, source, target):
-        copy = self.courier.start(axis, step, source, target)
+        copy = self.courier.start({axis: step}, source, target)
         self.copies.append(copy)
         self.coming.append(copy)
 
     def landing(self, stage, step):
-        first, second = self.order
-        sizes = self.place.sizes
-        if stage == 1:
-            return self.pool.at(1, **{first: step - 1})
-        if stage == 2:
-            return self.pool.at(1, **{first: sizes[first] - 1, second: step - 1})
-        return self.pool.at(1, **{first: sizes[first] - 1, second: sizes[second] - 1, "z": step - 1})
+        where = {axis: self.place.sizes[axis] - 1 for axis in self.order[: stage - 1]}
+        where[self.order[stage - 1]] = step - 1
+        return self.pool.at(1, **where)
 
     def send(self, stage):
-        axis = (self.order + "z")[stage - 1]
-        fixed = {a: self.place.at[a] for a in self.order[: stage - 1]}
+        axis = self.order[stage - 1]
+        fixed = place_of(self.place, self.order[: stage - 1])
         self.coming = []
         for step in self.place.steps(axis):
             source = self.pool.at(0, **{axis: self.place.source(axis, -step)}, **fixed)
@@ -613,9 +627,9 @@
         stage, place = self.stage, self.place
         self.stage += 1
         if stage == 3:
-            here = self.pool.at(0, **place_of(place, "xyz"))
+            here = self.pool.at(0, **place_of(place, self.order))
             total = here[...].astype(FULL)
-            for step in place.steps("z"):
+            for step in place.steps(self.order[2]):
                 total = total + self.landing(3, step)[...].astype(FULL)
             self.finish(total)
             return True
@@ -642,42 +656,46 @@
 
 
 class Total:
-    def __init__(self, courier, slots):
-        self.courier, self.place, self.slots = courier, courier.place, dict(zip("cxyz", slots))
-
-    def send(self, axis, block):
-        mine = self.slots[axis].at[self.place.at[axis]]
+    def __init__(self, courier, plane_slots, line_slots):
+        self.courier, self.place = courier, courier.place
+        self.stages = [
+            (plane_slots, self.place.plane()),
+            (line_slots, [{"z": step} for step in self.place.steps("z")]),
+        ]
+
+    def send(self, stage, block):
+        slots, peers = self.stages[stage]
+        at, sizes = self.place.at, self.place.sizes
+        index = at["z"] if stage else (at["y"] * sizes["x"] + at["x"]) * CORES + at["c"]
+        mine = slots.at[index]
         mine[...] = block
-        self.coming = [
-            self.courier.start(axis, step, mine, mine) for step in self.place.steps(axis)
-        ]
-
-    def receive(self, axis):
+        self.coming = [self.courier.start(steps, mine, mine) for steps in peers]
+
+    def receive(self, stage):
         for copy in self.coming:
             copy.wait_recv()
-        slots = self.slots[axis]
+        slots = self.stages[stage][0]
         total = slots[0]
         for index in range(1, slots.shape[0]):
             total = total + slots[index]
         return total
 
     def through(self, block):
-        for axis in "cxyz":
-            self.send(axis, block)
-            block = self.receive(axis)
+        for stage in range(2):
+            self.send(stage, block)
+            block = self.receive(stage)
         return block
 
 
-def total_slots(dims, shape):
-    sizes = dict(dims, c=CORES)
-    return [pltpu.VMEM((sizes[axis],) + shape, FULL) for axis in "cxyz"]
+def cut_rows(rows, width, parts):
+    size = rows // parts
+    return [((part * size, size), (0, width)) for part in range(parts)]
 
 
 def cut(rows, width, parts):
-    if rows % (16 * parts) == 0:
-        size = rows // parts
-        return [((part * size, size), (0, width)) for part in range(parts)]
     units = width // 128
+    if units % parts and rows % (16 * parts) == 0:
+        return cut_rows(rows, width, parts)
     marks = [units * part // parts * 128 for part in range(parts + 1)]
     return [((0, rows), (low, high - low)) for low, high in zip(marks, marks[1:]) if high > low]
 
@@ -685,9 +703,12 @@
 def pieces_of(blocks):
     found = []
     for index, (rows, width) in enumerate(blocks):
-        parts = max(2, min(4, rows * width // 16384 // 2 * 2))
+        parts = max(2, min(MOST_PIECES, rows * width // PIECE_SIZE))
         for row_range, column_range in cut(rows, width, parts):
-            found.append((index, row_range, column_range, ("xy", "yx")[len(found) % 2]))
+            found.append((index, row_range, column_range, ("zxy", "zyx")[len(found) % 2]))
+    across = [at for at, piece in enumerate(found) if piece[0] == WIDE][:ACROSS]
+    for turn, at in enumerate(across):
+        found[at] = found[at][:3] + (("xyz", "yxz")[turn % 2],)
     return found
 
 
@@ -727,10 +748,6 @@
 
 def row_sum(values):
     return jnp.sum(values, axis=1, keepdims=True)
-
-
-def curve(values):
-    return jnp.tanh(0.7978845608 * (values + 0.044715 * values * values * values))
 
 
 def squares(values):
@@ -794,6 +811,9 @@
         self.w_down = r.g_down.reshape(self.hidden_units, self.width)
         self.upward = r.upward.reshape(self.rows, self.hidden_units)
         self.active = r.active.reshape(self.rows, self.hidden_units)
+        self.joined = r.joined.reshape(3 * self.width, self.rows)
+        self.shape_heads = r.shape_heads.reshape(2 * self.width, self.rows)
+        self.shape_second = r.shape_second.reshape(self.rows, self.width)
 
     def span(self, pack):
         return pl.ds(pack * self.tokens, self.tokens)
@@ -850,7 +870,6 @@
         total = jnp.sum(blocks, axis=0)[6:7]
         r.weight_sum[...] = jnp.broadcast_to(row_sum(total), (1, 128))
         r.vgrad[...] = jnp.zeros(r.vgrad.shape, FULL)
-        r.gacc[...] = jnp.zeros(r.gacc.shape, FULL)
 
     def embed(self, pack):
         r, span = self.r, self.span(pack)
@@ -867,19 +886,23 @@
         for part in range(3):
             joined = dot(r.normed[span], self.w_qkv[:, part * width : (part + 1) * width])
             if part == 2:
-                r.joined[2 * width :, span] = joined.T.astype(LOW)
+                self.joined[2 * width :, span] = joined.T.astype(LOW)
                 continue
             r.turned[...] = joined.T
 
-            def one_head(head, part=part):
-                own = tile(head, HEAD)
-                at = pl.ds(pl.multiple_of(part * width + head * HEAD, HEAD), HEAD)
-                shape, scale = normal(r.turned[own], 0)
-                r.shape_heads[at, span] = shape.astype(LOW)
-                r.scale_heads[pl.ds(part * self.head_count + head, 1), span] = scale
-                r.joined[at, span] = (shape * r.gains[own, 3 + part : 4 + part]).astype(LOW)
-
-            loop(self.head_count, one_head)
+            def some_heads(group, part=part):
+                heads = [group * NORMS_AT_ONCE + member for member in range(NORMS_AT_ONCE)]
+                owns = [tile(head, HEAD) for head in heads]
+                found = [normal(r.turned[own], 0) for own in owns]
+                gains = [r.gains[own, 3 + part : 4 + part] for own in owns]
+                results = [shape * gain for (shape, _), gain in zip(found, gains)]
+                for head, (shape, scale), result in zip(heads, found, results):
+                    at = pl.ds(pl.multiple_of(part * width + head * HEAD, HEAD), HEAD)
+                    self.shape_heads[at, span] = shape.astype(LOW)
+                    r.scale_heads[pl.ds(part * self.head_count + head, 1), span] = scale
+                    self.joined[at, span] = result.astype(LOW)
+
+            loop(self.head_count // NORMS_AT_ONCE, some_heads)
 
     def mask(self, pack):
         r = self.r
@@ -894,32 +917,40 @@
         r, span = self.r, self.span(pack)
         self.mask(pack)
 
-        def one_head(head):
-            query, key, value = (r.joined[at, span] for at in self.head_parts(head, span))
-            scores = dot(key, query, TN) * HEAD ** (-0.5) + r.mask[...]
-            top = jnp.max(scores, axis=0, keepdims=True)
-            grown = jnp.exp(scores - top)
-            total = column_sum(grown)
-            r.log_total[pl.ds(head, 1), span] = top + jnp.log(total)
-            attention = (grown * (1.0 / total)).astype(LOW)
-            r.mixed[tile(head, HEAD), span] = dot(value, attention).astype(LOW)
-
-        loop(self.head_count, one_head)
+        def some_heads(group):
+            heads = [group * HEADS_AT_ONCE + member for member in range(HEADS_AT_ONCE)]
+            loaded = [[self.joined[at, span] for at in self.head_parts(head, span)] for head in heads]
+            mask = r.mask[...]
+            scores = [dot(key, query, TN) * SCORE_SCALE + mask for query, key, _ in loaded]
+            tops = [jnp.max(score, axis=0, keepdims=True) for score in scores]
+            grown = [jnp.exp2(score - top) for score, top in zip(scores, tops)]
+            totals = [column_sum(part) for part in grown]
+            shares = [(part * (1.0 / total)).astype(LOW) for part, total in zip(grown, totals)]
+            mixed = [dot(parts[2], share).astype(LOW) for parts, share in zip(loaded, shares)]
+            for head, top, total, result in zip(heads, tops, totals, mixed):
+                r.log_total[pl.ds(head, 1), span] = top + jnp.log2(total)
+                r.mixed[tile(head, HEAD), span] = result
+
+        loop(self.head_count // HEADS_AT_ONCE, some_heads)
 
     def join(self, pack):
         r, span = self.r, self.span(pack)
         second = r.stream[span] + dot(r.mixed[:, span], self.w_out[...], TN)
         shape, scale = normal(second, -1)
         r.stream[span] = second
-        r.shape_second[span] = shape.astype(LOW)
+        self.shape_second[span] = shape.astype(LOW)
         r.cols[span, 2:3] = scale
         r.hidden[span] = (shape * self.gain(1)).astype(LOW)
 
     def widen(self, index):
         at = tile(index, 256)
         upward = dot(self.r.hidden[...], self.w_up[:, at])
-        self.upward[:, at] = upward.astype(LOW)
-        self.active[:, at] = (upward * (0.5 * (1.0 + curve(upward)))).astype(LOW)
+        squared = upward * upward
+        bent = 0.5 + 0.5 * jnp.tanh(upward * (0.7978845608 + 0.7978845608 * 0.044715 * squared))
+        active = upward * bent
+        steep = 2.0 * 0.7978845608 + 6.0 * 0.7978845608 * 0.044715 * squared
+        self.active[:, at] = active.astype(LOW)
+        self.upward[:, at] = (bent + active * (1.0 - bent) * steep).astype(LOW)
 
     def narrow(self, index):
         at = tile(index, 256)
@@ -941,39 +972,45 @@
             out = jnp.where(inside, one, out)
         return out
 
-    def classify(self, pack):
-        r, span, slots, width = self.r, self.span(pack), self.slots, self.width
-        strip = 128
-        strips = self.tokens // strip
-
-        def strip_rows(index):
-            return pl.ds(pl.multiple_of(pack * self.tokens + index * strip, strip), strip)
+    def classify(self):
+        r, slots, width, packs = self.r, self.slots, self.width, self.packs
+        strip = STRIP
+        per_pack = self.tokens // strip
+        strips = packs * per_pack
 
         def finish_norm(index):
-            shape, _ = normal(r.stream[strip_rows(index)], -1)
-            r.low[strip_rows(index)] = (shape * self.gain(2)).astype(LOW)
+            rows = tile(index, strip)
+            shape, _ = normal(r.stream[rows], -1)
+            r.low[rows] = (shape * self.gain(2)).astype(LOW)
 
         loop(strips, finish_norm)
-        final = r.low[span]
         marks = self.head_marks()
         marks_low = marks.astype(LOW)
         probe = self.gain(5)
-        segment = r.segment[pack : pack + 1]
-        scores = dot((marks * probe).astype(LOW), final, NT) * HEAD ** (-0.5)
+        probe_marks = (marks * probe).astype(LOW)
+        finals = [r.low[self.span(pack)] for pack in range(packs)]
+        scores = [dot(probe_marks, final, NT) for final in finals]
+        scores = jnp.concatenate(scores, axis=0) * HEAD ** (-0.5)
+        tall = (marks.shape[0], self.tokens)
+        segment = [jnp.broadcast_to(r.segment[pack : pack + 1], tall) for pack in range(packs)]
+        segment = jnp.concatenate(segment, axis=0)
         top = self.image_spread(scores, segment, jnp.max, excluded)
         grown = jnp.where(segment < float(slots), jnp.exp(scores - top), 0.0)
         pooling = grown / jnp.maximum(self.image_spread(grown, segment, jnp.sum, 1.0), 1e-30)
-        member = (segment == iota((slots, self.tokens), 0)).astype(FULL)
         pool_wide = pooling.astype(LOW).astype(FULL)
         r.pool_heads[...] = pool_wide
-        stacked = [member * pool_wide[head : head + 1] for head in range(self.head_count)]
-        stacked = dot(jnp.concatenate(stacked, axis=0).astype(LOW), final)
-        pooled = jnp.zeros((slots, width), FULL)
-        for head in range(self.head_count):
-            pooled = pooled + stacked[head * slots : (head + 1) * slots] * marks[head : head + 1]
-        pooled = pooled.astype(LOW)
-        image_span = pl.ds(pack * slots, slots)
-        r.pooled[image_span] = pooled
+        for pack, final in enumerate(finals):
+            member = (r.segment[pack : pack + 1] == iota((slots, self.tokens), 0)).astype(FULL)
+            first = pack * marks.shape[0]
+            stacked = [
+                member * pool_wide[first + head : first + head + 1] for head in range(self.head_count)
+            ]
+            stacked = dot(jnp.concatenate(stacked, axis=0).astype(LOW), final)
+            pooled = jnp.zeros((slots, width), FULL)
+            for head in range(self.head_count):
+                pooled = pooled + stacked[head * slots : (head + 1) * slots] * marks[head : head + 1]
+            r.pooled[pack * slots : (pack + 1) * slots] = pooled.astype(LOW)
+        pooled = r.pooled[...]
         padded, classes = r.g_cls.shape[-1], r.w_cls.shape[1]
         logits = [dot(pooled, self.class_block(group)[...]) for group in range(self.groups)]
         logits = jnp.concatenate(logits, axis=1)
@@ -981,9 +1018,12 @@
         block = jnp.floor((lanes + 0.5) / padded)
         within = lanes - block * padded
         logits = jnp.where(within < classes, logits, excluded)
-        hit = block * classes + within == self.own_slots(r.labels, pack)
+        labels, weights = (
+            jnp.concatenate([self.own_slots(ref, pack) for pack in range(packs)], axis=0)
+            for ref in (r.labels, r.weights)
+        )
+        hit = block * classes + within == labels
         hit = (hit & (within < classes)).astype(FULL)
-        weights = self.own_slots(r.weights, pack)
         top = jnp.max(logits, axis=1, keepdims=True)
         log_total = top + jnp.log(row_sum(jnp.exp(logits - top)))
         losses = weights * (log_total - row_sum(hit * logits))
@@ -991,21 +1031,27 @@
         r.vgrad[6:7] += first * column_sum(losses)
         share = weights / r.weight_sum[:, :1]
         logit_grad = ((jnp.exp(logits - log_total) - hit) * share).astype(LOW)
-        r.logit_grad[image_span] = logit_grad
-        pooled_grad = jnp.zeros((slots, width), FULL)
+        r.logit_grad[...] = logit_grad
+        pooled_grad = jnp.zeros((packs * slots, width), FULL)
         for group in range(self.groups):
             part = logit_grad[:, group * padded : (group + 1) * padded]
             pooled_grad = pooled_grad + dot(part, self.class_block(group)[...], NT)
         r.image_high[...], r.image_rest[...] = halves(pooled_grad)
 
-        def image_rows(index):
-            owner = r.cols[strip_rows(index), 0:1]
-            member_rows = (iota((strip, slots), 1) == owner).astype(LOW)
-            return dot(member_rows, r.image_high[...]) + dot(member_rows, r.image_rest[...])
+        def strip_spots(index):
+            pack = index // per_pack
+            heads = pl.ds(pl.multiple_of(pack * marks.shape[0], 16), marks.shape[0])
+            images = pl.ds(pl.multiple_of(pack * slots, 16), slots)
+            return tile(index, strip), heads, images, tile(index % per_pack, strip)
+
+        def image_rows(rows, images):
+            member_rows = (iota((strip, slots), 1) == r.cols[rows, 0:1]).astype(LOW)
+            return dot(member_rows, r.image_high[images]) + dot(member_rows, r.image_rest[images])
 
         def weigh(index):
-            product = image_rows(index) * r.low[strip_rows(index)].astype(FULL)
-            r.score_heads[:, tile(index, strip)] = fine_dot(marks_low, product, NT)
+            rows, heads, images, lanes = strip_spots(index)
+            product = image_rows(rows, images) * r.low[rows].astype(FULL)
+            r.score_heads[heads, lanes] = fine_dot(marks_low, product, NT)
 
         loop(strips, weigh)
         weight_grad = r.score_heads[...]
@@ -1013,12 +1059,12 @@
         r.score_heads[...] = pooling * (weight_grad - mean) * HEAD ** (-0.5)
 
         def strip_back(index):
-            rows, lanes = strip_rows(index), tile(index, strip)
-            high, rest = halves(r.score_heads[:, lanes])
+            rows, heads, images, lanes = strip_spots(index)
+            high, rest = halves(r.score_heads[heads, lanes])
             score_rows = dot(high, marks_low, TN) + dot(rest, marks_low, TN)
-            pool_rows = dot(r.pool_heads[:, lanes].astype(LOW), marks_low, TN)
+            pool_rows = dot(r.pool_heads[heads, lanes].astype(LOW), marks_low, TN)
             r.vgrad[5:6] += column_sum(score_rows * r.low[rows].astype(FULL))
-            final_grad = pool_rows * image_rows(index) + score_rows * probe
+            final_grad = pool_rows * image_rows(rows, images) + score_rows * probe
             shape, scale = normal(r.stream[rows], -1)
             r.vgrad[2:3] += column_sum(final_grad * shape)
             residual_grad = normal_back(final_grad * self.gain(2), shape, scale, -1)
@@ -1029,6 +1075,7 @@
 
     def class_back(self):
         r = self.r
+        r.turned[...] = jnp.zeros(r.turned.shape, FULL)
         padded = r.g_cls.shape[-1]
         for group in range(self.groups):
             part = r.logit_grad[:, group * padded : (group + 1) * padded]
@@ -1037,13 +1084,7 @@
     def active_back(self, index):
         at = tile(index, 256)
         upstream = dot(self.r.low[...], self.w_down[at], NT)
-        upward = self.upward[:, at].astype(FULL)
-        bend = curve(upward)
-        squared = upward * upward
-        slope = 0.5 * (1.0 + bend) + (0.5 * 0.7978845608) * upward * (1.0 - bend * bend) * (
-            1.0 + (3 * 0.044715) * squared
-        )
-        self.upward[:, at] = (upstream * slope).astype(LOW)
+        self.upward[:, at] = (upstream * self.upward[:, at].astype(FULL)).astype(LOW)
 
     def down_weight(self, index):
         at = tile(index, 256)
@@ -1052,7 +1093,7 @@
     def second_back(self, pack):
         r, span = self.r, self.span(pack)
         upstream = dot(self.upward[span], self.w_up[...], NT)
-        shape = r.shape_second[span].astype(FULL)
+        shape = self.shape_second[span].astype(FULL)
         r.vgrad[1:2] += column_sum(upstream * shape)
         back = normal_back(upstream * self.gain(1), shape, r.cols[span, 2:3], -1)
         total = r.stream[span] + back
@@ -1077,34 +1118,56 @@
         r.mixed[:, span] = r.hidden[span].T
         count = self.head_count
 
-        def head_back(grad, part, head, at):
-            own = tile(head, HEAD)
-            shape = r.shape_heads[at, span].astype(FULL)
-            scale = r.scale_heads[pl.ds(part * count + head, 1), span]
-            term = grad * shape
-            for low in range(0, self.tokens, 128):
-                r.gacc[at] += term[:, low : low + 128]
-            back = normal_back(grad * r.gains[own, 3 + part : 4 + part], shape, scale, 0)
-            r.joined[at, span] = back.astype(LOW)
-
-        def one_head(head):
-            parts = self.head_parts(head, span)
-            query, key, value = (r.joined[at, span] for at in parts)
-            mixed_grad = r.mixed[tile(head, HEAD), span]
-            scores = dot(key, query, TN) * HEAD ** (-0.5) + r.mask[...]
-            attention = jnp.exp(scores - r.log_total[pl.ds(head, 1), span])
-            prob_grad = dot(value, mixed_grad, TN)
-            mean = column_sum(attention * prob_grad)
-            score_grad = (attention * (prob_grad - mean)).astype(LOW)
-            r.joined[parts[2], span] = dot(mixed_grad, attention.astype(LOW), NT).astype(LOW)
-            head_back(dot(key, score_grad) * HEAD ** (-0.5), 0, head, parts[0])
-            head_back(dot(query, score_grad, NT) * HEAD ** (-0.5), 1, head, parts[1])
-
-        loop(count, one_head)
+        def some_heads(group):
+            heads = [group * HEADS_AT_ONCE + member for member in range(HEADS_AT_ONCE)]
+            places = [self.head_parts(head, span) for head in heads]
+            loaded = [[self.joined[at, span] for at in place] for place in places]
+            mixed_grads = [r.mixed[tile(head, HEAD), span] for head in heads]
+            log_totals = [r.log_total[pl.ds(head, 1), span] for head in heads]
+            norms = []
+            for part in range(2):
+                for head, place in zip(heads, places):
+                    shape = self.shape_heads[place[part], span].astype(FULL)
+                    scale = r.scale_heads[pl.ds(part * count + head, 1), span]
+                    gain = r.gains[tile(head, HEAD), 3 + part : 4 + part]
+                    norms.append((shape, scale, gain))
+            mask = r.mask[...]
+            scores = [dot(key, query, TN) * SCORE_SCALE + mask for query, key, _ in loaded]
+            shares = [jnp.exp2(score - log_total) for score, log_total in zip(scores, log_totals)]
+            share_grads = [dot(parts[2], grad, TN) for parts, grad in zip(loaded, mixed_grads)]
+            means = [column_sum(share * grad) for share, grad in zip(shares, share_grads)]
+            score_grads = [
+                (share * (grad - mean)).astype(LOW)
+                for share, grad, mean in zip(shares, share_grads, means)
+            ]
+            value_grads = [
+                dot(grad, share.astype(LOW), NT) for grad, share in zip(mixed_grads, shares)
+            ]
+            grads = [dot(parts[1], grad) for parts, grad in zip(loaded, score_grads)]
+            grads += [dot(parts[0], grad, NT) for parts, grad in zip(loaded, score_grads)]
+            grads = [grad * HEAD ** (-0.5) for grad in grads]
+            terms = [grad * shape for grad, (shape, _, _) in zip(grads, norms)]
+            backs = [
+                normal_back(grad * gain, shape, scale, 0)
+                for grad, (shape, scale, gain) in zip(grads, norms)
+            ]
+            for place, grad in zip(places, value_grads):
+                self.joined[place[2], span] = grad.astype(LOW)
+            at = 0
+            for part in range(2):
+                lanes = pl.ds(part * 128, 128)
+                for head, place in zip(heads, places):
+                    term = terms[at]
+                    term = sum(term[:, low : low + 128] for low in range(0, self.tokens, 128))
+                    r.turned[tile(head, HEAD), lanes] += term
+                    self.joined[place[part], span] = backs[at].astype(LOW)
+                    at += 1
+
+        loop(count // HEADS_AT_ONCE, some_heads)
 
     def first_back(self, pack):
         r, span = self.r, self.span(pack)
-        upstream = dot(r.joined[:, span].T, self.w_qkv[...], NT)
+        upstream = dot(self.joined[:, span].T, self.w_qkv[...], NT)
         shape = r.shape_first[span].astype(FULL)
         r.vgrad[0:1] += column_sum(upstream * shape)
         back = normal_back(upstream * self.gain(0), shape, r.cols[span, 1:2], -1)
@@ -1115,7 +1178,7 @@
         turned = self.r.normed[:, rows].T
         for part in range(3):
             columns = pl.ds(part * COLUMNS, COLUMNS)
-            self.w_qkv[rows, columns] = dot(turned, self.r.joined[columns], NT).astype(LOW)
+            self.w_qkv[rows, columns] = dot(turned, self.joined[columns], NT).astype(LOW)
 
     def embed_weight(self):
         r, width = self.r, self.width
@@ -1128,16 +1191,18 @@
         self.w_embed[width:] = dot(r.pos[...], r.low[...], TN).astype(LOW)
 
     def head_gains(self):
-        r, width = self.r, self.width
+        r = self.r
         for part in range(2):
-            r.vgrad[3 + part : 4 + part] = column_sum(r.gacc[part * width : (part + 1) * width].T)
-
-
-def kernel(dims, names, pieces, class_pieces, *refs):
+            sums = r.turned[:, part * 128 : (part + 1) * 128]
+            r.vgrad[3 + part : 4 + part] = column_sum(sums.T)
+
+
+def kernel(dims, names, pieces, class_pieces, spots, *refs):
     r = types.SimpleNamespace(**dict(zip(names, refs)))
     place = Place(dims)
     barrier = pltpu.get_barrier_semaphore()
-    pl.semaphore_wait(barrier, place.tell(barrier))
+    greeted = place.plane() + [{"z": step} for step in place.steps("z")]
+    pl.semaphore_wait(barrier, place.tell(barrier, greeted))
     courier = Courier(place, r.send, r.recv)
     layer = Layer(r, place, dims)
     z, y, x, core = (place.at[axis] for axis in "zyxc")
@@ -1152,7 +1217,7 @@
         rows, half = shard.shape[0], shard.shape[1] // CORES
         at = pl.ds(pl.multiple_of(core * rows, 8), rows)
         other = pl.ds(pl.multiple_of((1 - core) * half, 128), half)
-        arriving.append(courier.start("c", 1, shard.at[:, other], pair.at[at]))
+        arriving.append(courier.start({"c": 1}, shard.at[:, other], pair.at[at]))
         pair[at] = shard[:, pl.ds(pl.multiple_of(core * half, 128), half)]
     r.g_vec[z, y, x, core] = jnp.zeros((8, 128), FULL)
     count = r.vectors.shape[1]
@@ -1176,15 +1241,17 @@
     def class_view(piece, core):
         return lambda z, y, x: r.g_cls.at[x, core, z, y, pl.ds(*piece[1])]
 
-    spreads = [Spread(courier, lambda z, y, x: r.g_vec.at[z, y, x, core], "xy")]
+    spreads = [Spread(courier, lambda z, y, x: r.g_vec.at[z, y, x, core], "zxy")]
     ready, last = {}, {}
-    for piece in pieces:
-        ready.setdefault(len(spreads), piece[0]) if piece[0] not in ready.values() else None
-        last[piece[0]] = len(spreads)
-        spreads.append(Spread(courier, matrix_view(piece, core), piece[3]))
-    for piece in class_pieces:
-        last[5] = len(spreads)
-        spreads.append(Spread(courier, class_view(piece, core), piece[3]))
+    sequence = [piece for piece in pieces if piece[0] < 4] + class_pieces
+    sequence += [piece for piece in pieces if piece[0] == 4]
+    for piece in sequence:
+        index = piece[0]
+        if index < 5 and index not in last:
+            ready[len(spreads)] = index
+        last[index] = len(spreads)
+        view = matrix_view(piece, core) if index < 5 else class_view(piece, core)
+        spreads.append(Spread(courier, view, piece[3]))
 
     def begin(position):
         if position in ready:
@@ -1195,7 +1262,7 @@
             full[index][z, y, x, :, across] = pairs[index][...].astype(LOW)
         spreads[position].begin()
 
-    lag = (-2, 0, 2, 4, 6)
+    lag = GATHER_LAGS
     actions = (
         begin,
         lambda i: spreads[i].middle(1),
@@ -1229,6 +1296,7 @@
     until(1)
     for pack in range(layer.packs):
         layer.project(pack)
+        turn()
         layer.attend(pack)
         turn()
     until(2)
@@ -1237,14 +1305,14 @@
     turn()
     until(3)
     tiles = layer.hidden_units // 256
-    loop(tiles, layer.widen)
-    turn()
+    for index in range(4):
+        loop(tiles // 4, lambda step: layer.widen(step + tiles // 4 * index))
+        turn()
+    until(5)
     until(4)
     loop(layer.width // 256, layer.narrow)
-    until(5)
-
-    for pack in range(layer.packs):
-        layer.classify(pack)
+
+    layer.classify()
     courier.finish()
     layer.class_back()
     left = {index: sum(piece[0] == index for piece in pieces) for index in order}
@@ -1261,7 +1329,7 @@
             count, half = owned[index].shape[0], owned[index].shape[1] // CORES
             across = pl.ds(pl.multiple_of(core * half, 128), half)
             other = pairs[index].at[pl.ds(pl.multiple_of((1 - core) * count, 8), count)]
-            closing[index] = courier.start("c", 1, other, owned[index].at[:, across])
+            closing[index] = courier.start({"c": 1}, other, owned[index].at[:, across])
             owned[index][:, across] = pairs[index][pl.ds(pl.multiple_of(core * count, 8), count)]
 
         return finish
@@ -1273,6 +1341,7 @@
         return finish
 
     under_way = []
+    clock = {"now": 0, "last": 0}
 
     def send_class():
         padded = r.g_cls.shape[-1]
@@ -1282,18 +1351,19 @@
             def view(core, piece=piece):
                 return class_view(piece, core)(ALL, ALL, ALL)
 
-            fold = Fold(courier, view, piece[3], pool, keep_class(piece))
+            fold = Fold(courier, view, piece[3][::-1], pool, keep_class(piece))
             fold.begin()
+            fold.entry = clock["last"] = max(clock["now"], clock["last"]) + 1
             under_way.append(fold)
 
-    def send_matrix(index, pool_ref, at):
+    def send_matrix(index, pool_ref):
         mine = [piece for piece in pieces if piece[0] == index]
         stack = pool_ref.shape[-2] // mine[0][1][1]
         spots, total = [], 0
         for position, (_, rows, columns, _) in enumerate(mine):
             if position % stack == 0:
-                total += columns[1]
-            spots.append(((position % stack * rows[1], rows[1]), at + total - columns[1]))
+                start, total = total, total + max(p[2][1] for p in mine[position : position + stack])
+            spots.append(((position % stack * rows[1], rows[1]), start))
         folds = []
         for piece, (rows, column) in zip(mine, spots):
             width = piece[2][1]
@@ -1302,34 +1372,35 @@
             def view(core, piece=piece):
                 return matrix_view(piece, core)(ALL, ALL, ALL)
 
-            fold = Fold(courier, view, piece[3], pool, keep(piece))
+            fold = Fold(courier, view, piece[3][::-1], pool, keep(piece))
             fold.begin()
+            fold.entry = clock["last"] = max(clock["now"], clock["last"]) + 1
             folds.append(fold)
         under_way.extend(folds)
-        return folds
-
-    def pump(times=1, abreast=4):
+
+    def pump(times=1):
         for _ in range(times):
-            for fold in list(under_way[:abreast]):
-                if fold.advance():
-                    under_way.remove(fold)
-
-    def drain(folds):
-        while any(fold in under_way for fold in folds):
-            pump()
+            clock["now"] += 1
+            for fold in list(under_way)[:: NEWEST_FIRST]:
+                if fold.due is None and fold.entry <= clock["now"]:
+                    fold.due = clock["now"]
+                if fold.due is not None and fold.due <= clock["now"]:
+                    fold.due = clock["now"] + FOLD_LAG
+                    if fold.advance():
+                        under_way.remove(fold)
 
     def free(which):
-        pl.semaphore_wait(r.free.at[which], place.tell(r.free.at[which]))
+        pl.semaphore_wait(r.free.at[which], place.tell(r.free.at[which], place.lines()))
 
     send_class()
-    loop(tiles // 2, layer.active_back)
-    pump()
-    loop(tiles // 2, lambda index: layer.active_back(index + tiles // 2))
-    pump()
-    loop(tiles, layer.down_weight)
+    for index in range(3):
+        loop(tiles // 3, lambda step: layer.active_back(step + tiles // 3 * index))
+        pump()
+    for index in range(3):
+        loop(tiles // 3, lambda step: layer.down_weight(step + tiles // 3 * index))
+        pump()
     free(0)
-    down_folds = send_matrix(4, r.active, 0)
-    pump()
+    send_matrix(4, r.active)
     for pack in range(layer.packs):
         layer.second_back(pack)
         pump()
@@ -1337,26 +1408,25 @@
         loop(layer.width // 256, lambda index: layer.up_weight(index, part))
         pump()
     free(1)
-    send_matrix(3, r.upward, 0)
+    send_matrix(3, r.upward)
     for pack in range(layer.packs):
         layer.mixed_back(pack)
     pump()
     loop(layer.width // 256, layer.out_weight)
-    send_matrix(2, r.pool_out, 0)
+    send_matrix(2, r.shape_second)
+    pump()
     for pack in range(layer.packs):
         layer.attend_back(pack)
-        pump()
+        pump(2)
     for pack in range(layer.packs):
         layer.first_back(pack)
         pump()
     loop(layer.width // 256, layer.qkv_weight)
-    drain(down_folds)
-    courier.sent([copy for fold in down_folds for copy in fold.copies])
     free(2)
-    half = full[1].shape[-1] // CORES
-    send_matrix(1, r.active, 0)
+    send_matrix(1, r.joined)
+    pump()
     layer.embed_weight()
-    send_matrix(0, r.active, 2 * half)
+    send_matrix(0, r.shape_heads)
     layer.head_gains()
     lanes = iota((1, layer.width), 1)
     devices = dims["x"] * dims["y"] * dims["z"] * CORES
@@ -1374,12 +1444,6 @@
         (r.m_embed, r.v_embed), (r.m_qkv, r.v_qkv), (r.m_out, r.v_out), (r.m_up, r.v_up),
         (r.m_down, r.v_down), (r.m_vectors, r.v_vectors), (r.m_cls, r.v_cls),
     ]
-    outs = [
-        (r.embed_new, r.embed_first, r.embed_second), (r.qkv_new, r.qkv_first, r.qkv_second),
-        (r.out_new, r.out_first, r.out_second), (r.up_new, r.up_first, r.up_second),
-        (r.down_new, r.down_first, r.down_second),
-        (r.vectors_new, r.vectors_first, r.vectors_second), (r.cls_new, r.cls_first, r.cls_second),
-    ]
     loads = []
     for position, (index, columns, rows, at) in enumerate(strips):
         for which in range(2):
@@ -1391,19 +1455,21 @@
                 )
             )
             loads[-1].start()
-    vec_total = Total(courier, (r.vec_c, r.vec_x, r.vec_y, r.vec_z))
-    vec_total.send("c", r.vgrad[...])
-    for before, after in zip("cxyz", "xyz "):
-        pump()
-        vec_sum = vec_total.receive(before)
-        if after != " ":
-            vec_total.send(after, vec_sum)
+    vec_total = Total(courier, r.vec_plane, r.vec_line)
+    vec_total.send(0, r.vgrad[...])
+    pump(2)
+    vec_total.send(1, vec_total.receive(0))
     while under_way:
         pump()
+    vec_sum = vec_total.receive(1)
     for index in order:
         closing[index].wait_recv()
     for load in loads:
         load.wait()
+
+    def put(name, value):
+        at, shape = spots[name]
+        r.small[pl.ds(at, shape[0]), pl.ds(0, shape[1])] = value
 
     vec_count = r.vectors.shape[1]
     device = ((z * dims["y"] + y) * dims["x"] + x) * CORES + core
@@ -1415,17 +1481,18 @@
     mats = list(zip(owned + [r.o_cls], shards + [r.w_cls]))
     parts = [squares(grad[...]) for grad, _ in mats] + [squares(weight[...]) for _, weight in mats]
     block = jnp.concatenate(parts + [wide_rows(r.vectors[...]), jnp.zeros((6, 128), FULL)], axis=0)
-    block = Total(courier, (r.one_c, r.one_x, r.one_y, r.one_z)).through(block)
+    block = Total(courier, r.one_plane, r.one_line).through(block)
     sums = row_sum(block)
     vec_squares = row_sum(vec_sum * vec_sum)
-    r.loss[...] = vec_sum[6:7, :2]
+    put("loss", vec_sum[6:7, :2])
     clip_norm = jnp.sqrt(column_sum(sums[:6]) + column_sum(vec_squares[:6]))
-    r.clip[...] = clip_norm
+    put("clip", clip_norm)
     factor = jnp.minimum(1.0, clip_limit / clip_norm)
     partial = {index: jnp.zeros((1, 128), FULL) for index in order}
     stores = []
 
-    def store(source, target):
+    def store(source, at, rows):
+        target = r.state.at[pl.ds(at, rows)]
         copy = pltpu.make_async_copy(source, target, r.local.at[len(loads) + len(stores)])
         copy.start()
         stores.append(copy)
@@ -1440,33 +1507,48 @@
         partial[index] = partial[index] + squares(update)
         for which, value in enumerate((first, second)):
             r.stream[spot[which]] = value
-            store(r.stream.at[spot[which]], outs[index][1 + which].at[:, columns])
+            store(r.stream.at[spot[which]], at + which * total_rows, rows)
     first, second = moments_step(r.o_cls[...] * factor, r.m_cls[...], r.v_cls[...])
-    r.cls_first[...], r.cls_second[...] = first, second
+    put("cls_first", first)
+    put("cls_second", second)
     class_update = update_of(first, second, r.w_cls[...])
     r.o_cls[...] = class_update
     first, second = moments_step(vec_grad * factor, r.m_vectors[...], r.v_vectors[...])
-    r.vectors_first[...], r.vectors_second[...] = first, second
+    put("vectors_first", first)
+    put("vectors_second", second)
     vec_update = update_of(first, second, r.vectors[...])
     parts = [partial[index] for index in order] + [squares(class_update), wide_rows(vec_update)]
     block = jnp.concatenate(parts + [jnp.zeros((4, 128), FULL)], axis=0)
-    block = Total(courier, (r.two_c, r.two_x, r.two_y, r.two_z)).through(block)
+    block = Total(courier, r.two_plane, r.two_line).through(block)
     grown = jnp.sqrt(row_sum(block))[:12]
     weight_norms = jnp.sqrt(sums[6:18])
-    r.norms[:, 0:1] = weight_norms
-    r.norms[:, 1:2] = grown
+    put("norms", jnp.concatenate([weight_norms, grown], axis=1))
     ratios = learn_rate * (weight_norms / grown)
     for index, columns, rows, at in strips:
         update = owned[index][:, columns]
         owned[index][:, columns] = shards[index][:, columns] - ratios[index : index + 1] * update
-        store(owned[index].at[:, columns], outs[index][0].at[:, columns])
-    r.cls_new[...] = r.w_cls[...] - ratios[5:6] * r.o_cls[...]
-    r.vectors_new[...] = r.vectors[...] - ratios[6:12] * vec_update
+        store(owned[index].at[:, columns], at + 2 * total_rows, rows)
+    put("cls_new", r.w_cls[...] - ratios[5:6] * r.o_cls[...])
+    put("vectors_new", r.vectors[...] - ratios[6:12] * vec_update)
     for copy in stores:
         copy.wait()
     courier.finish()
 
 
+def hand_out(shapes, spots, state, small, *outs):
+    total = sum(shape[0] * shape[1] // COLUMNS for shape in shapes)
+    at = 0
+    for index, (rows, wide) in enumerate(shapes):
+        for low in range(0, wide, COLUMNS):
+            for which, part in enumerate((2, 0, 1)):
+                out = outs[3 + 3 * index + which]
+                out[:, pl.ds(low, COLUMNS)] = state[pl.ds(part * total + at, rows)]
+            at += rows
+    for out, (at, shape) in zip(outs[:3] + outs[18:], spots.values()):
+        out[...] = small[pl.ds(at, shape[0]), pl.ds(0, shape[1])]
+
+
+KINDS = ("_new", "_first", "_second")
 WEIGHTS = ("embed", "qkv", "out", "up", "down", "vectors", "cls")
 
 
@@ -1481,8 +1563,8 @@
     padded = -(-w_cls.shape[1] // 128) * 128
     class_rows = w_cls.shape[0]
     class_pieces = [
-        (5, rows, columns, ("xy", "yx")[turn])
-        for turn, (rows, columns) in enumerate(cut(class_rows, padded, 2))
+        (5, rows, columns, ("zxy", "zyx")[turn])
+        for turn, (rows, columns) in enumerate(cut_rows(class_rows, padded, 2))
     ]
     packs, tokens, width = patches.shape
     rows = packs * tokens
@@ -1501,12 +1583,16 @@
     for position, name in enumerate(WEIGHTS):
         inputs["m_" + name], inputs["v_" + name] = moments[2 * position : 2 * position + 2]
         specs += [anywhere if position < 5 else vmem] * 2
-    outs = {"loss": (1, 2), "clip": (1, 1), "norms": (12, 2)}
-    out_specs = [vmem] * 3
-    for position, (name, param) in enumerate(zip(WEIGHTS, params)):
-        for kind in ("_new", "_first", "_second"):
-            outs[name + kind] = param.shape
-            out_specs.append(anywhere if position < 5 else vmem)
+    small = {"loss": (1, 2), "clip": (1, 1), "norms": (12, 2)}
+    for name, param in zip(WEIGHTS[5:], params[5:]):
+        small.update({name + kind: param.shape for kind in KINDS})
+    spots, tall = {}, 0
+    for name, shape in small.items():
+        spots[name] = (tall, shape)
+        tall += -(-shape[0] // 8) * 8
+    strips = sum(w.shape[0] * w.shape[1] // COLUMNS for w in mats)
+    outs = {"state": (3 * strips, COLUMNS), "small": (tall, padded)}
+    out_specs = [anywhere, vmem]
     scratch = {}
     for name, param, block in zip(WEIGHTS, mats, blocks):
         scratch["g_" + name] = pltpu.VMEM((Z, Y, X, block[0], param.shape[1]), LOW)
@@ -1516,16 +1602,16 @@
     scratch["g_cls"] = pltpu.VMEM((X, CORES, Z, Y, class_rows, padded), LOW)
     scratch["g_vec"] = pltpu.VMEM((Z, Y, X, CORES, 8, 128), FULL)
     scratch["pool_cls"] = pltpu.VMEM((X, Z, Y, class_rows, 2 * padded), LOW)
-    scratch["pool_out"] = pltpu.VMEM((Z, Y, X) + (blocks[2][0], 2 * blocks[2][1]), LOW)
-    low_rows = ("normed", "hidden", "shape_first", "shape_second", "low")
+    scratch["shape_second"] = pltpu.VMEM((Z, Y, X, rows // chips, width), LOW)
+    low_rows = ("normed", "hidden", "shape_first", "low")
     scratch.update({name: pltpu.VMEM((rows, width), LOW) for name in low_rows})
     scratch["pos"] = pltpu.VMEM((rows, 2 * POS), LOW)
     scratch["cols"] = pltpu.VMEM((rows, 128), FULL)
     scratch["segment"] = pltpu.VMEM((packs, tokens), FULL)
     scratch["stream"] = pltpu.VMEM((rows, width), FULL)
     scratch["turned"] = pltpu.VMEM((width, tokens), FULL)
-    scratch["joined"] = pltpu.VMEM((3 * width, rows), LOW)
-    scratch["shape_heads"] = pltpu.VMEM((2 * width, rows), LOW)
+    scratch["joined"] = pltpu.VMEM((Z, Y, X, 3 * width // chips, rows), LOW)
+    scratch["shape_heads"] = pltpu.VMEM((Z, Y, X, 2 * width // chips, rows), LOW)
     scratch["scale_heads"] = pltpu.VMEM((2 * heads, rows), FULL)
     scratch["log_total"] = pltpu.VMEM((heads, rows), FULL)
     scratch["mixed"] = pltpu.VMEM((width, rows), LOW)
@@ -1534,27 +1620,26 @@
     scratch["upward"], scratch["active"] = pltpu.VMEM(wide, LOW), pltpu.VMEM(wide, LOW)
     scratch["vec"], scratch["vgrad"] = pltpu.VMEM((8, width), FULL), pltpu.VMEM((8, width), FULL)
     scratch["gains"] = pltpu.VMEM((width, 8), FULL)
-    scratch["gacc"] = pltpu.VMEM((2 * width, 128), FULL)
     scratch["weight_sum"] = pltpu.VMEM((1, 128), FULL)
     scratch["pooled"] = pltpu.VMEM((images, width), LOW)
     for name in ("pool_heads", "score_heads"):
-        scratch[name] = pltpu.VMEM((16, tokens), FULL)
+        scratch[name] = pltpu.VMEM((16 * packs, tokens), FULL)
     for name in ("image_high", "image_rest"):
-        scratch[name] = pltpu.VMEM((heights.shape[1], width), LOW)
+        scratch[name] = pltpu.VMEM((images, width), LOW)
     scratch["logit_grad"] = pltpu.VMEM((images, X * CORES * padded), LOW)
     for name, shape in (("vec_", (8, width)), ("one_", (24, 128)), ("two_", (16, 128))):
-        for axis, slots in zip("cxyz", total_slots(dims, shape)):
-            scratch[name + axis] = slots
+        scratch[name + "plane"] = pltpu.VMEM((X * Y * CORES,) + shape, FULL)
+        scratch[name + "line"] = pltpu.VMEM((Z,) + shape, FULL)
     peers = (X - 1) + (Y - 1) + (Z - 1) + 1
-    count = (len(pieces) + len(class_pieces)) * (2 * peers + X - 1 + Y - 1)
-    count += 10 + 3 * peers + 2 * peers
+    count = (1 + len(pieces) + len(class_pieces)) * 3 * peers
+    count += 10 + 3 * (X * Y * CORES - 1 + Z - 1) + 2 * peers
     scratch["send"] = pltpu.SemaphoreType.DMA((count,))
     scratch["recv"] = pltpu.SemaphoreType.DMA((count,))
     scratch["local"] = pltpu.SemaphoreType.DMA((5 * sum(w.shape[1] // COLUMNS for w in mats),))
     scratch["free"] = pltpu.SemaphoreType.REGULAR((3,))
     names = list(inputs) + list(outs) + list(scratch)
-    loss_terms, clip_norm, *updated = pl.pallas_call(
-        functools.partial(kernel, dims, names, pieces, class_pieces),
+    state, rest = pl.pallas_call(
+        functools.partial(kernel, dims, names, pieces, class_pieces, spots),
         out_shape=[jax.ShapeDtypeStruct(shape, FULL) for shape in outs.values()],
         in_specs=specs,
         out_specs=out_specs,
@@ -1563,6 +1648,16 @@
             collective_id=0, has_side_effects=True, vmem_limit_bytes=(64 << 20) - 4096
         ),
     )(*inputs.values())
+    shapes = [small["loss"], small["clip"], small["norms"]]
+    for param in params:
+        shapes += [param.shape] * 3
+    loss_terms, clip_norm, *updated = pl.pallas_call(
+        functools.partial(hand_out, [w.shape for w in mats], spots),
+        out_shape=[jax.ShapeDtypeStruct(shape, FULL) for shape in shapes],
+        in_specs=[vmem] * 2,
+        out_specs=[vmem] * 24,
+        compiler_params=pltpu.CompilerParams(vmem_limit_bytes=32 << 20),
+    )(state, rest)
     return (loss_terms.reshape(2), clip_norm.reshape(()), *updated)
 
 

time: 373 us -> 262 us (0.70)
  Pallas kernels: 344 us -> 253 us
  local copies, waits for them, and re-layouts: 21.1 us -> 3.45 us
    pallas_call x1, Pallas kernels: 344 us -> 251 us  [kernel_body(): pl.pallas_call(functools.partial(kernel, dims, names, pieces, class_piece...]
    unnamed x55 -> x5, local copies, waits for them, and re-layouts: 21.1 us -> 3.45 us
where the time goes in v3:
time: 262 us; the launch traced here: 258 us
  Pallas kernels  253 us (97%)
  local copies, waits for them, and re-layouts  3.45 us (1%)
    pallas_call x1, Pallas kernels, kernel_body(): pl.pallas_call(functools.partial(kernel, dims, names, pieces, class_piece...  251 us

profile of v3, /device:TPU:0, one launch (start us, length us, event | category | flops | bytes accessed | tf_op | source)
XLA Modules:
  0.0 257.6 jit_solution(6106778228398777119)
XLA Ops:
  0.7 251.4 %shard_map.433 = (f32[960,768]{1,0:T(8,128)}, f32[344,256]{1,0:T(8,128)}) custom-call(bf16[1024,768]{1,0:T(8,128)(2,1)} %bitcast.3, s32[4,16]{1,0:T(4,128)} %refs_1_.1, s32[4,16]{1,0:T(4,128)} %refs_2_.1, s32[4,64]{1,0:T(4,128)} %refs_3_.1, s32[4,64]{1,0:T(4,128)} %refs_4_.1, f32[32,768]{1,0:T(8,128)} %refs_5_.1, f32[24,2304]{1,0:T(8,128)} %refs_6_.1, ...), custom_call_target="tpu_custom_call" | custom-call | tf_op jit(solution)/shard_map/pallas_call | solution.py:1641
  252.1 0.0 copy-start
  252.1 1.8 copy-done
  253.9 0.0 copy-start.1
  253.9 1.0 copy-done.1
  254.9 1.9 shard_map.434
  256.8 0.6 copy.50
Async XLA Ops:
  252.1 1.8 copy-start
  253.9 1.0 copy-start.1
